TPU v7x, 32 devices: a whole 2x2x4 slice. The times are simulated.
32 devices in a mesh: slab: 16 (over z, x, core), dom: 2 (over y).
Axes of the slice: x: 2, y: 2, z: 4, core: 2. Of those that a mesh axis runs over, the one named last changes fastest.
Arguments:
- positions: float32 [3, 196608], P(None, ('slab', 'dom')), may hold values from -6 to 6
- velocities: float32 [3, 196608], P(None, ('slab', 'dom')), may hold values from -6 to 6
- masses: float32 [196608], P(('slab', 'dom')), may hold values from 0.2 to 2
- owner_cell: int32 [196608, 1], P(('slab', 'dom')), may hold values from 0 to 127; in each aligned block of 6144 rows (0 to 6143, 6144 to 12287, ...) at most 64 rows name the same one
- counts: int32 [32], P(('slab', 'dom')), may hold values from 3072 to 6144, as said below
Outputs:
- state: float32 [10, 16, 128, 128], P(None, 'slab', 'dom')
- buddy: float32 [10, 16, 128, 128], P(None, 'slab', 'dom')
Inputs may be any that keep to these rules, and one draw needn't show every extreme that they name: owner_cell is the partner index of the owner times 64 plus its cell; among the rows of one device no value appears more than 64 times, and some device's rows name one value exactly 64 times. `counts`: some device has all 6144 rows live.
All inputs are finite; a program needn't handle non-finite values.
Results may differ from a plain program's by a relative error of at most 0.0003.
Values sent between devices are 32-bit elements; how exact they have to be, the bound alone decides.
No kernel may reach another device: no remote copies, remote signals or barrier semaphores. Data moves between devices by JAX's collectives and lax.ppermute only.
A program may use at most 64 MiB of HBM per device.

v0:
```python
import jax
import jax.numpy as jnp
from jax import lax
from jax.sharding import PartitionSpec as P

CELLS = 64


drift_step = 0.5
kick_step = 0.5
soften = 0.25
reach = 4.0
coupling = 0.25


def passed_along(value, axis, by):
    size = lax.axis_size(axis)
    return lax.ppermute(value, axis, [(i, (i + by) % size) for i in range(size)])


def with_halo(cells, sides, width):
    for axis, dim in sides:
        count = lax.axis_size(axis)
        head = lax.slice_in_dim(cells, 0, width, axis=dim)
        tail = lax.slice_in_dim(cells, cells.shape[dim] - width, cells.shape[dim], axis=dim)
        cells = jnp.concatenate(
            [
                lax.ppermute(tail, axis, [(i, (i + 1) % count) for i in range(count)]),
                cells,
                lax.ppermute(head, axis, [((i + 1) % count, i) for i in range(count)]),
            ],
            axis=dim,
        )
    return cells


def pair_accel(centre, others):
    separation = others[:3, None, :] - centre[:3, :, None]
    distance = jnp.sum(separation * separation, axis=0)
    inverse = lax.rsqrt(distance + soften)
    weight = others[3][None, :] * jnp.exp(-distance / reach) * inverse * inverse * inverse
    return coupling * jnp.sum(weight[None] * separation, axis=2)


def forces(shells, extended):
    width = shells.shape[2]
    centres = shells[:, 0].transpose(1, 0, 2)
    views = jnp.stack([extended[:, :, column : column + width] for column in range(3)], axis=2)
    others = views.transpose(3, 0, 1, 2, 4).reshape(width, 4, 9 * 128)

    def per_cell(pieces):
        return pair_accel(pieces[0], pieces[1])

    result = lax.map(per_cell, (centres, others), batch_size=2)
    return result.transpose(1, 0, 2)[:, None]


def per_device(positions, velocities, masses, owner_cell, counts):
    rows_dev = positions.shape[1]
    n_dom = lax.axis_size("dom")
    lanes = 128 // n_dom
    half_way = lax.axis_size("slab") // 2
    moved = positions + drift_step * velocities
    payload = jnp.concatenate([moved, masses[None, :], velocities], axis=0)
    target = owner_cell[:, 0]
    active = jnp.arange(rows_dev, dtype=jnp.int32) < counts[0]
    targets = n_dom * CELLS
    hits = (
        (target[:, None] == jnp.arange(targets, dtype=jnp.int32)[None, :]) & active[:, None]
    ).astype(jnp.int32)
    ranking = jnp.sum(jnp.cumsum(hits, axis=0) * hits, axis=1) - 1
    dom_target = target // CELLS
    cell_id = target % CELLS
    place = jnp.where(active, (cell_id * n_dom + dom_target) * lanes + ranking, CELLS * 128)
    buffer = jnp.zeros((7, CELLS * 128), jnp.float32).at[:, place].set(payload, mode="drop")
    buffer = buffer.reshape(7, CELLS, n_dom, lanes)
    arrived = lax.all_to_all(buffer, "dom", split_axis=2, concat_axis=2, tiled=True).reshape(
        7, 1, CELLS, 128
    )
    shells = arrived[:4]
    early = passed_along(arrived, "slab", half_way)
    extended = with_halo(shells, (("slab", 1), ("dom", 2)), 1)
    accel = forces(shells, extended)
    occupied = (arrived[3:4] > 0).astype(jnp.float32)
    accel = accel * occupied
    state = jnp.concatenate([arrived[:4], arrived[4:7] + kick_step * accel, accel], axis=0)
    later = passed_along(accel, "slab", half_way)
    buddy = jnp.concatenate([early[:4], early[4:7] + kick_step * later, later], axis=0)
    return (state, buddy)


def solution(mesh):
    placed = (
        P(None, ("slab", "dom")),
        P(None, ("slab", "dom")),
        P(("slab", "dom")),
        P(("slab", "dom"), None),
        P(("slab", "dom")),
    )
    return jax.shard_map(
        per_device,
        mesh=mesh,
        in_specs=placed,
        out_specs=(P(None, "slab", "dom", None), P(None, "slab", "dom", None)),
        check_vma=False,
    )
```

profile of v0, /device:TPU:0, one launch (start us, length us, event | category | flops | bytes accessed | tf_op | source)
XLA Modules:
  0.0 115.2 jit_solution(1045278511452034652)
XLA Ops:
  1.3 0.8 copy.46
  2.1 1.7 %fusion.3 = s32[128,48,128]{0,1,2:T(8,128)S(1)} fusion(s32[48,128]{0,1:T(8,128)S(1)} %copy.46, pred[48,128]{0,1:T(8,128)(4,1)S(1)} %add_compare_fusion), kind=kOutput, calls=%fused_computation.15 | output fusion | flops 102236160 | bytes 3176448 | tf_op jit(solution)/shard_map/reduce-window
  4.1 1.0 copy.47
  5.2 5.2 %fusion.2 = s32[6144]{0:T(1024)S(1)} fusion(s32[128,48,128]{0,2,1:T(8,128)S(1)} %copy.47, s32[6144]{0:T(1024)S(1)} %bitcast.83, pred[6144]{0:T(1024)(128)(4,1)S(1)} %iota_compare_fusion.2), kind=kLoop, calls=%fused_computation.14 | loop fusion | flops 3139584 | bytes 3201024 | tf_op jit(solution)/shard_map/reduce_sum | solution.py:71
  10.6 1.1 copy.48
  12.0 17.8 %scatter_custom_fusion = f32[7,8192]{0,1:T(8,128)} fusion(s32[6144]{0:T(1024)S(1)} %bitcast.87, f32[6144,7]{1,0:T(8,128)S(1)} %copy.48, f32[]{:T(128)} %constant.58.clone.1), kind=kCustom, calls=%fused_computation.21 | custom fusion | bytes 229380 | tf_op jit(solution)/shard_map/scatter | solution.py:75
  29.7 3.1 %copy.49 = f32[7,64,2,64]{3,1,0,2:T(8,128)S(1)} copy(f32[7,64,2,64]{0,3,2,1:T(8,128)} %bitcast.69) | data formatting | bytes 458752 | tf_op jit(solution)/shard_map/reshape | solution.py:76
  33.1 9.0 %all_to_all.5 = f32[2,1,28672]{2,1,0:T(1,128)S(1)} all-to-all(f32[2,1,28672]{2,1,0:T(1,128)S(1)} %reshape.117), channel_id=1, replica_groups=mesh['slab'=16,'dom'=2] {'dom'}, dimensions={0} | all-to-all | bytes 458752 | tf_op jit(solution)/shard_map/all_to_all | solution.py:77
  42.1 0.5 broadcast.133
  42.7 1.3 %reduce = f32[2,28672]{1,0:T(2,128)S(1)} reduce(f32[2,1,28672]{2,1,0:T(1,128)S(1)} %all_to_all.5, f32[]{:T(128)} %broadcast.133), dimensions={1}, to_apply=%all_to_all.3.reduce_sub_computation | reduce | bytes 458756 | tf_op jit(solution)/shard_map/all_to_all | solution.py:77
  44.8 4.4 %collective-permute-start.1 = (f32[4,1,64,128]{3,2,0,1:T(8,128)S(1)}, f32[4,1,64,128]{3,2,0,1:T(8,128)S(1)}, u32[]{:S(2)}, u32[]{:S(2)}) collective-permute-start(f32[4,1,64,128]{3,2,0,1:T(8,128)S(1)} %slice.55), channel_id=1, source_target_pairs={{2,0},{4,2},{6,4},{8,6},{10,8},{12,10},{14,12},{16,14},{18,16},{20... | collective-permute-start | bytes 393224 | tf_op jit(solution)/shard_map/ppermute | solution.py:30
  49.2 2.8 %collective-permute-done = f32[4,1,64,128]{3,2,0,1:T(8,128)S(1)} collective-permute-done((f32[4,1,64,128]{3,2,0,1:T(8,128)S(1)}, f32[4,1,64,128]{3,2,0,1:T(8,128)S(1)}, u32[]{:S(2)}, u32[]{:S(2)}) %collective-permute-start) | collective-permute-done | bytes 131104 | tf_op jit(solution)/shard_map/ppermute | solution.py:28
  52.2 1.9 %collective-permute-start.3 = (f32[4,3,1,128]{3,2,0,1:T(1,128)S(1)}, f32[4,3,1,128]{3,2,0,1:T(1,128)S(1)}, u32[]{:S(2)}, u32[]{:S(2)}) collective-permute-start(f32[4,3,1,128]{3,2,0,1:T(1,128)S(1)} %get-tuple-element.48), channel_id=1, source_target_pairs={{1,0},{0,1},{3,2},{2,3},{5,4},{4,5},{7,6},{6,7},{9,8},{8,9},{11,10... | collective-permute-start | bytes 18440 | tf_op jit(solution)/shard_map/ppermute | solution.py:30
  54.9 1.0 reshape.105
  55.8 0.7 collective-permute-start.4
  57.1 0.8 copy.52
  57.9 0.9 reshape_reshape.3
  58.8 47.6 %while.10 = (s32[]{:T(128)}, f32[32,2,3,128]{3,1,0,2:T(2,128)S(1)}, f32[32,2,4,1152]{3,2,1,0:T(4,128)S(1)}, f32[32,2,4,128]{3,1,0,2:T(2,128)S(1)}, s32[]{:T(128)}) while((s32[]{:T(128)}, f32[32,2,3,128]{3,1,0,2:T(2,128)S(1)}, f32[32,2,4,1152]{3,2,1,0:T(4,128)S(1)}, f32[32,2,4,128]{3,1,0,2:T(2,128)S(1)}, s32[]{:T(128)}) %tuple.31), condition=%wide.region_7.8_spmd, body=%wide.region_4.7_spmd.sunk | while | flops 7077890 | bytes 5098569 | solution.py:54
  59.8 0.5 fusion.23
  61.2 0.5 fusion.23
  106.4 2.2 %collective-permute-start.5 = (f32[3,1,64,128]{3,2,0,1:T(8,128)S(1)}, f32[3,1,64,128]{3,2,0,1:T(8,128)S(1)}, u32[]{:S(2)}, u32[]{:S(2)}) collective-permute-start(f32[3,1,64,128]{3,2,0,1:T(8,128)S(1)} %multiply_bitcast_fusion.1), channel_id=1, source_target_pairs={{0,16},{2,18},{4,20},{6,22},{8,24},{10,26},{12,28},{14,30},{16,0},... | collective-permute-start | bytes 294920 | tf_op jit(solution)/shard_map/ppermute | solution.py:18
  108.7 0.7 maximum_bitcast_fusion.1
  109.5 5.0 %collective-permute-done.5 = f32[3,1,64,128]{3,2,0,1:T(8,128)S(1)} collective-permute-done((f32[3,1,64,128]{3,2,0,1:T(8,128)S(1)}, f32[3,1,64,128]{3,2,0,1:T(8,128)S(1)}, u32[]{:S(2)}, u32[]{:S(2)}) %collective-permute-start.5) | collective-permute-done | bytes 98336 | tf_op jit(solution)/shard_map/ppermute | solution.py:18
  114.5 0.7 maximum_bitcast_fusion.2
  (430 shorter events, 46.9 us)
Async XLA Ops:
  4.1 1.1 copy-start.1
  5.2 5.3 %copy-start = (f32[3,6144]{1,0:T(4,128)S(1)}, f32[3,6144]{1,0:T(4,128)}, u32[]{:S(2)}) copy-start(f32[3,6144]{1,0:T(4,128)} %param.8) | copy-start | bytes 221188
  5.2 5.3 %copy-start.2 = (f32[3,6144]{1,0:T(4,128)S(1)}, f32[3,6144]{1,0:T(4,128)}, u32[]{:S(2)}) copy-start(f32[3,6144]{1,0:T(4,128)} %param.7) | copy-start | bytes 221188
  5.2 5.4 %copy-start.3 = (f32[6144]{0:T(1024)S(1)}, f32[6144]{0:T(1024)}, u32[]{:S(2)}) copy-start(f32[6144]{0:T(1024)} %param.9) | copy-start | bytes 73732
  44.7 7.2 %collective-permute-start = (f32[4,1,64,128]{3,2,0,1:T(8,128)S(1)}, f32[4,1,64,128]{3,2,0,1:T(8,128)S(1)}, u32[]{:S(2)}, u32[]{:S(2)}) collective-permute-start(f32[4,1,64,128]{3,2,0,1:T(8,128)S(1)} %slice.55), channel_id=1, source_target_pairs={{0,2},{2,4},{4,6},{6,8},{8,10},{10,12},{12,14},{14,16},{16,18},{18... | collective-permute-start | bytes 393224 | tf_op jit(solution)/shard_map/ppermute | solution.py:28
  44.8 7.2 %collective-permute-start.1 = (f32[4,1,64,128]{3,2,0,1:T(8,128)S(1)}, f32[4,1,64,128]{3,2,0,1:T(8,128)S(1)}, u32[]{:S(2)}, u32[]{:S(2)}) collective-permute-start(f32[4,1,64,128]{3,2,0,1:T(8,128)S(1)} %slice.55), channel_id=1, source_target_pairs={{2,0},{4,2},{6,4},{8,6},{10,8},{12,10},{14,12},{16,14},{18,16},{20... | collective-permute-start | bytes 393224 | tf_op jit(solution)/shard_map/ppermute | solution.py:30
  52.0 4.9 %collective-permute-start.2 = (f32[4,3,1,128]{3,2,0,1:T(1,128)S(1)}, f32[4,3,1,128]{3,2,0,1:T(1,128)S(1)}, u32[]{:S(2)}, u32[]{:S(2)}) collective-permute-start(f32[4,3,1,128]{3,2,0,1:T(1,128)S(1)} %get-tuple-element.47), channel_id=1, source_target_pairs={{0,1},{1,0},{2,3},{3,2},{4,5},{5,4},{6,7},{7,6},{8,9},{9,8},{10,11... | collective-permute-start | bytes 18440 | tf_op jit(solution)/shard_map/ppermute | solution.py:28
  52.2 4.7 %collective-permute-start.3 = (f32[4,3,1,128]{3,2,0,1:T(1,128)S(1)}, f32[4,3,1,128]{3,2,0,1:T(1,128)S(1)}, u32[]{:S(2)}, u32[]{:S(2)}) collective-permute-start(f32[4,3,1,128]{3,2,0,1:T(1,128)S(1)} %get-tuple-element.48), channel_id=1, source_target_pairs={{1,0},{0,1},{3,2},{2,3},{5,4},{4,5},{7,6},{6,7},{9,8},{8,9},{11,10... | collective-permute-start | bytes 18440 | tf_op jit(solution)/shard_map/ppermute | solution.py:30
  55.8 53.6 %collective-permute-start.4 = (f32[7,1,64,128]{3,2,0,1:T(8,128)}, f32[7,1,64,128]{3,2,0,1:T(8,128)S(1)}, u32[]{:S(2)}, u32[]{:S(2)}) collective-permute-start(f32[7,1,64,128]{3,2,0,1:T(8,128)} %reshape.105), channel_id=1, source_target_pairs={{0,16},{2,18},{4,20},{6,22},{8,24},{10,26},{12,28},{14,30},{16,0},... | collective-permute-start | bytes 688136 | tf_op jit(solution)/shard_map/ppermute | solution.py:18
  106.4 8.1 %collective-permute-start.5 = (f32[3,1,64,128]{3,2,0,1:T(8,128)S(1)}, f32[3,1,64,128]{3,2,0,1:T(8,128)S(1)}, u32[]{:S(2)}, u32[]{:S(2)}) collective-permute-start(f32[3,1,64,128]{3,2,0,1:T(8,128)S(1)} %multiply_bitcast_fusion.1), channel_id=1, source_target_pairs={{0,16},{2,18},{4,20},{6,22},{8,24},{10,26},{12,28},{14,30},{16,0},... | collective-permute-start | bytes 294920 | tf_op jit(solution)/shard_map/ppermute | solution.py:18
where the time goes:
time: 115 us
  other arithmetic  52.9 us (46%)
  local copies, waits for them, and re-layouts  31.5 us (27%)
  starting transfers between devices  9.54 us (8%)
  blocking collectives  9.03 us (8%)
  waiting for transfers between devices  7.78 us (7%)
  loops' own time  2.86 us (2%)
  between operations  1.6 us (1%)
    scatter x1, local copies, waits for them, and re-layouts, per_device(): jnp.zeros((7, CELLS * 128), jnp.float32).at[:, place]  17.8 us
    reduce_sum x32, other arithmetic, pair_accel(): return coupling * jnp.sum(weight[None] * separation, axis=2)  16.1 us
    reduce_sum x32, other arithmetic, pair_accel(): distance = jnp.sum(separation * separation, axis=0)  13.1 us
    mul x32, other arithmetic, pair_accel(): others[3][None, :] * jnp.exp(-distance / reach) * inverse * inverse  12.8 us
    all_to_all x1, blocking collectives, per_device(): lax.all_to_all(buffer, 'dom', split_axis=2, concat_axis=2, tiled=True)  9.03 us
    ppermute x2, starting transfers between devices, with_halo(): lax.ppermute(head, axis, [((i + 1) % count, i) for i in range(count)])  6.35 us
    reduce_sum x1, other arithmetic, per_device(): ranking = jnp.sum(jnp.cumsum(hits, axis=0) * hits, axis=1) - 1  5.24 us
    ppermute x2, waiting for transfers between devices, passed_along(): lax.ppermute(value, axis, [(i, (i + by) % size) for i in range(size)])  5.02 us
  transfers between devices with their start and end apart: 6, of which 2 were waited for; matrix products, arithmetic and copies ran while one was open for 43% of the time, Pallas kernels for 0%

commit v1 on v0

v1 whole, which is shorter than its diff:
```python
import functools
import math

import jax
import jax.numpy as jnp
from jax import lax
from jax.experimental import pallas as pl
from jax.experimental.pallas import tpu as pltpu
from jax.sharding import PartitionSpec as P

CELLS = 64
LANES = 128

drift_step = 0.5
kick_step = 0.5
soften = 0.25
reach = 4.0
coupling = 0.25

scale = math.log2(math.e) / reach
fold = scale**1.5 * math.exp(soften / reach)

f32 = jnp.float32
bf16 = jnp.bfloat16
NN = (((1,), (0,)), ((), ()))
NT = (((1,), (1,)), ((), ()))
TN = (((0,), (0,)), ((), ()))
FEATURES = 32
EDGES = 8


def split(value, pieces):
    parts = []
    for _ in range(pieces):
        head = value.astype(bf16).astype(f32)
        parts.append(head)
        value = value - head
    return parts


def pack_kernel(n_dom, me_ref, count_ref, pos_ref, vel_ref, mass_ref, owner_ref, *refs):
    outs, (hot_ref, rank_ref, total_ref) = refs[:-3], refs[-3:]
    rows = pos_ref.shape[1]
    targets, lanes = n_dom * CELLS, LANES // n_dom
    chunk = 256
    before = (
        lax.broadcasted_iota(jnp.int32, (chunk, chunk + LANES), 0)
        < lax.broadcasted_iota(jnp.int32, (chunk, chunk + LANES), 1)
    ).astype(f32).astype(bf16)
    carry = jnp.zeros((targets, LANES), f32)
    number = lax.broadcasted_iota(jnp.int32, (targets, chunk), 0)
    for at in range(0, rows, chunk):
        target = owner_ref[:, at : at + chunk] - me_ref[0] * CELLS
        target = jnp.where(target < 0, target + targets, target)
        place = lax.broadcasted_iota(jnp.int32, (1, chunk), 1) + at
        target = jnp.where(place < count_ref[0], target, -1)
        same = number == target
        hot = jnp.where(same, 1.0, 0.0).astype(bf16)
        hot_ref[:, at : at + chunk] = hot
        seen = lax.dot_general(hot, before, NN, preferred_element_type=f32)
        wide = jnp.concatenate([carry] * (chunk // LANES), axis=1)
        rank = jnp.sum(jnp.where(same, seen[:, :chunk] + wide, 0.0), axis=0, keepdims=True)
        rank_ref[:, at : at + chunk] = rank.astype(jnp.int32)
        carry = carry + seen[:, chunk:]
    step = 1024
    row = lax.broadcasted_iota(jnp.int32, (lanes, step), 0)
    for at in range(0, rows, step):
        span = slice(at, at + step)
        mark = jnp.where(row == rank_ref[:, span], 1.0, 0.0)
        values = [pos_ref[i : i + 1, span] + drift_step * vel_ref[i : i + 1, span] for i in range(3)]
        values += [mass_ref[:, span]]
        values += [vel_ref[i : i + 1, span] for i in range(3)]
        pieces = [split(value, 3) for value in values]
        hot = hot_ref[:, span]
        left = [
            jnp.concatenate([(mark * piece[k]).astype(bf16) for piece in pieces], axis=0)
            for k in range(3)
        ]
        part = lax.dot_general(
            jnp.concatenate(left, axis=1),
            jnp.concatenate([hot] * 3, axis=1),
            NT,
            preferred_element_type=f32,
        )
        size = 7 * lanes
        if at == 0:
            total_ref[:size] = part
            total_ref[size:] = jnp.zeros((lanes, targets), f32)
        else:
            total_ref[:size] += part
    groups = 8 * lanes // LANES
    half = groups // 2
    packed = [
        jnp.concatenate(
            [
                total_ref[g * LANES : (g + 1) * LANES, t : t + LANES].T
                for t in range(0, targets, LANES)
            ],
            axis=0,
        )
        for g in range(groups)
    ]
    for by in range(n_dom):
        low, high = by * CELLS, (by + 1) * CELLS
        edge_high, edge_low = high % targets, (low - 1) % targets
        for g in range(groups):
            edges = jnp.concatenate(
                [
                    packed[g][edge_high : edge_high + 1],
                    packed[g][edge_low : edge_low + 1],
                    jnp.zeros((EDGES - 2, LANES), f32),
                ],
                axis=0,
            )
            both = jnp.concatenate([packed[g][low:high], edges], axis=0)
            outs[by][g] = both
            if g < half:
                outs[n_dom + by][g] = both


def merged(pieces, comp, n_dom):
    lanes = LANES // n_dom
    group, inside = comp // n_dom, comp % n_dom
    plane = None
    for k, piece in enumerate(pieces):
        value = piece[group]
        shift = ((k - inside) % n_dom) * lanes
        if shift:
            value = pltpu.roll(value, shift, 1)
        if plane is None:
            plane = value
        else:
            lane = lax.broadcasted_iota(jnp.int32, value.shape, 1)
            plane = jnp.where(lane // lanes == k, value, plane)
    return plane


def put_rows(ref, slab, k, plane, stride):
    for at in range(0, CELLS, 8):
        ref[slab, pl.ds((at + 1) * stride + k, 8, stride=stride), :] = plane[at : at + 8]
    ref[slab, pl.ds((CELLS + 1) * stride + k, 1), :] = plane[CELLS : CELLS + 1]
    ref[slab, pl.ds(k, 1), :] = plane[CELLS + 1 : CELLS + 2]


def pair_kernel(n_dom, me_ref, *refs):
    n_in = 3 * n_dom
    ins, (state_ref, accel_ref) = refs[:n_in], refs[n_in : n_in + 2]
    far, near, summed, centre_rows, far_rows, sum_rows, out_rows, *work = refs[n_in + 2 :]
    dist, heavy, light = work[0:2], work[2:4], work[4:6]
    root = math.sqrt(scale)
    weight = coupling * fold / root
    own = None
    for slab in range(3):
        pieces = ins[slab * n_dom : (slab + 1) * n_dom]
        planes = [merged(pieces, comp, n_dom) for comp in range(4)]
        if slab == 1:
            own = [plane[:CELLS] for plane in planes]
        x = [plane * root for plane in planes[:3]]
        norm = x[0] * x[0] + x[1] * x[1] + x[2] * x[2]
        one, none = jnp.ones_like(norm), jnp.zeros_like(norm)
        cut = [split(value, 3) for value in x]
        far_feat, near_feat = [], []
        for h, m, l in cut:
            far_feat += [h, m, h, l, h, m]
            near_feat += [-2.0 * v for v in (h, h, m, h, l, m)]
        far_feat += [one] * 3 + split(norm, 3)
        near_feat += split(norm + scale * soften, 3) + [one] * 3
        for k in range(FEATURES):
            put_rows(far, slab, k, far_feat[k] if k < len(far_feat) else none, FEATURES)
            if slab == 1:
                value = near_feat[k] if k < len(near_feat) else none
                put_rows(near, 0, k, value, FEATURES)
        mass = planes[3] * weight
        terms = [split(mass * value, 3) for value in x] + [split(mass, 3)]
        for comp in range(4):
            for k in range(3):
                put_rows(summed, slab, 3 * comp + k, terms[comp][k], 16)
        for k in range(12, 16):
            put_rows(summed, slab, k, none, 16)

    def cast(e, _):
        for slab in range(3):
            rows = pl.ds(pl.multiple_of(e * FEATURES, FEATURES), FEATURES)
            far_rows[e, slab] = far[slab, rows, :].astype(bf16)
            sums = pl.ds(pl.multiple_of(e * 16, 16), 16)
            sum_rows[e, slab] = summed[slab, sums, :].astype(bf16)
        centre_rows[e] = near[0, rows, :].astype(bf16)
        return 0

    lax.fori_loop(0, CELLS + 2, cast, 0)

    def distances(c, b):
        for k in range(3):
            others = jnp.concatenate([far_rows[c + k, slab] for slab in range(3)], axis=1)
            dist[b][k * 384 : (k + 1) * 384] = lax.dot_general(
                others, centre_rows[c + 1], TN, preferred_element_type=f32
            )

    def weights(b):
        s = dist[b][...]
        inverse = lax.rsqrt(s)
        w = jnp.exp2(-s) * (inverse * inverse * inverse)
        head = w.astype(bf16)
        heavy[b][...] = head
        light[b][...] = (w - head.astype(f32)).astype(bf16)

    def sums(c, b):
        terms = jnp.concatenate(
            [sum_rows[c + k, slab] for k in range(3) for slab in range(3)], axis=1
        )
        total = lax.dot_general(terms, heavy[b][...], NN, preferred_element_type=f32)
        total += lax.dot_general(terms, light[b][...], NN, preferred_element_type=f32)
        out_rows[pl.ds(pl.multiple_of(c * 16, 16), 16), :] = total

    distances(0, 0)
    distances(1, 1)
    weights(0)

    def body(i, _):
        for b in range(2):
            c = 2 * i + b
            sums(c, b)
            distances(jnp.minimum(c + 2, CELLS - 1), b)
            weights(1 - b)
        return 0

    lax.fori_loop(0, CELLS // 2, body, 0)
    rows = [out_rows[pl.ds(k, CELLS, stride=16), :] for k in range(12)]
    total = [rows[3 * comp] + rows[3 * comp + 1] + rows[3 * comp + 2] for comp in range(4)]
    live = own[3] > 0
    turn = me_ref[0] * (LANES // n_dom)
    pieces = ins[n_dom : 2 * n_dom]
    for comp in range(3):
        accel = jnp.where(live, total[comp] - (own[comp] * root) * total[3], 0.0)
        accel = pltpu.roll(accel, turn, 1)
        speed = pltpu.roll(merged(pieces, 4 + comp, n_dom)[:CELLS], turn, 1)
        state_ref[comp, 0] = pltpu.roll(own[comp], turn, 1)
        state_ref[4 + comp, 0] = speed + kick_step * accel
        state_ref[7 + comp, 0] = accel
        accel_ref[comp] = accel
    state_ref[3, 0] = pltpu.roll(own[3], turn, 1)


def buddy_kernel(n_dom, me_ref, *refs):
    pieces, accel_ref, out_ref = refs[:n_dom], refs[n_dom], refs[n_dom + 1]
    turn = me_ref[0] * (LANES // n_dom)
    for comp in range(7):
        plane = pltpu.roll(merged(pieces, comp, n_dom)[:CELLS], turn, 1)
        if comp >= 4:
            accel = accel_ref[comp - 4]
            plane = plane + kick_step * accel
            out_ref[3 + comp, 0] = accel
        out_ref[comp, 0] = plane


def call(kernel, n_smem, n_vmem, out_shape, scratch=(), name=None, cost=None):
    smem = pl.BlockSpec(memory_space=pltpu.SMEM)
    vmem = pl.BlockSpec(memory_space=pltpu.VMEM)
    return pl.pallas_call(
        kernel,
        in_specs=[smem] * n_smem + [vmem] * n_vmem,
        out_specs=jax.tree.map(lambda _: vmem, out_shape),
        out_shape=out_shape,
        scratch_shapes=scratch,
        name=name,
        compiler_params=pltpu.CompilerParams(vmem_limit_bytes=48 << 20),
        cost_estimate=cost,
    )


def sent(value, n_slab, n_dom, by_slab, by_dom):
    pairs = [
        (s * n_dom + d, (s + by_slab) % n_slab * n_dom + (d + by_dom) % n_dom)
        for s in range(n_slab)
        for d in range(n_dom)
    ]
    return lax.ppermute(value, ("slab", "dom"), pairs)


def per_device(positions, velocities, masses, owner_cell, counts):
    n_slab, n_dom = lax.axis_size("slab"), lax.axis_size("dom")
    rows = positions.shape[1]
    lanes = LANES // n_dom
    targets = n_dom * CELLS
    groups = 8 * lanes // LANES
    half = groups // 2
    tall = CELLS + EDGES
    me = lax.axis_index("dom").astype(jnp.int32).reshape(1)
    shape = lambda *dims, dtype=f32: jax.ShapeDtypeStruct(dims, dtype)

    packed = call(
        functools.partial(pack_kernel, n_dom),
        2,
        4,
        [shape(groups, tall, LANES)] * n_dom + [shape(half, tall, LANES)] * n_dom,
        [
            pltpu.VMEM((targets, rows), bf16),
            pltpu.VMEM((1, rows), jnp.int32),
            pltpu.VMEM((8 * lanes, targets), f32),
        ],
        name="pack",
    )(me, counts, positions, velocities, masses.reshape(1, rows), owner_cell.reshape(1, rows))
    whole, shells = packed[:n_dom], packed[n_dom:]

    own = [whole[0]] + [sent(whole[-k % n_dom], n_slab, n_dom, 0, -k) for k in range(1, n_dom)]
    halo = {
        side: [sent(shells[-k % n_dom], n_slab, n_dom, side, -k) for k in range(n_dom)]
        for side in (1, -1)
    }
    early = [sent(piece, n_slab, n_dom, n_slab // 2, 0) for piece in own]
    state, accel = call(
        functools.partial(pair_kernel, n_dom),
        1,
        3 * n_dom,
        [shape(10, 1, CELLS, LANES), shape(3, CELLS, LANES)],
        [
            pltpu.VMEM((3, (CELLS + 2) * FEATURES, LANES), f32),
            pltpu.VMEM((1, (CELLS + 2) * FEATURES, LANES), f32),
            pltpu.VMEM((3, (CELLS + 2) * 16, LANES), f32),
            pltpu.VMEM((CELLS + 2, FEATURES, LANES), bf16),
            pltpu.VMEM((CELLS + 2, 3, FEATURES, LANES), bf16),
            pltpu.VMEM((CELLS + 2, 3, 16, LANES), bf16),
            pltpu.VMEM((CELLS * 16, LANES), f32),
        ]
        + [pltpu.VMEM((1152, LANES), f32)] * 2
        + [pltpu.VMEM((1152, LANES), bf16)] * 4,
        name="pairs",
    )(me, *halo[1], *own, *halo[-1])
    later = sent(accel, n_slab, n_dom, n_slab // 2, 0)
    buddy = call(
        functools.partial(buddy_kernel, n_dom),
        1,
        n_dom + 1,
        shape(10, 1, CELLS, LANES),
        name="buddy",
    )(me, *early, later)
    return state, buddy


def solution(mesh):
    placed = (
        P(None, ("slab", "dom")),
        P(None, ("slab", "dom")),
        P(("slab", "dom")),
        P(("slab", "dom"), None),
        P(("slab", "dom")),
    )
    return jax.shard_map(
        per_device,
        mesh=mesh,
        in_specs=placed,
        out_specs=(P(None, "slab", "dom", None), P(None, "slab", "dom", None)),
        check_vma=False,
    )
```

time: 115 us -> 62.1 us (0.54)
  other arithmetic: 52.9 us -> 0 us
  Pallas kernels: 0 us -> 32.4 us
  local copies, waits for them, and re-layouts: 31.5 us -> 3.25 us
  blocking collectives: 9.03 us -> 0 us
  starting transfers between devices: 9.54 us -> 14 us
  waiting for transfers between devices: 7.78 us -> 10.8 us
  loops' own time: 2.86 us -> 0 us
    reduce_sum x65 -> x0, other arithmetic: 34.5 us -> none  [the longest x32 16.1 us: pair_accel(): return coupling * jnp.sum(weight[None] * separation, axis=2)]
    pallas_call x0 -> x3, Pallas kernels: none -> 32.4 us  [the longest x1 25.6 us: per_device(): call(functools.partial(pair_kernel, n_dom), 1, 3 * n_dom, [shape(10, 1, C...]
    scatter x1 -> x0, local copies, waits for them, and re-layouts: 17.8 us -> none  [per_device(): jnp.zeros((7, CELLS * 128), jnp.float32).at[:, place]]
    mul x65 -> x0, other arithmetic: 13 us -> none  [the longest x32 12.8 us: pair_accel(): others[3][None, :] * jnp.exp(-distance / reach) * inverse * inverse]
    all_to_all x1 -> x0, blocking collectives: 9.03 us -> none  [per_device(): lax.all_to_all(buffer, 'dom', split_axis=2, concat_axis=2, tiled=True)]
    ppermute x6 -> x8, starting transfers between devices: 9.54 us -> 14 us  [sent(): return lax.ppermute(value, ('slab', 'dom'), pairs)]
    reshape x2 -> x0, local copies, waits for them, and re-layouts: 4.07 us -> none  [the longest x1 3.1 us: per_device(): buffer = buffer.reshape(7, CELLS, n_dom, lanes)]
    ppermute x6 -> x8, waiting for transfers between devices: 7.78 us -> 10.8 us  [sent(): return lax.ppermute(value, ('slab', 'dom'), pairs)]
  transfers between devices with their start and end apart: 6 -> 8, of which waited for: 2 -> 2; matrix products, arithmetic and copies ran while one was open for 43% -> 0% of each run, Pallas kernels for 0% -> 41%
where the time goes in v1:
time: 62.1 us; the launch traced here: 61.8 us
  Pallas kernels  32.4 us (52%)
  starting transfers between devices  14 us (23%)
  waiting for transfers between devices  10.8 us (17%)
  local copies, waits for them, and re-layouts  3.25 us (5%)
  between operations  1.31 us (2%)
    pallas_call x1, Pallas kernels, per_device(): call(functools.partial(pair_kernel, n_dom), 1, 3 * n_dom, [shape(10, 1, C...  25.6 us
    ppermute x8, starting transfers between devices, sent(): return lax.ppermute(value, ('slab', 'dom'), pairs)  14 us
    ppermute x8, waiting for transfers between devices, sent(): return lax.ppermute(value, ('slab', 'dom'), pairs)  10.8 us
    pallas_call x1, Pallas kernels, per_device(): call(functools.partial(pack_kernel, n_dom), 2, 4, [shape(groups, tall, LA...  5.84 us
    unnamed x8, local copies, waits for them, and re-layouts  3.25 us
  transfers between devices with their start and end apart: 8, of which 2 were waited for; matrix products, arithmetic and copies ran while one was open for 0% of the time, Pallas kernels for 41%

profile of v1, /device:TPU:0, one launch (start us, length us, event | category | flops | bytes accessed | tf_op | source)
XLA Modules:
  0.0 61.8 jit_solution(5494471847958063775)
XLA Ops:
  1.3 0.0 copy-start
  1.3 0.9 %copy-done = f32[3,6144]{1,0:T(4,128)S(1)} copy-done((f32[3,6144]{1,0:T(4,128)S(1)}, f32[3,6144]{1,0:T(4,128)}, u32[]{:S(2)}) %copy-start) | copy-done | bytes 73752
  2.2 0.9 %copy-done.1 = f32[3,6144]{1,0:T(4,128)S(1)} copy-done((f32[3,6144]{1,0:T(4,128)S(1)}, f32[3,6144]{1,0:T(4,128)}, u32[]{:S(2)}) %copy-start.1) | copy-done | bytes 73752
  3.1 0.7 %copy-done.2 = f32[6144]{0:T(1024)S(1)} copy-done((f32[6144]{0:T(1024)S(1)}, f32[6144]{0:T(1024)}, u32[]{:S(2)}) %copy-start.2) | copy-done | bytes 24600
  3.8 0.7 %copy-done.3 = s32[6144,1]{0,1:T(1,128)S(1)} copy-done((s32[6144,1]{0,1:T(1,128)S(1)}, s32[6144,1]{0,1:T(1,128)}, u32[]{:S(2)}) %copy-start.3) | copy-done | bytes 24600
  4.5 5.8 %pack.1 = (f32[4,72,128]{2,1,0:T(8,128)S(1)}, f32[4,72,128]{2,1,0:T(8,128)S(1)}, f32[2,72,128]{2,1,0:T(8,128)S(1)}, f32[2,72,128]{2,1,0:T(8,128)S(1)}) custom-call(s32[1]{0:T(128)} %bitcast.me_ref, s32[1]{0:T(128)S(6)} %copy.7.count_ref, f32[3,6144]{1,0:T(4,128)S(1)} %copy-done, f32[3,6144]{1,0:T(4,128)S(1)} %copy-done.1, f32[1,6144]{1,0:T(1,128)S(1)} %bitcast.3, ...), custom_call_target="tpu_custom_call" | custom-call | tf_op jit(solution)/shard_map/pack/pallas_call | solution.py:291
  10.4 3.0 %collective-permute-start.2 = (f32[4,72,128]{2,1,0:T(8,128)S(1)}, f32[4,72,128]{2,1,0:T(8,128)S(1)}, u32[]{:S(2)}, u32[]{:S(2)}) collective-permute-start(f32[4,72,128]{2,1,0:T(8,128)S(1)} %get-tuple-element.11), channel_id=1, source_target_pairs={{0,1},{1,0},{2,3},{3,2},{4,5},{5,4},{6,7},{7,6},{8,9},{9,8},{10,11... | collective-permute-start | bytes 442376 | tf_op jit(solution)/shard_map/ppermute | solution.py:277
  13.4 3.7 %collective-permute-start.3 = (f32[2,72,128]{2,1,0:T(8,128)S(1)}, f32[2,72,128]{2,1,0:T(8,128)S(1)}, u32[]{:S(2)}, u32[]{:S(2)}) collective-permute-start(f32[2,72,128]{2,1,0:T(8,128)S(1)} %get-tuple-element.8), channel_id=1, source_target_pairs={{0,30},{1,31},{2,0},{3,1},{4,2},{5,3},{6,4},{7,5},{8,6},{9,7},{10,... | collective-permute-start | bytes 221192 | tf_op jit(solution)/shard_map/ppermute | solution.py:277
  17.1 0.0 collective-permute-start
  17.1 4.4 %collective-permute-start.4 = (f32[2,72,128]{2,1,0:T(8,128)S(1)}, f32[2,72,128]{2,1,0:T(8,128)S(1)}, u32[]{:S(2)}, u32[]{:S(2)}) collective-permute-start(f32[2,72,128]{2,1,0:T(8,128)S(1)} %get-tuple-element.9), channel_id=1, source_target_pairs={{0,31},{1,30},{2,1},{3,0},{4,3},{5,2},{6,5},{7,4},{8,7},{9,6},{10,... | collective-permute-start | bytes 221192 | tf_op jit(solution)/shard_map/ppermute | solution.py:277
  21.5 0.0 collective-permute-start.1
  21.5 0.0 collective-permute-done.3.refs_4_
  21.5 0.0 collective-permute-start.5
  21.5 0.0 collective-permute-done.2.refs_3_
  21.5 2.9 %collective-permute-start.6 = (f32[4,72,128]{2,1,0:T(8,128)S(1)}, f32[4,72,128]{2,1,0:T(8,128)S(1)}, u32[]{:S(2)}, u32[]{:S(2)}) collective-permute-start(f32[4,72,128]{2,1,0:T(8,128)S(1)} %collective-permute-done.2.refs_3_), channel_id=1, source_target_pairs={{0,16},{1,17},{2,18},{3,19},{4,20},{5,21},{6,22},{7,23},{8,24},{9,... | collective-permute-start | bytes 442376 | tf_op jit(solution)/shard_map/ppermute | solution.py:277
  24.4 0.0 collective-permute-done.refs_0_
  24.4 0.0 collective-permute-done.4.refs_5_
  24.4 5.3 %collective-permute-done.1.refs_1_ = f32[2,72,128]{2,1,0:T(8,128)S(1)} collective-permute-done((f32[2,72,128]{2,1,0:T(8,128)S(1)}, f32[2,72,128]{2,1,0:T(8,128)S(1)}, u32[]{:S(2)}, u32[]{:S(2)}) %collective-permute-start.1) | collective-permute-done | bytes 73760 | tf_op jit(solution)/shard_map/ppermute | solution.py:277
  29.7 25.6 %pairs.1 = (f32[10,1,64,128]{3,2,1,0:T(8,128)}, f32[3,64,128]{2,1,0:T(8,128)S(1)}) custom-call(s32[1]{0:T(128)} %bitcast.me_ref, f32[2,72,128]{2,1,0:T(8,128)S(1)} %collective-permute-done.refs_0_, f32[2,72,128]{2,1,0:T(8,128)S(1)} %collective-permute-done.1.refs_1_, f32[4,72,128]{2,1,0:T(8,128)S(1)} %get-tuple-element.10.refs_2_, ...), custom_call_target="tpu_custom_call" | custom-call | tf_op jit(solution)/shard_map/pairs/pallas_call | solution.py:311
  55.3 0.0 collective-permute-start.7
  55.3 0.0 collective-permute-done.5.refs_0_
  55.3 5.5 %collective-permute-done.7.refs_2_ = f32[3,64,128]{2,1,0:T(8,128)S(1)} collective-permute-done((f32[3,64,128]{2,1,0:T(8,128)S(1)}, f32[3,64,128]{2,1,0:T(8,128)S(1)}, u32[]{:S(2)}, u32[]{:S(2)}) %collective-permute-start.7) | collective-permute-done | bytes 98336 | tf_op jit(solution)/shard_map/ppermute | solution.py:277
  60.8 0.0 collective-permute-done.6.refs_1_
  60.8 1.0 %buddy.1 = f32[10,1,64,128]{3,2,1,0:T(8,128)} custom-call(s32[1]{0:T(128)} %bitcast.me_ref, f32[4,72,128]{2,1,0:T(8,128)S(1)} %collective-permute-done.5.refs_0_, f32[4,72,128]{2,1,0:T(8,128)S(1)} %collective-permute-done.6.refs_1_, f32[3,64,128]{2,1,0:T(8,128)S(1)} %collective-permute-done.7.refs_2_), custom_call_target="tpu_custom_call" | custom-call | tf_op jit(solution)/shard_map/buddy/pallas_call | solution.py:330
  (3 shorter events, 0.0 us)
Async XLA Ops:
  1.3 0.9 %copy-start = (f32[3,6144]{1,0:T(4,128)S(1)}, f32[3,6144]{1,0:T(4,128)}, u32[]{:S(2)}) copy-start(f32[3,6144]{1,0:T(4,128)} %pos_ref.1) | copy-start | bytes 221188
  2.2 0.9 %copy-start.1 = (f32[3,6144]{1,0:T(4,128)S(1)}, f32[3,6144]{1,0:T(4,128)}, u32[]{:S(2)}) copy-start(f32[3,6144]{1,0:T(4,128)} %vel_ref.1) | copy-start | bytes 221188
  3.1 0.7 %copy-start.2 = (f32[6144]{0:T(1024)S(1)}, f32[6144]{0:T(1024)}, u32[]{:S(2)}) copy-start(f32[6144]{0:T(1024)} %param.7) | copy-start | bytes 73732
  3.8 0.7 %copy-start.3 = (s32[6144,1]{0,1:T(1,128)S(1)}, s32[6144,1]{0,1:T(1,128)}, u32[]{:S(2)}) copy-start(s32[6144,1]{0,1:T(1,128)} %param.8) | copy-start | bytes 73732
  10.4 11.1 %collective-permute-start.2 = (f32[4,72,128]{2,1,0:T(8,128)S(1)}, f32[4,72,128]{2,1,0:T(8,128)S(1)}, u32[]{:S(2)}, u32[]{:S(2)}) collective-permute-start(f32[4,72,128]{2,1,0:T(8,128)S(1)} %get-tuple-element.11), channel_id=1, source_target_pairs={{0,1},{1,0},{2,3},{3,2},{4,5},{5,4},{6,7},{7,6},{8,9},{9,8},{10,11... | collective-permute-start | bytes 442376 | tf_op jit(solution)/shard_map/ppermute | solution.py:277
  13.4 8.1 %collective-permute-start.3 = (f32[2,72,128]{2,1,0:T(8,128)S(1)}, f32[2,72,128]{2,1,0:T(8,128)S(1)}, u32[]{:S(2)}, u32[]{:S(2)}) collective-permute-start(f32[2,72,128]{2,1,0:T(8,128)S(1)} %get-tuple-element.8), channel_id=1, source_target_pairs={{0,30},{1,31},{2,0},{3,1},{4,2},{5,3},{6,4},{7,5},{8,6},{9,7},{10,... | collective-permute-start | bytes 221192 | tf_op jit(solution)/shard_map/ppermute | solution.py:277
  17.1 7.3 %collective-permute-start = (f32[2,72,128]{2,1,0:T(8,128)S(1)}, f32[2,72,128]{2,1,0:T(8,128)S(1)}, u32[]{:S(2)}, u32[]{:S(2)}) collective-permute-start(f32[2,72,128]{2,1,0:T(8,128)S(1)} %get-tuple-element.8), channel_id=1, source_target_pairs={{0,2},{1,3},{2,4},{3,5},{4,6},{5,7},{6,8},{7,9},{8,10},{9,11},{10,... | collective-permute-start | bytes 221192 | tf_op jit(solution)/shard_map/ppermute | solution.py:277
  17.1 7.3 %collective-permute-start.4 = (f32[2,72,128]{2,1,0:T(8,128)S(1)}, f32[2,72,128]{2,1,0:T(8,128)S(1)}, u32[]{:S(2)}, u32[]{:S(2)}) collective-permute-start(f32[2,72,128]{2,1,0:T(8,128)S(1)} %get-tuple-element.9), channel_id=1, source_target_pairs={{0,31},{1,30},{2,1},{3,0},{4,3},{5,2},{6,5},{7,4},{8,7},{9,6},{10,... | collective-permute-start | bytes 221192 | tf_op jit(solution)/shard_map/ppermute | solution.py:277
  21.5 8.2 %collective-permute-start.1 = (f32[2,72,128]{2,1,0:T(8,128)S(1)}, f32[2,72,128]{2,1,0:T(8,128)S(1)}, u32[]{:S(2)}, u32[]{:S(2)}) collective-permute-start(f32[2,72,128]{2,1,0:T(8,128)S(1)} %get-tuple-element.9), channel_id=1, source_target_pairs={{0,3},{1,2},{2,5},{3,4},{4,7},{5,6},{6,9},{7,8},{8,11},{9,10},{10,... | collective-permute-start | bytes 221192 | tf_op jit(solution)/shard_map/ppermute | solution.py:277
  21.5 33.8 %collective-permute-start.5 = (f32[4,72,128]{2,1,0:T(8,128)S(1)}, f32[4,72,128]{2,1,0:T(8,128)S(1)}, u32[]{:S(2)}, u32[]{:S(2)}) collective-permute-start(f32[4,72,128]{2,1,0:T(8,128)S(1)} %get-tuple-element.10.refs_2_), channel_id=1, source_target_pairs={{0,16},{1,17},{2,18},{3,19},{4,20},{5,21},{6,22},{7,23},{8,24},{9,... | collective-permute-start | bytes 442376 | tf_op jit(solution)/shard_map/ppermute | solution.py:277
  21.5 39.3 %collective-permute-start.6 = (f32[4,72,128]{2,1,0:T(8,128)S(1)}, f32[4,72,128]{2,1,0:T(8,128)S(1)}, u32[]{:S(2)}, u32[]{:S(2)}) collective-permute-start(f32[4,72,128]{2,1,0:T(8,128)S(1)} %collective-permute-done.2.refs_3_), channel_id=1, source_target_pairs={{0,16},{1,17},{2,18},{3,19},{4,20},{5,21},{6,22},{7,23},{8,24},{9,... | collective-permute-start | bytes 442376 | tf_op jit(solution)/shard_map/ppermute | solution.py:277
  55.3 5.5 %collective-permute-start.7 = (f32[3,64,128]{2,1,0:T(8,128)S(1)}, f32[3,64,128]{2,1,0:T(8,128)S(1)}, u32[]{:S(2)}, u32[]{:S(2)}) collective-permute-start(f32[3,64,128]{2,1,0:T(8,128)S(1)} %get-tuple-element.13), channel_id=1, source_target_pairs={{0,16},{1,17},{2,18},{3,19},{4,20},{5,21},{6,22},{7,23},{8,24},{9,... | collective-permute-start | bytes 294920 | tf_op jit(solution)/shard_map/ppermute | solution.py:277

commit v2 on v1

v2 whole, which is shorter than its diff:
```python
import functools
import math

import jax
import jax.numpy as jnp
from jax import lax
from jax.experimental import pallas as pl
from jax.experimental.pallas import tpu as pltpu
from jax.sharding import PartitionSpec as P

CELLS = 64
LANES = 128

drift_step = 0.5
kick_step = 0.5
soften = 0.25
reach = 4.0
coupling = 0.25

scale = math.log2(math.e) / reach
fold = scale**1.5 * math.exp(soften / reach)

f32 = jnp.float32
bf16 = jnp.bfloat16
NN = (((1,), (0,)), ((), ()))
NT = (((1,), (1,)), ((), ()))
TN = (((0,), (0,)), ((), ()))
FEATURES = 32
EDGES = 8


def split(value, pieces):
    parts = []
    for _ in range(pieces):
        head = value.astype(bf16).astype(f32)
        parts.append(head)
        value = value - head
    return parts


def pack_kernel(n_dom, me_ref, count_ref, pos_ref, vel_ref, mass_ref, owner_ref, *refs):
    outs, (hot_ref, rank_ref, total_ref) = refs[:-3], refs[-3:]
    rows = pos_ref.shape[1]
    targets, lanes = n_dom * CELLS, LANES // n_dom
    chunk = 256
    before = (
        lax.broadcasted_iota(jnp.int32, (chunk, chunk + LANES), 0)
        < lax.broadcasted_iota(jnp.int32, (chunk, chunk + LANES), 1)
    ).astype(f32).astype(bf16)
    carry = jnp.zeros((targets, LANES), f32)
    number = lax.broadcasted_iota(jnp.int32, (targets, chunk), 0)
    for at in range(0, rows, chunk):
        target = owner_ref[:, at : at + chunk] - me_ref[0] * CELLS
        target = jnp.where(target < 0, target + targets, target)
        place = lax.broadcasted_iota(jnp.int32, (1, chunk), 1) + at
        target = jnp.where(place < count_ref[0], target, -1)
        same = number == target
        hot = jnp.where(same, 1.0, 0.0).astype(bf16)
        hot_ref[:, at : at + chunk] = hot
        seen = lax.dot_general(hot, before, NN, preferred_element_type=f32)
        wide = jnp.concatenate([carry] * (chunk // LANES), axis=1)
        rank = jnp.sum(jnp.where(same, seen[:, :chunk] + wide, 0.0), axis=0, keepdims=True)
        rank_ref[:, at : at + chunk] = rank.astype(jnp.int32)
        carry = carry + seen[:, chunk:]
    step = 1024
    row = lax.broadcasted_iota(jnp.int32, (lanes, step), 0)
    for at in range(0, rows, step):
        span = slice(at, at + step)
        mark = jnp.where(row == rank_ref[:, span], 1.0, 0.0)
        values = [pos_ref[i : i + 1, span] + drift_step * vel_ref[i : i + 1, span] for i in range(3)]
        values += [mass_ref[:, span]]
        values += [vel_ref[i : i + 1, span] for i in range(3)]
        pieces = [split(value, 3) for value in values]
        hot = hot_ref[:, span]
        left = [
            jnp.concatenate([(mark * piece[k]).astype(bf16) for piece in pieces], axis=0)
            for k in range(3)
        ]
        part = lax.dot_general(
            jnp.concatenate(left, axis=1),
            jnp.concatenate([hot] * 3, axis=1),
            NT,
            preferred_element_type=f32,
        )
        size = 7 * lanes
        if at == 0:
            total_ref[:size] = part
            total_ref[size:] = jnp.zeros((lanes, targets), f32)
        else:
            total_ref[:size] += part
    groups = 8 * lanes // LANES
    packed = [
        jnp.concatenate(
            [
                total_ref[g * LANES : (g + 1) * LANES, t : t + LANES].T
                for t in range(0, targets, LANES)
            ],
            axis=0,
        )
        for g in range(groups)
    ]
    for by in range(n_dom):
        low, high = by * CELLS, (by + 1) * CELLS
        edge_high, edge_low = high % targets, (low - 1) % targets
        for g in range(groups):
            edges = jnp.concatenate(
                [
                    packed[g][edge_high : edge_high + 1],
                    packed[g][edge_low : edge_low + 1],
                    jnp.zeros((EDGES - 2, LANES), f32),
                ],
                axis=0,
            )
            both = jnp.concatenate([packed[g][low:high], edges], axis=0)
            outs[by][g] = both


def merged(pieces, comp, n_dom):
    lanes = LANES // n_dom
    group, inside = comp // n_dom, comp % n_dom
    plane = None
    for k, piece in enumerate(pieces):
        value = piece[group]
        shift = ((k - inside) % n_dom) * lanes
        if shift:
            value = pltpu.roll(value, shift, 1)
        if plane is None:
            plane = value
        else:
            lane = lax.broadcasted_iota(jnp.int32, value.shape, 1)
            plane = jnp.where(lane // lanes == k, value, plane)
    return plane


def put_rows(ref, k, plane, stride, cells, edges):
    low, high = cells
    for c in range(low - edges, high + edges):
        if c >= 0 and c % 8 == 0 and c + 8 <= min(high + edges, CELLS):
            at = (c - low + edges) * stride + k
            ref[pl.ds(at, 8, stride=stride), :] = plane[c : c + 8]
        elif c < 0 or c >= CELLS or c < -(-max(low - edges, 0) // 8) * 8 or c >= min(high + edges, CELLS) // 8 * 8:
            row = CELLS + 1 if c < 0 else c
            at = (c - low + edges) * stride + k
            ref[pl.ds(at, 1), :] = plane[row : row + 1]


def build(shells_ref, cells, far, summed, near=None):
    root = math.sqrt(scale)
    x = [shells_ref[comp] * root for comp in range(3)]
    norm = x[0] * x[0] + x[1] * x[1] + x[2] * x[2]
    one, none = jnp.ones_like(norm), jnp.zeros_like(norm)
    far_feat, near_feat = [], []
    for h, m, l in [split(value, 3) for value in x]:
        far_feat += [h, m, h, l, h, m]
        near_feat += [-2.0 * v for v in (h, h, m, h, l, m)]
    far_feat += [one] * 3 + split(norm, 3)
    near_feat += split(norm + scale * soften, 3) + [one] * 3
    for k in range(FEATURES):
        put_rows(far, k, far_feat[k] if k < len(far_feat) else none, FEATURES, cells, 1)
        if near is not None:
            put_rows(near, k, near_feat[k] if k < len(near_feat) else none, FEATURES, cells, 0)
    mass = shells_ref[3] * (coupling * fold / root)
    terms = [part for value in x + [None] for part in split(mass if value is None else mass * value, 3)]
    for k in range(16):
        put_rows(summed, k, terms[k] if k < 12 else none, 16, cells, 1)


def cast_rows(pairs):
    for source, target in pairs:
        tall = target.shape[1]
        for e in range(target.shape[0]):
            target[e] = source[e * tall : (e + 1) * tall].astype(bf16)


def pair_loop(count, per, far_rows, sum_rows, centre, out, dist, heavy, light):
    blocks = [(k, n) for k in range(3) for n in range(len(far_rows))]
    tall = LANES * len(blocks)
    wide = 3

    def distances(step, b):
        for u in range(per):
            c = step * per + u
            for at in range(0, len(blocks), wide):
                others = jnp.concatenate(
                    [far_rows[n][c + k] for k, n in blocks[at : at + wide]], axis=1
                )
                low = u * tall + at * LANES
                dist[b][low : low + wide * LANES] = lax.dot_general(
                    others, centre(c), TN, preferred_element_type=f32
                )

    def weights(b):
        for at in range(0, per * tall, 64):
            s = dist[b][at : at + 64]
            inverse = lax.rsqrt(s)
            w = jnp.exp2(-s) * (inverse * inverse * inverse)
            head = w.astype(bf16)
            heavy[b][at : at + 64] = head
            light[b][at : at + 64] = (w - head.astype(f32)).astype(bf16)

    def sums(step, b):
        for u in range(per):
            c = step * per + u
            terms = jnp.concatenate([sum_rows[n][c + k] for k, n in blocks], axis=1)
            span = slice(u * tall, (u + 1) * tall)
            total = lax.dot_general(terms, heavy[b][span], NN, preferred_element_type=f32)
            total += lax.dot_general(terms, light[b][span], NN, preferred_element_type=f32)
            out[c] = total

    steps = count // per
    distances(0, 0)
    distances(1, 1)
    weights(0)

    def body(i, _):
        for b in range(2):
            step = 2 * i + b
            sums(step, b)
            distances(jnp.minimum(step + 2, steps - 1), b)
            weights(1 - b)
        return 0

    lax.fori_loop(0, steps // 2, body, 0)


def join_kernel(n_dom, me_ref, *refs):
    pieces, (shells_ref, planes_ref) = refs[:n_dom], refs[n_dom:]
    turn = me_ref[0] * (LANES // n_dom)
    for comp in range(7):
        plane = pltpu.roll(merged(pieces, comp, n_dom), turn, 1)
        if comp < 4:
            shells_ref[comp] = plane
        planes_ref[comp] = plane[:CELLS]


def own_kernel(shells_ref, near_out, out_ref, far, near, summed, far_rows, sum_rows, *work):
    cells = (0, CELLS)
    build(shells_ref, cells, far, summed, near)
    cast_rows([(far, far_rows), (near, near_out), (summed, sum_rows)])
    centre = lambda c: near_out[c]
    pair_loop(
        CELLS, 2, [far_rows], [sum_rows], centre, out_ref, work[0:2], work[2:4], work[4:6]
    )


def side_kernel(cells, up_ref, down_ref, near_ref, own_out, planes_ref, accel_ref, *refs):
    low, high = cells
    fars, sums, far_rows, sum_rows = refs[0:2], refs[2:4], refs[4:6], refs[6:8]
    out, work = refs[8], refs[9:]
    for side, shells_ref in enumerate((up_ref, down_ref)):
        build(shells_ref, cells, fars[side], sums[side])
    cast_rows([(fars[0], far_rows[0]), (fars[1], far_rows[1]), (sums[0], sum_rows[0]), (sums[1], sum_rows[1])])
    centre = lambda c: near_ref[c + low]
    pair_loop(
        high - low, 1, far_rows, sum_rows, centre, out, work[0:2], work[2:4], work[4:6]
    )
    flat = out.reshape((high - low) * 16, LANES)
    flat_own = own_out.reshape(CELLS * 16, LANES)
    rows = [
        flat[pl.ds(k, high - low, stride=16), :]
        + flat_own[pl.ds(low * 16 + k, high - low, stride=16), :]
        for k in range(12)
    ]
    total = [rows[3 * comp] + rows[3 * comp + 1] + rows[3 * comp + 2] for comp in range(4)]
    live = planes_ref[3, low:high] > 0
    for comp in range(3):
        centre_at = planes_ref[comp, low:high] * math.sqrt(scale)
        accel_ref[comp] = jnp.where(live, total[comp] - centre_at * total[3], 0.0)


def kick_kernel(planes_ref, *refs):
    accels, out_ref = refs[:-1], refs[-1]
    for comp in range(4):
        out_ref[comp, 0] = planes_ref[comp]
    low = 0
    for accel_ref in accels:
        high = low + accel_ref.shape[1]
        for comp in range(3):
            accel = accel_ref[comp]
            out_ref[4 + comp, 0, low:high] = planes_ref[4 + comp, low:high] + kick_step * accel
            out_ref[7 + comp, 0, low:high] = accel
        low = high


def call(kernel, n_smem, n_vmem, out_shape, scratch=(), name=None, cost=None, n_block=0):
    smem = pl.BlockSpec(memory_space=pltpu.SMEM)
    vmem = pl.BlockSpec(memory_space=pltpu.VMEM)
    block = pl.BlockSpec()
    return pl.pallas_call(
        kernel,
        in_specs=[smem] * n_smem + [block] * n_block + [vmem] * n_vmem,
        out_specs=jax.tree.map(lambda _: vmem, out_shape),
        out_shape=out_shape,
        scratch_shapes=scratch,
        name=name,
        compiler_params=pltpu.CompilerParams(vmem_limit_bytes=48 << 20),
        cost_estimate=cost,
    )


def sent(value, n_slab, n_dom, by_slab, by_dom):
    pairs = [
        (s * n_dom + d, (s + by_slab) % n_slab * n_dom + (d + by_dom) % n_dom)
        for s in range(n_slab)
        for d in range(n_dom)
    ]
    return lax.ppermute(value, ("slab", "dom"), pairs)


def per_device(positions, velocities, masses, owner_cell, counts):
    n_slab, n_dom = lax.axis_size("slab"), lax.axis_size("dom")
    rows = positions.shape[1]
    lanes = LANES // n_dom
    targets = n_dom * CELLS
    groups = 8 * lanes // LANES
    tall = CELLS + EDGES
    me = lax.axis_index("dom").astype(jnp.int32).reshape(1)
    shape = lambda *dims, dtype=f32: jax.ShapeDtypeStruct(dims, dtype)

    whole = call(
        functools.partial(pack_kernel, n_dom),
        2,
        0,
        [shape(groups, tall, LANES)] * n_dom,
        [
            pltpu.VMEM((targets, rows), bf16),
            pltpu.VMEM((1, rows), jnp.int32),
            pltpu.VMEM((8 * lanes, targets), f32),
        ],
        name="pack",
        n_block=4,
    )(me, counts, positions, velocities, masses.reshape(1, rows), owner_cell.reshape(1, rows))

    own = [whole[0]] + [sent(whole[-k % n_dom], n_slab, n_dom, 0, -k) for k in range(1, n_dom)]
    shells, planes = call(
        functools.partial(join_kernel, n_dom),
        1,
        n_dom,
        [shape(4, tall, LANES), shape(7, CELLS, LANES)],
        name="join",
    )(me, *own)
    below, above = (sent(shells, n_slab, n_dom, side, 0) for side in (1, -1))
    early = sent(planes, n_slab, n_dom, n_slab // 2, 0)

    def pair_work(size):
        return [pltpu.VMEM((size, LANES), f32)] * 2 + [pltpu.VMEM((size, LANES), bf16)] * 4

    def row_work(count, copies):
        edged = count + 2
        return (
            [pltpu.VMEM((edged * FEATURES, LANES), f32)] * copies,
            [pltpu.VMEM((edged * 16, LANES), f32)] * copies,
            [pltpu.VMEM((edged, FEATURES, LANES), bf16)] * copies,
            [pltpu.VMEM((edged, 16, LANES), bf16)] * copies,
        )

    far, summed, far_rows, sum_rows = row_work(CELLS, 1)
    near, sums = call(
        own_kernel,
        0,
        1,
        [shape(CELLS, FEATURES, LANES, dtype=bf16), shape(CELLS, 16, LANES)],
        far + [pltpu.VMEM((CELLS * FEATURES, LANES), f32)] + summed + far_rows + sum_rows + pair_work(768),
        name="own_slab",
        cost=pl.CostEstimate(flops=8_000_000_000, bytes_accessed=1_000_000, transcendentals=0),
    )(shells)
    accels = []
    for cells in ((0, 40), (40, CELLS)):
        count = cells[1] - cells[0]
        far, summed, far_rows, sum_rows = row_work(count, 2)
        accels.append(
            call(
                functools.partial(side_kernel, cells),
                0,
                5,
                shape(3, count, LANES),
                far + summed + far_rows + sum_rows + [pltpu.VMEM((count, 16, LANES), f32)] + pair_work(768),
                name="side_slabs",
                cost=pl.CostEstimate(flops=8_000_000_000, bytes_accessed=1_000_000, transcendentals=0),
            )(below, above, near, sums, planes)
        )
    later = [sent(accel, n_slab, n_dom, n_slab // 2, 0) for accel in accels]
    out = shape(10, 1, CELLS, LANES)
    state = call(kick_kernel, 0, 3, out, name="state")(planes, *accels)
    buddy = call(kick_kernel, 0, 3, out, name="buddy")(early, *later)
    return state, buddy


def solution(mesh):
    placed = (
        P(None, ("slab", "dom")),
        P(None, ("slab", "dom")),
        P(("slab", "dom")),
        P(("slab", "dom"), None),
        P(("slab", "dom")),
    )
    return jax.shard_map(
        per_device,
        mesh=mesh,
        in_specs=placed,
        out_specs=(P(None, "slab", "dom", None), P(None, "slab", "dom", None)),
        check_vma=False,
    )
```

time: 62.1 us -> 58.4 us (0.940)
  waiting for transfers between devices: 10.8 us -> 6.94 us
  Pallas kernels: 32.4 us -> 34.9 us
  starting transfers between devices: 14 us -> 11.7 us
    ppermute x8 -> x6, waiting for transfers between devices: 10.8 us -> 6.94 us  [sent(): return lax.ppermute(value, ('slab', 'dom'), pairs)]
    pallas_call x3 -> x7, Pallas kernels: 32.4 us -> 34.9 us  [the longest x2 17.7 us: per_device(): call(functools.partial(side_kernel, cells), 0, 5, shape(3, count, LANES),...]
    ppermute x8 -> x6, starting transfers between devices: 14 us -> 11.7 us  [sent(): return lax.ppermute(value, ('slab', 'dom'), pairs)]
  transfers between devices with their start and end apart: 8 -> 6, of which waited for: 2 -> 2; matrix products, arithmetic and copies ran while one was open for 0% -> 0% of each run, Pallas kernels for 41% -> 48%
where the time goes in v2:
time: 58.4 us; the launch traced here: 58.1 us
  Pallas kernels  34.9 us (60%)
  starting transfers between devices  11.7 us (20%)
  waiting for transfers between devices  6.94 us (12%)
  local copies, waits for them, and re-layouts  3.25 us (6%)
  between operations  1.33 us (2%)
    pallas_call x2, Pallas kernels, per_device(): call(functools.partial(side_kernel, cells), 0, 5, shape(3, count, LANES),...  17.7 us
    ppermute x6, starting transfers between devices, sent(): return lax.ppermute(value, ('slab', 'dom'), pairs)  11.7 us
    pallas_call x1, Pallas kernels, per_device(): call(own_kernel, 0, 1, [shape(CELLS, FEATURES, LANES, dtype=bf16), shape(...  9.6 us
    ppermute x6, waiting for transfers between devices, sent(): return lax.ppermute(value, ('slab', 'dom'), pairs)  6.94 us
    pallas_call x1, Pallas kernels, per_device(): call(functools.partial(pack_kernel, n_dom), 2, 0, [shape(groups, tall, LA...  5.84 us
    unnamed x8, local copies, waits for them, and re-layouts  3.25 us
  transfers between devices with their start and end apart: 6, of which 2 were waited for; matrix products, arithmetic and copies ran while one was open for 0% of the time, Pallas kernels for 48%

profile of v2, /device:TPU:0, one launch (start us, length us, event | category | flops | bytes accessed | tf_op | source)
XLA Modules:
  0.0 58.1 jit_solution(5039853404509771686)
XLA Ops:
  1.3 0.0 copy-start
  1.3 0.9 %copy-done = f32[3,6144]{1,0:T(4,128)S(1)} copy-done((f32[3,6144]{1,0:T(4,128)S(1)}, f32[3,6144]{1,0:T(4,128)}, u32[]{:S(2)}) %copy-start) | copy-done | bytes 73752
  2.2 0.9 %copy-done.1 = f32[3,6144]{1,0:T(4,128)S(1)} copy-done((f32[3,6144]{1,0:T(4,128)S(1)}, f32[3,6144]{1,0:T(4,128)}, u32[]{:S(2)}) %copy-start.1) | copy-done | bytes 73752
  3.1 0.7 %copy-done.2 = f32[6144]{0:T(1024)S(1)} copy-done((f32[6144]{0:T(1024)S(1)}, f32[6144]{0:T(1024)}, u32[]{:S(2)}) %copy-start.2) | copy-done | bytes 24600
  3.8 0.7 %copy-done.3 = s32[6144,1]{0,1:T(1,128)S(1)} copy-done((s32[6144,1]{0,1:T(1,128)S(1)}, s32[6144,1]{0,1:T(1,128)}, u32[]{:S(2)}) %copy-start.3) | copy-done | bytes 24600
  4.5 5.8 %pack.1 = (f32[4,72,128]{2,1,0:T(8,128)S(1)}, f32[4,72,128]{2,1,0:T(8,128)S(1)}) custom-call(s32[1]{0:T(128)} %bitcast.me_ref, s32[1]{0:T(128)S(6)} %copy.7.count_ref, f32[3,6144]{1,0:T(4,128)S(1)} %copy-done, f32[3,6144]{1,0:T(4,128)S(1)} %copy-done.1, f32[1,6144]{1,0:T(1,128)S(1)} %bitcast.3, s32[1,6144]{1,0:T(1,128)S(1)} %bitcast.4), custom_call_target="tpu_custom_call" | custom-call | tf_op jit(solution)/shard_map/pack/pallas_call | solution.py:320
  10.4 3.0 %collective-permute-start = (f32[4,72,128]{2,1,0:T(8,128)S(1)}, f32[4,72,128]{2,1,0:T(8,128)S(1)}, u32[]{:S(2)}, u32[]{:S(2)}) collective-permute-start(f32[4,72,128]{2,1,0:T(8,128)S(1)} %get-tuple-element.9), channel_id=1, source_target_pairs={{0,1},{1,0},{2,3},{3,2},{4,5},{5,4},{6,7},{7,6},{8,9},{9,8},{10,11... | collective-permute-start | bytes 442376 | tf_op jit(solution)/shard_map/ppermute | solution.py:307
  13.4 3.8 %collective-permute-done.refs_1_ = f32[4,72,128]{2,1,0:T(8,128)S(1)} collective-permute-done((f32[4,72,128]{2,1,0:T(8,128)S(1)}, f32[4,72,128]{2,1,0:T(8,128)S(1)}, u32[]{:S(2)}, u32[]{:S(2)}) %collective-permute-start) | collective-permute-done | bytes 147488 | tf_op jit(solution)/shard_map/ppermute | solution.py:307
  17.3 0.2 join.1
  17.5 0.1 collective-permute-start.1
  17.6 4.4 %collective-permute-start.2 = (f32[4,72,128]{2,1,0:T(8,128)S(1)}, f32[4,72,128]{2,1,0:T(8,128)S(1)}, u32[]{:S(2)}, u32[]{:S(2)}) collective-permute-start(f32[4,72,128]{2,1,0:T(8,128)S(1)} %get-tuple-element.11.shells_ref), channel_id=1, source_target_pairs={{0,30},{1,31},{2,0},{3,1},{4,2},{5,3},{6,4},{7,5},{8,6},{9,7},{10,... | collective-permute-start | bytes 442376 | tf_op jit(solution)/shard_map/ppermute | solution.py:307
  22.0 9.6 %own_slab.1 = (bf16[64,32,128]{2,1,0:T(8,128)(2,1)S(1)}, f32[64,16,128]{2,1,0:T(8,128)S(1)}) custom-call(f32[4,72,128]{2,1,0:T(8,128)S(1)} %get-tuple-element.11.shells_ref), custom_call_target="tpu_custom_call" | custom-call | flops 8000000000 | bytes 1000000 | tf_op jit(solution)/shard_map/own_slab/pallas_call | solution.py:358
  31.6 1.1 %collective-permute-start.3 = (f32[7,64,128]{2,1,0:T(8,128)S(1)}, f32[7,64,128]{2,1,0:T(8,128)S(1)}, u32[]{:S(2)}, u32[]{:S(2)}) collective-permute-start(f32[7,64,128]{2,1,0:T(8,128)S(1)} %get-tuple-element.10.planes_ref), channel_id=1, source_target_pairs={{0,16},{1,17},{2,18},{3,19},{4,20},{5,21},{6,22},{7,23},{8,24},{9,... | collective-permute-start | bytes 688136 | tf_op jit(solution)/shard_map/ppermute | solution.py:307
  32.7 0.0 collective-permute-done.1.up_ref
  32.7 0.0 collective-permute-done.2.down_ref
  32.7 11.0 %side_slabs.2.refs_0_ = f32[3,40,128]{2,1,0:T(8,128)S(1)} custom-call(f32[4,72,128]{2,1,0:T(8,128)S(1)} %collective-permute-done.1.up_ref, f32[4,72,128]{2,1,0:T(8,128)S(1)} %collective-permute-done.2.down_ref, bf16[64,32,128]{2,1,0:T(8,128)(2,1)S(1)} %get-tuple-element.12.near_ref, f32[64,16,128]{2,1,0:T(8,128)S(1)} %get-tuple-element.13.own_out, ...), custom_call_target="tpu_custom_call" | custom-call | flops 8000000000 | bytes 1000000 | tf_op jit(solution)/shard_map/side_slabs/pallas_call | solution.py:372
  43.7 2.0 %collective-permute-start.4 = (f32[3,40,128]{2,1,0:T(8,128)S(1)}, f32[3,40,128]{2,1,0:T(8,128)S(1)}, u32[]{:S(2)}, u32[]{:S(2)}) collective-permute-start(f32[3,40,128]{2,1,0:T(8,128)S(1)} %side_slabs.2.refs_0_), channel_id=1, source_target_pairs={{0,16},{1,17},{2,18},{3,19},{4,20},{5,21},{6,22},{7,23},{8,24},{9,... | collective-permute-start | bytes 184328 | tf_op jit(solution)/shard_map/ppermute | solution.py:307
  45.7 6.7 %side_slabs.3.refs_1_ = f32[3,24,128]{2,1,0:T(8,128)S(1)} custom-call(f32[4,72,128]{2,1,0:T(8,128)S(1)} %collective-permute-done.1.up_ref, f32[4,72,128]{2,1,0:T(8,128)S(1)} %collective-permute-done.2.down_ref, bf16[64,32,128]{2,1,0:T(8,128)(2,1)S(1)} %get-tuple-element.12.near_ref, f32[64,16,128]{2,1,0:T(8,128)S(1)} %get-tuple-element.13.own_out, ...), custom_call_target="tpu_custom_call" | custom-call | flops 8000000000 | bytes 1000000 | tf_op jit(solution)/shard_map/side_slabs/pallas_call | solution.py:372
  52.4 1.1 %collective-permute-start.5 = (f32[3,24,128]{2,1,0:T(8,128)S(1)}, f32[3,24,128]{2,1,0:T(8,128)S(1)}, u32[]{:S(2)}, u32[]{:S(2)}) collective-permute-start(f32[3,24,128]{2,1,0:T(8,128)S(1)} %side_slabs.3.refs_1_), channel_id=1, source_target_pairs={{0,16},{1,17},{2,18},{3,19},{4,20},{5,21},{6,22},{7,23},{8,24},{9,... | collective-permute-start | bytes 110600 | tf_op jit(solution)/shard_map/ppermute | solution.py:307
  53.5 0.7 %state.1 = f32[10,1,64,128]{3,2,1,0:T(8,128)} custom-call(f32[7,64,128]{2,1,0:T(8,128)S(1)} %get-tuple-element.10.planes_ref, f32[3,40,128]{2,1,0:T(8,128)S(1)} %side_slabs.2.refs_0_, f32[3,24,128]{2,1,0:T(8,128)S(1)} %side_slabs.3.refs_1_), custom_call_target="tpu_custom_call" | custom-call | tf_op jit(solution)/shard_map/state/pallas_call | solution.py:384
  54.2 3.1 %collective-permute-done.5.refs_1_ = f32[3,24,128]{2,1,0:T(8,128)S(1)} collective-permute-done((f32[3,24,128]{2,1,0:T(8,128)S(1)}, f32[3,24,128]{2,1,0:T(8,128)S(1)}, u32[]{:S(2)}, u32[]{:S(2)}) %collective-permute-start.5) | collective-permute-done | bytes 36896 | tf_op jit(solution)/shard_map/ppermute | solution.py:307
  57.3 0.0 collective-permute-done.4.refs_0_
  57.3 0.0 collective-permute-done.3.planes_ref
  57.3 0.8 %buddy.1 = f32[10,1,64,128]{3,2,1,0:T(8,128)} custom-call(f32[7,64,128]{2,1,0:T(8,128)S(1)} %collective-permute-done.3.planes_ref, f32[3,40,128]{2,1,0:T(8,128)S(1)} %collective-permute-done.4.refs_0_, f32[3,24,128]{2,1,0:T(8,128)S(1)} %collective-permute-done.5.refs_1_), custom_call_target="tpu_custom_call" | custom-call | tf_op jit(solution)/shard_map/buddy/pallas_call | solution.py:385
  (3 shorter events, 0.0 us)
Async XLA Ops:
  1.3 0.9 %copy-start = (f32[3,6144]{1,0:T(4,128)S(1)}, f32[3,6144]{1,0:T(4,128)}, u32[]{:S(2)}) copy-start(f32[3,6144]{1,0:T(4,128)} %pos_ref.1) | copy-start | bytes 221188
  2.2 0.9 %copy-start.1 = (f32[3,6144]{1,0:T(4,128)S(1)}, f32[3,6144]{1,0:T(4,128)}, u32[]{:S(2)}) copy-start(f32[3,6144]{1,0:T(4,128)} %vel_ref.1) | copy-start | bytes 221188
  3.1 0.7 %copy-start.2 = (f32[6144]{0:T(1024)S(1)}, f32[6144]{0:T(1024)}, u32[]{:S(2)}) copy-start(f32[6144]{0:T(1024)} %param.7) | copy-start | bytes 73732
  3.8 0.7 %copy-start.3 = (s32[6144,1]{0,1:T(1,128)S(1)}, s32[6144,1]{0,1:T(1,128)}, u32[]{:S(2)}) copy-start(s32[6144,1]{0,1:T(1,128)} %param.8) | copy-start | bytes 73732
  10.4 6.9 %collective-permute-start = (f32[4,72,128]{2,1,0:T(8,128)S(1)}, f32[4,72,128]{2,1,0:T(8,128)S(1)}, u32[]{:S(2)}, u32[]{:S(2)}) collective-permute-start(f32[4,72,128]{2,1,0:T(8,128)S(1)} %get-tuple-element.9), channel_id=1, source_target_pairs={{0,1},{1,0},{2,3},{3,2},{4,5},{5,4},{6,7},{7,6},{8,9},{9,8},{10,11... | collective-permute-start | bytes 442376 | tf_op jit(solution)/shard_map/ppermute | solution.py:307
  17.5 15.2 %collective-permute-start.1 = (f32[4,72,128]{2,1,0:T(8,128)S(1)}, f32[4,72,128]{2,1,0:T(8,128)S(1)}, u32[]{:S(2)}, u32[]{:S(2)}) collective-permute-start(f32[4,72,128]{2,1,0:T(8,128)S(1)} %get-tuple-element.11.shells_ref), channel_id=1, source_target_pairs={{0,2},{1,3},{2,4},{3,5},{4,6},{5,7},{6,8},{7,9},{8,10},{9,11},{10,... | collective-permute-start | bytes 442376 | tf_op jit(solution)/shard_map/ppermute | solution.py:307
  17.6 15.1 %collective-permute-start.2 = (f32[4,72,128]{2,1,0:T(8,128)S(1)}, f32[4,72,128]{2,1,0:T(8,128)S(1)}, u32[]{:S(2)}, u32[]{:S(2)}) collective-permute-start(f32[4,72,128]{2,1,0:T(8,128)S(1)} %get-tuple-element.11.shells_ref), channel_id=1, source_target_pairs={{0,30},{1,31},{2,0},{3,1},{4,2},{5,3},{6,4},{7,5},{8,6},{9,7},{10,... | collective-permute-start | bytes 442376 | tf_op jit(solution)/shard_map/ppermute | solution.py:307
  31.6 25.7 %collective-permute-start.3 = (f32[7,64,128]{2,1,0:T(8,128)S(1)}, f32[7,64,128]{2,1,0:T(8,128)S(1)}, u32[]{:S(2)}, u32[]{:S(2)}) collective-permute-start(f32[7,64,128]{2,1,0:T(8,128)S(1)} %get-tuple-element.10.planes_ref), channel_id=1, source_target_pairs={{0,16},{1,17},{2,18},{3,19},{4,20},{5,21},{6,22},{7,23},{8,24},{9,... | collective-permute-start | bytes 688136 | tf_op jit(solution)/shard_map/ppermute | solution.py:307
  43.7 13.6 %collective-permute-start.4 = (f32[3,40,128]{2,1,0:T(8,128)S(1)}, f32[3,40,128]{2,1,0:T(8,128)S(1)}, u32[]{:S(2)}, u32[]{:S(2)}) collective-permute-start(f32[3,40,128]{2,1,0:T(8,128)S(1)} %side_slabs.2.refs_0_), channel_id=1, source_target_pairs={{0,16},{1,17},{2,18},{3,19},{4,20},{5,21},{6,22},{7,23},{8,24},{9,... | collective-permute-start | bytes 184328 | tf_op jit(solution)/shard_map/ppermute | solution.py:307
  52.4 4.9 %collective-permute-start.5 = (f32[3,24,128]{2,1,0:T(8,128)S(1)}, f32[3,24,128]{2,1,0:T(8,128)S(1)}, u32[]{:S(2)}, u32[]{:S(2)}) collective-permute-start(f32[3,24,128]{2,1,0:T(8,128)S(1)} %side_slabs.3.refs_1_), channel_id=1, source_target_pairs={{0,16},{1,17},{2,18},{3,19},{4,20},{5,21},{6,22},{7,23},{8,24},{9,... | collective-permute-start | bytes 110600 | tf_op jit(solution)/shard_map/ppermute | solution.py:307

commit v3 on v2

v3 whole, which is shorter than its diff:
```python
import functools
import math

import jax
import jax.numpy as jnp
from jax import lax
from jax.experimental import pallas as pl
from jax.experimental.pallas import tpu as pltpu
from jax.sharding import PartitionSpec as P

CELLS = 64
LANES = 128

drift_step = 0.5
kick_step = 0.5
soften = 0.25
reach = 4.0
coupling = 0.25

scale = math.log2(math.e) / reach
fold = scale**1.5 * math.exp(soften / reach)

f32 = jnp.float32
bf16 = jnp.bfloat16
NN = (((1,), (0,)), ((), ()))
NT = (((1,), (1,)), ((), ()))
TN = (((0,), (0,)), ((), ()))
FEATURES = 32
EDGES = 8


def split(value, pieces):
    parts = []
    for _ in range(pieces):
        head = value.astype(bf16).astype(f32)
        parts.append(head)
        value = value - head
    return parts


def pack_kernel(n_dom, me_ref, count_ref, pos_any, vel_any, mass_any, owner_any, *refs):
    outs, refs = refs[:n_dom], refs[n_dom:]
    pos_ref, vel_ref, mass_ref, owner_ref, rank_ref, target_ref, total_ref, sems = refs
    copies = [
        pltpu.make_async_copy(source, target, sems.at[i])
        for i, (source, target) in enumerate(
            [(owner_any, owner_ref), (pos_any, pos_ref), (vel_any, vel_ref), (mass_any, mass_ref)]
        )
    ]
    for copy in copies:
        copy.start()
    rows = pos_ref.shape[1]
    targets, lanes = n_dom * CELLS, LANES // n_dom
    part = lanes // 2
    chunk = 256
    before = (
        lax.broadcasted_iota(jnp.int32, (chunk, chunk + LANES), 0)
        < lax.broadcasted_iota(jnp.int32, (chunk, chunk + LANES), 1)
    ).astype(f32).astype(bf16)
    carry = jnp.zeros((targets, LANES), f32)
    number = lax.broadcasted_iota(jnp.int32, (targets, chunk), 0)
    copies[0].wait()
    for at in range(0, rows, chunk):
        target = owner_ref[:, at : at + chunk] - me_ref[0] * CELLS
        target = jnp.where(target < 0, target + targets, target)
        place = lax.broadcasted_iota(jnp.int32, (1, chunk), 1) + at
        target = jnp.where(place < count_ref[0], target, -1)
        target_ref[:, at : at + chunk] = target
        same = number == target
        hot = jnp.where(same, 1.0, 0.0).astype(bf16)
        seen = lax.dot_general(hot, before, NN, preferred_element_type=f32)
        wide = jnp.concatenate([carry] * (chunk // LANES), axis=1)
        rank = jnp.sum(jnp.where(same, seen[:, :chunk] + wide, 0.0), axis=0, keepdims=True)
        rank_ref[:, at : at + chunk] = rank.astype(jnp.int32)
        carry = carry + seen[:, chunk:]
    for copy in copies[1:]:
        copy.wait()
    step = 1024
    row = lax.broadcasted_iota(jnp.int32, (part, step), 0)
    column = lax.broadcasted_iota(jnp.int32, (2 * targets, step), 0)
    for at in range(0, rows, step):
        span = slice(at, at + step)
        rank, target = rank_ref[:, span], target_ref[:, span]
        upper = rank >= part
        mark = jnp.where(row == jnp.where(upper, rank - part, rank), 1.0, 0.0)
        place = jnp.where(upper & (target >= 0), target + targets, target)
        hot = jnp.where(column == place, 1.0, 0.0).astype(bf16)
        values = [pos_ref[i : i + 1, span] + drift_step * vel_ref[i : i + 1, span] for i in range(3)]
        values += [mass_ref[:, span]]
        values += [vel_ref[i : i + 1, span] for i in range(3)]
        pieces = [split(value, 2) for value in values]
        left = [
            jnp.concatenate([(mark * piece[k]).astype(bf16) for piece in pieces], axis=0)
            for k in range(2)
        ]
        found = lax.dot_general(
            jnp.concatenate(left, axis=1),
            jnp.concatenate([hot] * 2, axis=1),
            NT,
            preferred_element_type=f32,
        )
        for comp in range(7):
            for half in range(2):
                low = comp * lanes + half * part
                value = found[comp * part : (comp + 1) * part, half * targets : (half + 1) * targets]
                if at == 0:
                    total_ref[low : low + part] = value
                else:
                    total_ref[low : low + part] += value
    total_ref[7 * lanes :] = jnp.zeros((lanes, targets), f32)
    groups = 8 * lanes // LANES
    packed = [
        jnp.concatenate(
            [
                total_ref[g * LANES : (g + 1) * LANES, t : t + LANES].T
                for t in range(0, targets, LANES)
            ],
            axis=0,
        )
        for g in range(groups)
    ]
    for by in range(n_dom):
        low, high = by * CELLS, (by + 1) * CELLS
        edge_high, edge_low = high % targets, (low - 1) % targets
        for g in range(groups):
            edges = jnp.concatenate(
                [
                    packed[g][edge_high : edge_high + 1],
                    packed[g][edge_low : edge_low + 1],
                    jnp.zeros((EDGES - 2, LANES), f32),
                ],
                axis=0,
            )
            outs[by][g] = jnp.concatenate([packed[g][low:high], edges], axis=0)


def merged(pieces, comp, n_dom):
    lanes = LANES // n_dom
    group, inside = comp // n_dom, comp % n_dom
    plane = None
    for k, piece in enumerate(pieces):
        value = piece[group]
        shift = ((k - inside) % n_dom) * lanes
        if shift:
            value = pltpu.roll(value, shift, 1)
        if plane is None:
            plane = value
        else:
            lane = lax.broadcasted_iota(jnp.int32, value.shape, 1)
            plane = jnp.where(lane // lanes == k, value, plane)
    return plane


def build(shells_ref, rows_ref, far_ref, sum_ref, near_ref=None):
    root = math.sqrt(scale)
    tall = shells_ref.shape[1]
    rows_ref[...] = jnp.zeros_like(rows_ref)
    for at in range(0, tall, 8):
        for comp in range(4):
            rows_ref[pl.ds(at * 8 + comp, 8, stride=8), :] = shells_ref[comp, at : at + 8, :]
    for at in range(0, tall, 8):
        value = rows_ref[at * 8 : (at + 8) * 8]
        row = lax.broadcasted_iota(jnp.int32, value.shape, 0) % 8

        def spread(array):
            total = jnp.sum(array.reshape(8, 8, LANES), axis=1, keepdims=True)
            return jnp.broadcast_to(total, (8, 8, LANES)).reshape(64, LANES)

        mass = spread(jnp.where(row == 3, value, 0.0)) * (coupling * fold / root)
        place = jnp.where(row < 3, value * root, 0.0)
        norm = spread(place * place)
        h, m, l = split(place, 3)
        down = lambda array, by: pltpu.roll(array, by, 0)

        def ends(array, first):
            parts = split(array, 3)
            ones = (row >= 3 - first) & (row < 6 - first)
            kept = jnp.where(ones, 1.0, 0.0)
            for i in range(3):
                kept = jnp.where(row == first + i, parts[i], kept)
            return kept

        def put(ref, groups):
            both = [
                jnp.concatenate(
                    [groups[i].reshape(8, 8, LANES), groups[i + 1].reshape(8, 8, LANES)], axis=1
                )
                for i in range(0, len(groups), 2)
            ]
            count = min(8, ref.shape[0] - at)
            if count > 0:
                value = jnp.concatenate(both, axis=1).astype(bf16)
                ref[at : at + count] = value[:count]

        h3, m3, l3 = down(h, 3), down(m, 3), down(l, 3)
        put(far_ref, [h + m3, h + l3, h + m3, ends(norm, 3)])
        if near_ref is not None:
            near = [-2.0 * (h + h3), -2.0 * (m + h3), -2.0 * (l + m3)]
            put(near_ref, near + [ends(norm + scale * soften, 0)])
        terms = split(mass * jnp.where(row == 3, 1.0, place), 3)
        put(sum_ref, [terms[0] + down(terms[1], 4), terms[2]])


def pair_loop(cells, per, far_rows, sum_rows, centre, out, dist, heavy, light):
    blocks = [(k, n) for k in range(3) for n in range(len(far_rows))]
    tall = LANES * len(blocks)
    wide = 3
    first, count = cells[0], cells[1] - cells[0]

    def beside(c, k):
        at = c + first + k - 1
        return jnp.where(at < 0, CELLS + 1, at) if k == 0 else at

    def distances(step, b):
        for u in range(per):
            c = step * per + u
            for at in range(0, len(blocks), wide):
                others = jnp.concatenate(
                    [far_rows[n][beside(c, k)] for k, n in blocks[at : at + wide]], axis=1
                )
                low = u * tall + at * LANES
                dist[b][low : low + wide * LANES] = lax.dot_general(
                    others, centre[c + first], TN, preferred_element_type=f32
                )

    def weights(b):
        for at in range(0, per * tall, 64):
            s = dist[b][at : at + 64]
            inverse = lax.rsqrt(s)
            w = jnp.exp2(-s) * (inverse * inverse * inverse)
            head = w.astype(bf16)
            heavy[b][at : at + 64] = head
            light[b][at : at + 64] = (w - head.astype(f32)).astype(bf16)

    def sums(step, b):
        for u in range(per):
            c = step * per + u
            terms = jnp.concatenate([sum_rows[n][beside(c, k)] for k, n in blocks], axis=1)
            span = slice(u * tall, (u + 1) * tall)
            total = lax.dot_general(terms, heavy[b][span], NN, preferred_element_type=f32)
            total += lax.dot_general(terms, light[b][span], NN, preferred_element_type=f32)
            out[c] = total

    steps = count // per
    distances(0, 0)
    distances(1, 1)
    weights(0)

    def body(i, _):
        for b in range(2):
            step = 2 * i + b
            sums(step, b)
            distances(jnp.minimum(step + 2, steps - 1), b)
            weights(1 - b)
        return 0

    lax.fori_loop(0, steps // 2, body, 0)


def join_kernel(n_dom, me_ref, *refs):
    pieces, (shells_ref, planes_ref) = refs[:n_dom], refs[n_dom:]
    turn = me_ref[0] * (LANES // n_dom)
    for comp in range(7):
        plane = pltpu.roll(merged(pieces, comp, n_dom), turn, 1)
        if comp < 4:
            shells_ref[comp] = plane
        planes_ref[comp] = plane[:CELLS]


def own_kernel(shells_ref, near_out, out_ref, rows, far_rows, sum_rows, *work):
    build(shells_ref, rows, far_rows, sum_rows, near_out)
    pair_loop(
        (0, CELLS), 2, [far_rows], [sum_rows], near_out, out_ref, work[0:2], work[2:4], work[4:6]
    )


def side_kernel(cells, up_ref, down_ref, near_ref, own_out, planes_ref, accel_ref, *refs):
    low, high = cells
    count = high - low
    rows, far_rows, sum_rows, out, work = refs[0], refs[1:3], refs[3:5], refs[5], refs[6:]
    for side, shells_ref in enumerate((up_ref, down_ref)):
        build(shells_ref, rows, far_rows[side], sum_rows[side])
    pair_loop(cells, 1, far_rows, sum_rows, near_ref, out, work[0:2], work[2:4], work[4:6])
    both = out[...] + own_out[low:high]
    both = (both[:, :8] + both[:, 8:]).reshape(count * 8, LANES)
    rows[: count * 8] = both + pltpu.roll(both, count * 8 - 4, 0)
    total = [rows[pl.ds(comp, count, stride=8), :] for comp in range(4)]
    live = planes_ref[3, low:high] > 0
    for comp in range(3):
        centre_at = planes_ref[comp, low:high] * math.sqrt(scale)
        accel_ref[comp] = jnp.where(live, total[comp] - centre_at * total[3], 0.0)


def kick_kernel(planes_ref, *refs):
    accels, out_ref = refs[:-1], refs[-1]
    for comp in range(4):
        out_ref[comp, 0] = planes_ref[comp]
    low = 0
    for accel_ref in accels:
        high = low + accel_ref.shape[1]
        for comp in range(3):
            accel = accel_ref[comp]
            out_ref[4 + comp, 0, low:high] = planes_ref[4 + comp, low:high] + kick_step * accel
            out_ref[7 + comp, 0, low:high] = accel
        low = high


def call(kernel, n_smem, n_vmem, out_shape, scratch=(), name=None, cost=None, n_any=0):
    smem = pl.BlockSpec(memory_space=pltpu.SMEM)
    vmem = pl.BlockSpec(memory_space=pltpu.VMEM)
    here = pl.BlockSpec(memory_space=pl.ANY)
    return pl.pallas_call(
        kernel,
        in_specs=[smem] * n_smem + [here] * n_any + [vmem] * n_vmem,
        out_specs=jax.tree.map(lambda _: vmem, out_shape),
        out_shape=out_shape,
        scratch_shapes=scratch,
        name=name,
        compiler_params=pltpu.CompilerParams(vmem_limit_bytes=48 << 20),
        cost_estimate=cost,
    )


def sent(value, n_slab, n_dom, by_slab, by_dom):
    pairs = [
        (s * n_dom + d, (s + by_slab) % n_slab * n_dom + (d + by_dom) % n_dom)
        for s in range(n_slab)
        for d in range(n_dom)
    ]
    return lax.ppermute(value, ("slab", "dom"), pairs)


def per_device(positions, velocities, masses, owner_cell, counts):
    n_slab, n_dom = lax.axis_size("slab"), lax.axis_size("dom")
    rows = positions.shape[1]
    lanes = LANES // n_dom
    targets = n_dom * CELLS
    groups = 8 * lanes // LANES
    tall = CELLS + EDGES
    me = lax.axis_index("dom").astype(jnp.int32).reshape(1)
    shape = lambda *dims, dtype=f32: jax.ShapeDtypeStruct(dims, dtype)

    whole = call(
        functools.partial(pack_kernel, n_dom),
        2,
        0,
        [shape(groups, tall, LANES)] * n_dom,
        [
            pltpu.VMEM((3, rows), f32),
            pltpu.VMEM((3, rows), f32),
            pltpu.VMEM((1, rows), f32),
            pltpu.VMEM((1, rows), jnp.int32),
            pltpu.VMEM((1, rows), jnp.int32),
            pltpu.VMEM((1, rows), jnp.int32),
            pltpu.VMEM((8 * lanes, targets), f32),
            pltpu.SemaphoreType.DMA((4,)),
        ],
        name="pack",
        n_any=4,
    )(me, counts, positions, velocities, masses.reshape(1, rows), owner_cell.reshape(1, rows))

    own = [whole[0]] + [sent(whole[-k % n_dom], n_slab, n_dom, 0, -k) for k in range(1, n_dom)]
    shells, planes = call(
        functools.partial(join_kernel, n_dom),
        1,
        n_dom,
        [shape(4, tall, LANES), shape(7, CELLS, LANES)],
        name="join",
    )(me, *own)
    below, above = (sent(shells, n_slab, n_dom, side, 0) for side in (1, -1))
    early = sent(planes, n_slab, n_dom, n_slab // 2, 0)

    def pair_work(size):
        return [pltpu.VMEM((size, LANES), f32)] * 2 + [pltpu.VMEM((size, LANES), bf16)] * 4

    def row_work(copies):
        return (
            [pltpu.VMEM((tall * 8, LANES), f32)]
            + [pltpu.VMEM((tall, FEATURES, LANES), bf16)] * copies
            + [pltpu.VMEM((tall, 16, LANES), bf16)] * copies
        )

    near, sums = call(
        own_kernel,
        0,
        1,
        [shape(CELLS, FEATURES, LANES, dtype=bf16), shape(CELLS, 16, LANES)],
        row_work(1) + pair_work(768),
        name="own_slab",
        cost=pl.CostEstimate(flops=8_000_000_000, bytes_accessed=1_000_000, transcendentals=0),
    )(shells)
    accels = []
    for cells in ((0, 40), (40, CELLS)):
        count = cells[1] - cells[0]
        accels.append(
            call(
                functools.partial(side_kernel, cells),
                0,
                5,
                shape(3, count, LANES),
                row_work(2) + [pltpu.VMEM((count, 16, LANES), f32)] + pair_work(768),
                name="side_slabs",
                cost=pl.CostEstimate(flops=8_000_000_000, bytes_accessed=1_000_000, transcendentals=0),
            )(below, above, near, sums, planes)
        )
    later = [sent(accel, n_slab, n_dom, n_slab // 2, 0) for accel in accels]
    out = shape(10, 1, CELLS, LANES)
    state = call(kick_kernel, 0, 3, out, name="state")(planes, *accels)
    buddy = call(kick_kernel, 0, 3, out, name="buddy")(early, *later)
    return state, buddy


def solution(mesh):
    placed = (
        P(None, ("slab", "dom")),
        P(None, ("slab", "dom")),
        P(("slab", "dom")),
        P(("slab", "dom"), None),
        P(("slab", "dom")),
    )
    return jax.shard_map(
        per_device,
        mesh=mesh,
        in_specs=placed,
        out_specs=(P(None, "slab", "dom", None), P(None, "slab", "dom", None)),
        check_vma=False,
    )
```

time: 58.4 us -> 54.9 us (0.940)
  Pallas kernels: 34.9 us -> 31.4 us
    pallas_call x1, Pallas kernels: 5.84 us -> 4.26 us  [per_device(): call(functools.partial(pack_kernel, n_dom), 2, 0, [shape(groups, tall, LA...]
    pallas_call x1, Pallas kernels: 9.6 us -> 8.27 us  [per_device(): call(own_kernel, 0, 1, [shape(CELLS, FEATURES, LANES, dtype=bf16), shape(...]
    pallas_call x2, Pallas kernels: 17.7 us -> 17.1 us  [per_device(): call(functools.partial(side_kernel, cells), 0, 5, shape(3, count, LANES),...]
where the time goes in v3:
time: 54.9 us; the launch traced here: 54.6 us
  Pallas kernels  31.4 us (57%)
  starting transfers between devices  11.6 us (21%)
  waiting for transfers between devices  6.96 us (13%)
  local copies, waits for them, and re-layouts  3.25 us (6%)
  between operations  1.34 us (2%)
    pallas_call x2, Pallas kernels, per_device(): call(functools.partial(side_kernel, cells), 0, 5, shape(3, count, LANES),...  17.1 us
    ppermute x6, starting transfers between devices, sent(): return lax.ppermute(value, ('slab', 'dom'), pairs)  11.6 us
    pallas_call x1, Pallas kernels, per_device(): call(own_kernel, 0, 1, [shape(CELLS, FEATURES, LANES, dtype=bf16), shape(...  8.27 us
    ppermute x6, waiting for transfers between devices, sent(): return lax.ppermute(value, ('slab', 'dom'), pairs)  6.96 us
    pallas_call x1, Pallas kernels, per_device(): call(functools.partial(pack_kernel, n_dom), 2, 0, [shape(groups, tall, LA...  4.26 us
    unnamed x8, local copies, waits for them, and re-layouts  3.25 us
  transfers between devices with their start and end apart: 6, of which 2 were waited for; matrix products, arithmetic and copies ran while one was open for 0% of the time, Pallas kernels for 48%

profile of v3, /device:TPU:0, one launch (start us, length us, event | category | flops | bytes accessed | tf_op | source)
XLA Modules:
  0.0 54.6 jit_solution(789503620413897010)
XLA Ops:
  1.3 0.0 copy-start
  1.3 0.9 %copy-done = f32[3,6144]{1,0:T(4,128)S(1)} copy-done((f32[3,6144]{1,0:T(4,128)S(1)}, f32[3,6144]{1,0:T(4,128)}, u32[]{:S(2)}) %copy-start) | copy-done | bytes 73752
  2.2 0.9 %copy-done.1 = f32[3,6144]{1,0:T(4,128)S(1)} copy-done((f32[3,6144]{1,0:T(4,128)S(1)}, f32[3,6144]{1,0:T(4,128)}, u32[]{:S(2)}) %copy-start.1) | copy-done | bytes 73752
  3.1 0.7 %copy-done.2 = f32[6144]{0:T(1024)S(1)} copy-done((f32[6144]{0:T(1024)S(1)}, f32[6144]{0:T(1024)}, u32[]{:S(2)}) %copy-start.2) | copy-done | bytes 24600
  3.8 0.7 %copy-done.3 = s32[6144,1]{0,1:T(1,128)S(1)} copy-done((s32[6144,1]{0,1:T(1,128)S(1)}, s32[6144,1]{0,1:T(1,128)}, u32[]{:S(2)}) %copy-start.3) | copy-done | bytes 24600
  4.5 4.3 %pack.1 = (f32[4,72,128]{2,1,0:T(8,128)S(1)}, f32[4,72,128]{2,1,0:T(8,128)S(1)}) custom-call(s32[1]{0:T(128)} %bitcast.me_ref, s32[1]{0:T(128)S(6)} %copy.7.count_ref, f32[3,6144]{1,0:T(4,128)S(1)} %copy-done, f32[3,6144]{1,0:T(4,128)S(1)} %copy-done.1, f32[1,6144]{1,0:T(1,128)S(1)} %bitcast.3, s32[1,6144]{1,0:T(1,128)S(1)} %bitcast.4), custom_call_target="tpu_custom_call" | custom-call | tf_op jit(solution)/shard_map/pack/pallas_call | solution.py:343
  8.8 3.0 %collective-permute-start = (f32[4,72,128]{2,1,0:T(8,128)S(1)}, f32[4,72,128]{2,1,0:T(8,128)S(1)}, u32[]{:S(2)}, u32[]{:S(2)}) collective-permute-start(f32[4,72,128]{2,1,0:T(8,128)S(1)} %get-tuple-element.9), channel_id=1, source_target_pairs={{0,1},{1,0},{2,3},{3,2},{4,5},{5,4},{6,7},{7,6},{8,9},{9,8},{10,11... | collective-permute-start | bytes 442376 | tf_op jit(solution)/shard_map/ppermute | solution.py:330
  11.8 3.8 %collective-permute-done.refs_1_ = f32[4,72,128]{2,1,0:T(8,128)S(1)} collective-permute-done((f32[4,72,128]{2,1,0:T(8,128)S(1)}, f32[4,72,128]{2,1,0:T(8,128)S(1)}, u32[]{:S(2)}, u32[]{:S(2)}) %collective-permute-start) | collective-permute-done | bytes 147488 | tf_op jit(solution)/shard_map/ppermute | solution.py:330
  15.7 0.2 join.1
  15.9 0.1 collective-permute-start.1
  16.0 4.4 %collective-permute-start.2 = (f32[4,72,128]{2,1,0:T(8,128)S(1)}, f32[4,72,128]{2,1,0:T(8,128)S(1)}, u32[]{:S(2)}, u32[]{:S(2)}) collective-permute-start(f32[4,72,128]{2,1,0:T(8,128)S(1)} %get-tuple-element.11.shells_ref), channel_id=1, source_target_pairs={{0,30},{1,31},{2,0},{3,1},{4,2},{5,3},{6,4},{7,5},{8,6},{9,7},{10,... | collective-permute-start | bytes 442376 | tf_op jit(solution)/shard_map/ppermute | solution.py:330
  20.4 8.3 %own_slab.1 = (bf16[64,32,128]{2,1,0:T(8,128)(2,1)S(1)}, f32[64,16,128]{2,1,0:T(8,128)S(1)}) custom-call(f32[4,72,128]{2,1,0:T(8,128)S(1)} %get-tuple-element.11.shells_ref), custom_call_target="tpu_custom_call" | custom-call | flops 8000000000 | bytes 1000000 | tf_op jit(solution)/shard_map/own_slab/pallas_call | solution.py:383
  28.7 1.1 %collective-permute-start.3 = (f32[7,64,128]{2,1,0:T(8,128)S(1)}, f32[7,64,128]{2,1,0:T(8,128)S(1)}, u32[]{:S(2)}, u32[]{:S(2)}) collective-permute-start(f32[7,64,128]{2,1,0:T(8,128)S(1)} %get-tuple-element.10.planes_ref), channel_id=1, source_target_pairs={{0,16},{1,17},{2,18},{3,19},{4,20},{5,21},{6,22},{7,23},{8,24},{9,... | collective-permute-start | bytes 688136 | tf_op jit(solution)/shard_map/ppermute | solution.py:330
  29.8 0.0 collective-permute-done.1.up_ref
  29.8 0.0 collective-permute-done.2.down_ref
  29.8 10.4 %side_slabs.2.refs_0_ = f32[3,40,128]{2,1,0:T(8,128)S(1)} custom-call(f32[4,72,128]{2,1,0:T(8,128)S(1)} %collective-permute-done.1.up_ref, f32[4,72,128]{2,1,0:T(8,128)S(1)} %collective-permute-done.2.down_ref, bf16[64,32,128]{2,1,0:T(8,128)(2,1)S(1)} %get-tuple-element.12.near_ref, f32[64,16,128]{2,1,0:T(8,128)S(1)} %get-tuple-element.13.own_out, ...), custom_call_target="tpu_custom_call" | custom-call | flops 8000000000 | bytes 1000000 | tf_op jit(solution)/shard_map/side_slabs/pallas_call | solution.py:396
  40.2 2.0 %collective-permute-start.4 = (f32[3,40,128]{2,1,0:T(8,128)S(1)}, f32[3,40,128]{2,1,0:T(8,128)S(1)}, u32[]{:S(2)}, u32[]{:S(2)}) collective-permute-start(f32[3,40,128]{2,1,0:T(8,128)S(1)} %side_slabs.2.refs_0_), channel_id=1, source_target_pairs={{0,16},{1,17},{2,18},{3,19},{4,20},{5,21},{6,22},{7,23},{8,24},{9,... | collective-permute-start | bytes 184328 | tf_op jit(solution)/shard_map/ppermute | solution.py:330
  42.1 6.7 %side_slabs.3.refs_1_ = f32[3,24,128]{2,1,0:T(8,128)S(1)} custom-call(f32[4,72,128]{2,1,0:T(8,128)S(1)} %collective-permute-done.1.up_ref, f32[4,72,128]{2,1,0:T(8,128)S(1)} %collective-permute-done.2.down_ref, bf16[64,32,128]{2,1,0:T(8,128)(2,1)S(1)} %get-tuple-element.12.near_ref, f32[64,16,128]{2,1,0:T(8,128)S(1)} %get-tuple-element.13.own_out, ...), custom_call_target="tpu_custom_call" | custom-call | flops 8000000000 | bytes 1000000 | tf_op jit(solution)/shard_map/side_slabs/pallas_call | solution.py:396
  48.9 1.1 %collective-permute-start.5 = (f32[3,24,128]{2,1,0:T(8,128)S(1)}, f32[3,24,128]{2,1,0:T(8,128)S(1)}, u32[]{:S(2)}, u32[]{:S(2)}) collective-permute-start(f32[3,24,128]{2,1,0:T(8,128)S(1)} %side_slabs.3.refs_1_), channel_id=1, source_target_pairs={{0,16},{1,17},{2,18},{3,19},{4,20},{5,21},{6,22},{7,23},{8,24},{9,... | collective-permute-start | bytes 110600 | tf_op jit(solution)/shard_map/ppermute | solution.py:330
  50.0 0.7 %state.1 = f32[10,1,64,128]{3,2,1,0:T(8,128)} custom-call(f32[7,64,128]{2,1,0:T(8,128)S(1)} %get-tuple-element.10.planes_ref, f32[3,40,128]{2,1,0:T(8,128)S(1)} %side_slabs.2.refs_0_, f32[3,24,128]{2,1,0:T(8,128)S(1)} %side_slabs.3.refs_1_), custom_call_target="tpu_custom_call" | custom-call | tf_op jit(solution)/shard_map/state/pallas_call | solution.py:408
  50.7 3.1 %collective-permute-done.5.refs_1_ = f32[3,24,128]{2,1,0:T(8,128)S(1)} collective-permute-done((f32[3,24,128]{2,1,0:T(8,128)S(1)}, f32[3,24,128]{2,1,0:T(8,128)S(1)}, u32[]{:S(2)}, u32[]{:S(2)}) %collective-permute-start.5) | collective-permute-done | bytes 36896 | tf_op jit(solution)/shard_map/ppermute | solution.py:330
  53.8 0.0 collective-permute-done.4.refs_0_
  53.8 0.0 collective-permute-done.3.planes_ref
  53.8 0.8 %buddy.1 = f32[10,1,64,128]{3,2,1,0:T(8,128)} custom-call(f32[7,64,128]{2,1,0:T(8,128)S(1)} %collective-permute-done.3.planes_ref, f32[3,40,128]{2,1,0:T(8,128)S(1)} %collective-permute-done.4.refs_0_, f32[3,24,128]{2,1,0:T(8,128)S(1)} %collective-permute-done.5.refs_1_), custom_call_target="tpu_custom_call" | custom-call | tf_op jit(solution)/shard_map/buddy/pallas_call | solution.py:409
  (3 shorter events, 0.0 us)
Async XLA Ops:
  1.3 0.9 %copy-start = (f32[3,6144]{1,0:T(4,128)S(1)}, f32[3,6144]{1,0:T(4,128)}, u32[]{:S(2)}) copy-start(f32[3,6144]{1,0:T(4,128)} %pos_any.1) | copy-start | bytes 221188
  2.2 0.9 %copy-start.1 = (f32[3,6144]{1,0:T(4,128)S(1)}, f32[3,6144]{1,0:T(4,128)}, u32[]{:S(2)}) copy-start(f32[3,6144]{1,0:T(4,128)} %vel_any.1) | copy-start | bytes 221188
  3.1 0.7 %copy-start.2 = (f32[6144]{0:T(1024)S(1)}, f32[6144]{0:T(1024)}, u32[]{:S(2)}) copy-start(f32[6144]{0:T(1024)} %param.7) | copy-start | bytes 73732
  3.8 0.7 %copy-start.3 = (s32[6144,1]{0,1:T(1,128)S(1)}, s32[6144,1]{0,1:T(1,128)}, u32[]{:S(2)}) copy-start(s32[6144,1]{0,1:T(1,128)} %param.8) | copy-start | bytes 73732
  8.8 6.9 %collective-permute-start = (f32[4,72,128]{2,1,0:T(8,128)S(1)}, f32[4,72,128]{2,1,0:T(8,128)S(1)}, u32[]{:S(2)}, u32[]{:S(2)}) collective-permute-start(f32[4,72,128]{2,1,0:T(8,128)S(1)} %get-tuple-element.9), channel_id=1, source_target_pairs={{0,1},{1,0},{2,3},{3,2},{4,5},{5,4},{6,7},{7,6},{8,9},{9,8},{10,11... | collective-permute-start | bytes 442376 | tf_op jit(solution)/shard_map/ppermute | solution.py:330
  15.9 13.8 %collective-permute-start.1 = (f32[4,72,128]{2,1,0:T(8,128)S(1)}, f32[4,72,128]{2,1,0:T(8,128)S(1)}, u32[]{:S(2)}, u32[]{:S(2)}) collective-permute-start(f32[4,72,128]{2,1,0:T(8,128)S(1)} %get-tuple-element.11.shells_ref), channel_id=1, source_target_pairs={{0,2},{1,3},{2,4},{3,5},{4,6},{5,7},{6,8},{7,9},{8,10},{9,11},{10,... | collective-permute-start | bytes 442376 | tf_op jit(solution)/shard_map/ppermute | solution.py:330
  16.0 13.8 %collective-permute-start.2 = (f32[4,72,128]{2,1,0:T(8,128)S(1)}, f32[4,72,128]{2,1,0:T(8,128)S(1)}, u32[]{:S(2)}, u32[]{:S(2)}) collective-permute-start(f32[4,72,128]{2,1,0:T(8,128)S(1)} %get-tuple-element.11.shells_ref), channel_id=1, source_target_pairs={{0,30},{1,31},{2,0},{3,1},{4,2},{5,3},{6,4},{7,5},{8,6},{9,7},{10,... | collective-permute-start | bytes 442376 | tf_op jit(solution)/shard_map/ppermute | solution.py:330
  28.7 25.1 %collective-permute-start.3 = (f32[7,64,128]{2,1,0:T(8,128)S(1)}, f32[7,64,128]{2,1,0:T(8,128)S(1)}, u32[]{:S(2)}, u32[]{:S(2)}) collective-permute-start(f32[7,64,128]{2,1,0:T(8,128)S(1)} %get-tuple-element.10.planes_ref), channel_id=1, source_target_pairs={{0,16},{1,17},{2,18},{3,19},{4,20},{5,21},{6,22},{7,23},{8,24},{9,... | collective-permute-start | bytes 688136 | tf_op jit(solution)/shard_map/ppermute | solution.py:330
  40.2 13.6 %collective-permute-start.4 = (f32[3,40,128]{2,1,0:T(8,128)S(1)}, f32[3,40,128]{2,1,0:T(8,128)S(1)}, u32[]{:S(2)}, u32[]{:S(2)}) collective-permute-start(f32[3,40,128]{2,1,0:T(8,128)S(1)} %side_slabs.2.refs_0_), channel_id=1, source_target_pairs={{0,16},{1,17},{2,18},{3,19},{4,20},{5,21},{6,22},{7,23},{8,24},{9,... | collective-permute-start | bytes 184328 | tf_op jit(solution)/shard_map/ppermute | solution.py:330
  48.9 4.9 %collective-permute-start.5 = (f32[3,24,128]{2,1,0:T(8,128)S(1)}, f32[3,24,128]{2,1,0:T(8,128)S(1)}, u32[]{:S(2)}, u32[]{:S(2)}) collective-permute-start(f32[3,24,128]{2,1,0:T(8,128)S(1)} %side_slabs.3.refs_1_), channel_id=1, source_target_pairs={{0,16},{1,17},{2,18},{3,19},{4,20},{5,21},{6,22},{7,23},{8,24},{9,... | collective-permute-start | bytes 110600 | tf_op jit(solution)/shard_map/ppermute | solution.py:330

commit v4 on v3

--- a/solution.py
+++ b/solution.py
@@ -39,7 +39,7 @@
 
 
 def pack_kernel(n_dom, me_ref, count_ref, pos_any, vel_any, mass_any, owner_any, *refs):
-    outs, refs = refs[:n_dom], refs[n_dom:]
+    outs, refs = refs[: 2 * n_dom], refs[2 * n_dom :]
     pos_ref, vel_ref, mass_ref, owner_ref, rank_ref, target_ref, total_ref, sems = refs
     copies = [
         pltpu.make_async_copy(source, target, sems.at[i])
@@ -122,7 +122,7 @@
     for by in range(n_dom):
         low, high = by * CELLS, (by + 1) * CELLS
         edge_high, edge_low = high % targets, (low - 1) % targets
-        for g in range(groups):
+        for g in range(groups // 2):
             edges = jnp.concatenate(
                 [
                     packed[g][edge_high : edge_high + 1],
@@ -132,6 +132,7 @@
                 axis=0,
             )
             outs[by][g] = jnp.concatenate([packed[g][low:high], edges], axis=0)
+            outs[n_dom + by][g] = packed[groups // 2 + g][low:high]
 
 
 def merged(pieces, comp, n_dom):
@@ -258,13 +259,18 @@
 
 
 def join_kernel(n_dom, me_ref, *refs):
-    pieces, (shells_ref, planes_ref) = refs[:n_dom], refs[n_dom:]
+    pieces, shells_ref = refs[:n_dom], refs[n_dom]
     turn = me_ref[0] * (LANES // n_dom)
-    for comp in range(7):
-        plane = pltpu.roll(merged(pieces, comp, n_dom), turn, 1)
-        if comp < 4:
-            shells_ref[comp] = plane
-        planes_ref[comp] = plane[:CELLS]
+    for comp in range(4):
+        shells_ref[comp] = pltpu.roll(merged(pieces, comp, n_dom), turn, 1)
+
+
+def speeds_kernel(n_dom, me_ref, shells_ref, *refs):
+    pieces, planes_ref = refs[:n_dom], refs[n_dom]
+    turn = me_ref[0] * (LANES // n_dom)
+    planes_ref[:4] = shells_ref[:, :CELLS]
+    for comp in range(3):
+        planes_ref[4 + comp] = pltpu.roll(merged(pieces, comp, n_dom), turn, 1)
 
 
 def own_kernel(shells_ref, near_out, out_ref, rows, far_rows, sum_rows, *work):
@@ -274,20 +280,20 @@
     )
 
 
-def side_kernel(cells, up_ref, down_ref, near_ref, own_out, planes_ref, accel_ref, *refs):
+def side_kernel(cells, up_ref, down_ref, near_ref, own_out, shells_ref, accel_ref, *refs):
     low, high = cells
     count = high - low
     rows, far_rows, sum_rows, out, work = refs[0], refs[1:3], refs[3:5], refs[5], refs[6:]
-    for side, shells_ref in enumerate((up_ref, down_ref)):
-        build(shells_ref, rows, far_rows[side], sum_rows[side])
+    for side, there_ref in enumerate((up_ref, down_ref)):
+        build(there_ref, rows, far_rows[side], sum_rows[side])
     pair_loop(cells, 1, far_rows, sum_rows, near_ref, out, work[0:2], work[2:4], work[4:6])
     both = out[...] + own_out[low:high]
     both = (both[:, :8] + both[:, 8:]).reshape(count * 8, LANES)
     rows[: count * 8] = both + pltpu.roll(both, count * 8 - 4, 0)
     total = [rows[pl.ds(comp, count, stride=8), :] for comp in range(4)]
-    live = planes_ref[3, low:high] > 0
+    live = shells_ref[3, low:high] > 0
     for comp in range(3):
-        centre_at = planes_ref[comp, low:high] * math.sqrt(scale)
+        centre_at = shells_ref[comp, low:high] * math.sqrt(scale)
         accel_ref[comp] = jnp.where(live, total[comp] - centre_at * total[3], 0.0)
 
 
@@ -305,19 +311,33 @@
         low = high
 
 
-def call(kernel, n_smem, n_vmem, out_shape, scratch=(), name=None, cost=None, n_any=0):
+def last_kick_kernel(low, _, planes_ref, accel_ref, out_ref, kicked, sem):
+    high = low + accel_ref.shape[1]
+    for comp in range(3):
+        accel = accel_ref[comp]
+        kicked[comp, 0] = planes_ref[4 + comp, low:high] + kick_step * accel
+        kicked[3 + comp, 0] = accel
+    copy = pltpu.make_async_copy(kicked, out_ref.at[4:10, :, low:high], sem)
+    copy.start()
+    copy.wait()
+
+
+def call(
+    kernel, n_smem, n_vmem, out_shape, scratch=(), name=None, cost=None, n_any=0, n_same=0, vmem_mib=48
+):
     smem = pl.BlockSpec(memory_space=pltpu.SMEM)
     vmem = pl.BlockSpec(memory_space=pltpu.VMEM)
-    here = pl.BlockSpec(memory_space=pl.ANY)
+    here = pl.BlockSpec(memory_space=pltpu.HBM)
     return pl.pallas_call(
         kernel,
         in_specs=[smem] * n_smem + [here] * n_any + [vmem] * n_vmem,
-        out_specs=jax.tree.map(lambda _: vmem, out_shape),
+        out_specs=jax.tree.map(lambda _: here if n_same else vmem, out_shape),
         out_shape=out_shape,
         scratch_shapes=scratch,
         name=name,
-        compiler_params=pltpu.CompilerParams(vmem_limit_bytes=48 << 20),
+        compiler_params=pltpu.CompilerParams(vmem_limit_bytes=vmem_mib << 20),
         cost_estimate=cost,
+        input_output_aliases={i: i for i in range(n_same)},
     )
 
 
@@ -335,7 +355,7 @@
     rows = positions.shape[1]
     lanes = LANES // n_dom
     targets = n_dom * CELLS
-    groups = 8 * lanes // LANES
+    half = 4 * lanes // LANES
     tall = CELLS + EDGES
     me = lax.axis_index("dom").astype(jnp.int32).reshape(1)
     shape = lambda *dims, dtype=f32: jax.ShapeDtypeStruct(dims, dtype)
@@ -344,7 +364,7 @@
         functools.partial(pack_kernel, n_dom),
         2,
         0,
-        [shape(groups, tall, LANES)] * n_dom,
+        [shape(half, tall, LANES)] * n_dom + [shape(half, CELLS, LANES)] * n_dom,
         [
             pltpu.VMEM((3, rows), f32),
             pltpu.VMEM((3, rows), f32),
@@ -357,16 +377,25 @@
         ],
         name="pack",
         n_any=4,
+        vmem_mib=63,
     )(me, counts, positions, velocities, masses.reshape(1, rows), owner_cell.reshape(1, rows))
 
-    own = [whole[0]] + [sent(whole[-k % n_dom], n_slab, n_dom, 0, -k) for k in range(1, n_dom)]
-    shells, planes = call(
-        functools.partial(join_kernel, n_dom),
+    def swapped(parts):
+        return [parts[0]] + [
+            sent(parts[-k % n_dom], n_slab, n_dom, 0, -k) for k in range(1, n_dom)
+        ]
+
+    places, speeds = swapped(whole[:n_dom]), swapped(whole[n_dom:])
+    shells = call(
+        functools.partial(join_kernel, n_dom), 1, n_dom, shape(4, tall, LANES), name="join"
+    )(me, *places)
+    planes = call(
+        functools.partial(speeds_kernel, n_dom),
         1,
-        n_dom,
-        [shape(4, tall, LANES), shape(7, CELLS, LANES)],
-        name="join",
-    )(me, *own)
+        1 + n_dom,
+        shape(7, CELLS, LANES),
+        name="speeds",
+    )(me, shells, *speeds)
     below, above = (sent(shells, n_slab, n_dom, side, 0) for side in (1, -1))
     early = sent(planes, n_slab, n_dom, n_slab // 2, 0)
 
@@ -390,7 +419,8 @@
         cost=pl.CostEstimate(flops=8_000_000_000, bytes_accessed=1_000_000, transcendentals=0),
     )(shells)
     accels = []
-    for cells in ((0, 40), (40, CELLS)):
+    cut = CELLS * 3 // 4
+    for cells in ((0, cut), (cut, CELLS)):
         count = cells[1] - cells[0]
         accels.append(
             call(
@@ -401,12 +431,22 @@
                 row_work(2) + [pltpu.VMEM((count, 16, LANES), f32)] + pair_work(768),
                 name="side_slabs",
                 cost=pl.CostEstimate(flops=8_000_000_000, bytes_accessed=1_000_000, transcendentals=0),
-            )(below, above, near, sums, planes)
+            )(below, above, near, sums, shells)
         )
     later = [sent(accel, n_slab, n_dom, n_slab // 2, 0) for accel in accels]
     out = shape(10, 1, CELLS, LANES)
     state = call(kick_kernel, 0, 3, out, name="state")(planes, *accels)
-    buddy = call(kick_kernel, 0, 3, out, name="buddy")(early, *later)
+    part = call(kick_kernel, 0, 2, out, name="buddy")(early, later[0])
+    buddy = call(
+        functools.partial(last_kick_kernel, cut),
+        0,
+        2,
+        out,
+        [pltpu.VMEM((6, 1, CELLS - cut, LANES), f32), pltpu.SemaphoreType.DMA],
+        name="buddy_end",
+        n_any=1,
+        n_same=1,
+    )(part, early, later[1])
     return state, buddy
 
 

time: 54.9 us -> 52.2 us (0.951)
  waiting for transfers between devices: 6.96 us -> 4.21 us
  local copies, waits for them, and re-layouts: 3.25 us -> 0.89 us
  Pallas kernels: 31.4 us -> 33.1 us
  starting transfers between devices: 11.6 us -> 12.5 us
    ppermute x6 -> x7, waiting for transfers between devices: 6.96 us -> 4.21 us  [sent(): return lax.ppermute(value, ('slab', 'dom'), pairs)]
    unnamed x8 -> x4, local copies, waits for them, and re-layouts: 3.25 us -> 0.89 us
    pallas_call x3 -> x5, Pallas kernels: 5.26 us -> 7.04 us  [the longest x1 5.34 us: per_device(): call(functools.partial(pack_kernel, n_dom), 2, 0, [shape(half, tall, LANE...]
    ppermute x6 -> x7, starting transfers between devices: 11.6 us -> 12.5 us  [sent(): return lax.ppermute(value, ('slab', 'dom'), pairs)]
  transfers between devices with their start and end apart: 6 -> 7, of which waited for: 2 -> 2; matrix products, arithmetic and copies ran while one was open for 0% -> 0% of each run, Pallas kernels for 48% -> 52%
where the time goes in v4:
time: 52.2 us; the launch traced here: 52 us
  Pallas kernels  33.1 us (63%)
  starting transfers between devices  12.5 us (24%)
  waiting for transfers between devices  4.21 us (8%)
  between operations  1.35 us (3%)
  local copies, waits for them, and re-layouts  0.89 us (2%)
    pallas_call x2, Pallas kernels, per_device(): call(functools.partial(side_kernel, cells), 0, 5, shape(3, count, LANES),...  17.1 us
    ppermute x7, starting transfers between devices, sent(): return lax.ppermute(value, ('slab', 'dom'), pairs)  12.5 us
    pallas_call x1, Pallas kernels, per_device(): call(own_kernel, 0, 1, [shape(CELLS, FEATURES, LANES, dtype=bf16), shape(...  8.27 us
    pallas_call x1, Pallas kernels, per_device(): call(functools.partial(pack_kernel, n_dom), 2, 0, [shape(half, tall, LANE...  5.34 us
    ppermute x7, waiting for transfers between devices, sent(): return lax.ppermute(value, ('slab', 'dom'), pairs)  4.21 us
  transfers between devices with their start and end apart: 7, of which 2 were waited for; matrix products, arithmetic and copies ran while one was open for 0% of the time, Pallas kernels for 52%

profile of v4, /device:TPU:0, one launch (start us, length us, event | category | flops | bytes accessed | tf_op | source)
XLA Modules:
  0.0 52.0 jit_solution(7768616580704736393)
XLA Ops:
  1.3 5.3 %pack.1 = (f32[2,72,128]{2,1,0:T(8,128)}, f32[2,72,128]{2,1,0:T(8,128)}, f32[2,64,128]{2,1,0:T(8,128)}, f32[2,64,128]{2,1,0:T(8,128)}) custom-call(s32[1]{0:T(128)} %bitcast.me_ref, s32[1]{0:T(128)S(6)} %copy.9.count_ref, f32[3,6144]{1,0:T(4,128)} %pos_any.1, f32[3,6144]{1,0:T(4,128)} %vel_any.1, f32[1,6144]{1,0:T(1,128)} %bitcast.3, s32[1,6144]{1,0:T(1,128)} %bitcast.4), custom_call_target="tpu_custom_call" | custom-call | tf_op jit(solution)/shard_map/pack/pallas_call | solution.py:363
  6.6 3.0 %collective-permute-start = (f32[2,72,128]{2,1,0:T(8,128)}, f32[2,72,128]{2,1,0:T(8,128)S(1)}, u32[]{:S(2)}, u32[]{:S(2)}) collective-permute-start(f32[2,72,128]{2,1,0:T(8,128)} %get-tuple-element.9), channel_id=1, source_target_pairs={{0,1},{1,0},{2,3},{3,2},{4,5},{5,4},{6,7},{7,6},{8,9},{9,8},{10,11... | collective-permute-start | bytes 221192 | tf_op jit(solution)/shard_map/ppermute | solution.py:350
  9.7 0.1 collective-permute-start.1
  9.7 2.7 %collective-permute-done.refs_1_ = f32[2,72,128]{2,1,0:T(8,128)S(1)} collective-permute-done((f32[2,72,128]{2,1,0:T(8,128)}, f32[2,72,128]{2,1,0:T(8,128)S(1)}, u32[]{:S(2)}, u32[]{:S(2)}) %collective-permute-start) | collective-permute-done | bytes 73760 | tf_op jit(solution)/shard_map/ppermute | solution.py:350
  12.4 0.9 %copy-done = f32[2,72,128]{2,1,0:T(8,128)S(1)} copy-done((f32[2,72,128]{2,1,0:T(8,128)S(1)}, f32[2,72,128]{2,1,0:T(8,128)}, u32[]{:S(2)}) %copy-start) | copy-done | bytes 73752
  13.3 0.2 join.1.shells_ref
  13.5 0.1 collective-permute-start.2
  13.6 4.4 %collective-permute-start.3 = (f32[4,72,128]{2,1,0:T(8,128)S(1)}, f32[4,72,128]{2,1,0:T(8,128)S(1)}, u32[]{:S(2)}, u32[]{:S(2)}) collective-permute-start(f32[4,72,128]{2,1,0:T(8,128)S(1)} %join.1.shells_ref), channel_id=1, source_target_pairs={{0,30},{1,31},{2,0},{3,1},{4,2},{5,3},{6,4},{7,5},{8,6},{9,7},{10,... | collective-permute-start | bytes 442376 | tf_op jit(solution)/shard_map/ppermute | solution.py:350
  18.0 8.3 %own_slab.1 = (bf16[64,32,128]{2,1,0:T(8,128)(2,1)S(1)}, f32[64,16,128]{2,1,0:T(8,128)S(1)}) custom-call(f32[4,72,128]{2,1,0:T(8,128)S(1)} %join.1.shells_ref), custom_call_target="tpu_custom_call" | custom-call | flops 8000000000 | bytes 1000000 | tf_op jit(solution)/shard_map/own_slab/pallas_call | solution.py:412
  26.3 0.0 collective-permute-done.1.refs_1_
  26.3 0.2 speeds.1.planes_ref
  26.4 1.8 %collective-permute-start.4 = (f32[7,64,128]{2,1,0:T(8,128)S(1)}, f32[7,64,128]{2,1,0:T(8,128)S(1)}, u32[]{:S(2)}, u32[]{:S(2)}) collective-permute-start(f32[7,64,128]{2,1,0:T(8,128)S(1)} %speeds.1.planes_ref), channel_id=1, source_target_pairs={{0,16},{1,17},{2,18},{3,19},{4,20},{5,21},{6,22},{7,23},{8,24},{9,... | collective-permute-start | bytes 688136 | tf_op jit(solution)/shard_map/ppermute | solution.py:350
  28.2 0.0 collective-permute-done.2.up_ref
  28.3 0.0 collective-permute-done.3.down_ref
  28.3 12.1 %side_slabs.2.refs_0_ = f32[3,48,128]{2,1,0:T(8,128)S(1)} custom-call(f32[4,72,128]{2,1,0:T(8,128)S(1)} %collective-permute-done.2.up_ref, f32[4,72,128]{2,1,0:T(8,128)S(1)} %collective-permute-done.3.down_ref, bf16[64,32,128]{2,1,0:T(8,128)(2,1)S(1)} %get-tuple-element.12.near_ref, f32[64,16,128]{2,1,0:T(8,128)S(1)} %get-tuple-element.13.own_out, ...), custom_call_target="tpu_custom_call" | custom-call | flops 8000000000 | bytes 1000000 | tf_op jit(solution)/shard_map/side_slabs/pallas_call | solution.py:426
  40.4 1.3 %collective-permute-start.5 = (f32[3,48,128]{2,1,0:T(8,128)S(1)}, f32[3,48,128]{2,1,0:T(8,128)S(1)}, u32[]{:S(2)}, u32[]{:S(2)}) collective-permute-start(f32[3,48,128]{2,1,0:T(8,128)S(1)} %side_slabs.2.refs_0_), channel_id=1, source_target_pairs={{0,16},{1,17},{2,18},{3,19},{4,20},{5,21},{6,22},{7,23},{8,24},{9,... | collective-permute-start | bytes 221192 | tf_op jit(solution)/shard_map/ppermute | solution.py:350
  41.7 4.9 %side_slabs.3.refs_1_ = f32[3,16,128]{2,1,0:T(8,128)S(1)} custom-call(f32[4,72,128]{2,1,0:T(8,128)S(1)} %collective-permute-done.2.up_ref, f32[4,72,128]{2,1,0:T(8,128)S(1)} %collective-permute-done.3.down_ref, bf16[64,32,128]{2,1,0:T(8,128)(2,1)S(1)} %get-tuple-element.12.near_ref, f32[64,16,128]{2,1,0:T(8,128)S(1)} %get-tuple-element.13.own_out, ...), custom_call_target="tpu_custom_call" | custom-call | flops 8000000000 | bytes 1000000 | tf_op jit(solution)/shard_map/side_slabs/pallas_call | solution.py:426
  46.6 1.8 %collective-permute-start.6 = (f32[3,16,128]{2,1,0:T(8,128)S(1)}, f32[3,16,128]{2,1,0:T(8,128)S(1)}, u32[]{:S(2)}, u32[]{:S(2)}) collective-permute-start(f32[3,16,128]{2,1,0:T(8,128)S(1)} %side_slabs.3.refs_1_), channel_id=1, source_target_pairs={{0,16},{1,17},{2,18},{3,19},{4,20},{5,21},{6,22},{7,23},{8,24},{9,... | collective-permute-start | bytes 73736 | tf_op jit(solution)/shard_map/ppermute | solution.py:350
  48.4 0.7 %state.1 = f32[10,1,64,128]{3,2,1,0:T(8,128)} custom-call(f32[7,64,128]{2,1,0:T(8,128)S(1)} %speeds.1.planes_ref, f32[3,48,128]{2,1,0:T(8,128)S(1)} %side_slabs.2.refs_0_, f32[3,16,128]{2,1,0:T(8,128)S(1)} %side_slabs.3.refs_1_), custom_call_target="tpu_custom_call" | custom-call | tf_op jit(solution)/shard_map/state/pallas_call | solution.py:438
  49.2 0.0 collective-permute-done.5.refs_0_
  49.2 0.0 collective-permute-done.4.planes_ref
  49.2 0.7 %buddy.1._ = f32[10,1,64,128]{3,2,1,0:T(8,128)} custom-call(f32[7,64,128]{2,1,0:T(8,128)S(1)} %collective-permute-done.4.planes_ref, f32[3,48,128]{2,1,0:T(8,128)S(1)} %collective-permute-done.5.refs_0_), custom_call_target="tpu_custom_call" | custom-call | tf_op jit(solution)/shard_map/buddy/pallas_call | solution.py:439
  49.9 1.5 %collective-permute-done.6.accel_ref = f32[3,16,128]{2,1,0:T(8,128)S(1)} collective-permute-done((f32[3,16,128]{2,1,0:T(8,128)S(1)}, f32[3,16,128]{2,1,0:T(8,128)S(1)}, u32[]{:S(2)}, u32[]{:S(2)}) %collective-permute-start.6) | collective-permute-done | bytes 24608 | tf_op jit(solution)/shard_map/ppermute | solution.py:350
  51.4 0.6 %buddy_end.1 = f32[10,1,64,128]{3,2,1,0:T(8,128)} custom-call(f32[10,1,64,128]{3,2,1,0:T(8,128)} %buddy.1._, f32[7,64,128]{2,1,0:T(8,128)S(1)} %collective-permute-done.4.planes_ref, f32[3,16,128]{2,1,0:T(8,128)S(1)} %collective-permute-done.6.accel_ref), custom_call_target="tpu_custom_call", output_to_operand_aliasing={{}: (0, {})} | custom-call | tf_op jit(solution)/shard_map/buddy_end/pallas_call | solution.py:440
  (3 shorter events, 0.0 us)
Async XLA Ops:
  6.6 5.8 %collective-permute-start = (f32[2,72,128]{2,1,0:T(8,128)}, f32[2,72,128]{2,1,0:T(8,128)S(1)}, u32[]{:S(2)}, u32[]{:S(2)}) collective-permute-start(f32[2,72,128]{2,1,0:T(8,128)} %get-tuple-element.9), channel_id=1, source_target_pairs={{0,1},{1,0},{2,3},{3,2},{4,5},{5,4},{6,7},{7,6},{8,9},{9,8},{10,11... | collective-permute-start | bytes 221192 | tf_op jit(solution)/shard_map/ppermute | solution.py:350
  9.7 16.6 %collective-permute-start.1 = (f32[2,64,128]{2,1,0:T(8,128)}, f32[2,64,128]{2,1,0:T(8,128)S(1)}, u32[]{:S(2)}, u32[]{:S(2)}) collective-permute-start(f32[2,64,128]{2,1,0:T(8,128)} %get-tuple-element.11), channel_id=1, source_target_pairs={{0,1},{1,0},{2,3},{3,2},{4,5},{5,4},{6,7},{7,6},{8,9},{9,8},{10,11... | collective-permute-start | bytes 196616 | tf_op jit(solution)/shard_map/ppermute | solution.py:350
  12.4 0.9 %copy-start = (f32[2,72,128]{2,1,0:T(8,128)S(1)}, f32[2,72,128]{2,1,0:T(8,128)}, u32[]{:S(2)}) copy-start(f32[2,72,128]{2,1,0:T(8,128)} %get-tuple-element.8.refs_0_) | copy-start | bytes 221188
  13.5 12.8 %copy-start.1 = (f32[2,64,128]{2,1,0:T(8,128)S(1)}, f32[2,64,128]{2,1,0:T(8,128)}, u32[]{:S(2)}) copy-start(f32[2,64,128]{2,1,0:T(8,128)} %get-tuple-element.10.refs_0_) | copy-start | bytes 196612
  13.5 14.8 %collective-permute-start.2 = (f32[4,72,128]{2,1,0:T(8,128)S(1)}, f32[4,72,128]{2,1,0:T(8,128)S(1)}, u32[]{:S(2)}, u32[]{:S(2)}) collective-permute-start(f32[4,72,128]{2,1,0:T(8,128)S(1)} %join.1.shells_ref), channel_id=1, source_target_pairs={{0,2},{1,3},{2,4},{3,5},{4,6},{5,7},{6,8},{7,9},{8,10},{9,11},{10,... | collective-permute-start | bytes 442376 | tf_op jit(solution)/shard_map/ppermute | solution.py:350
  13.6 14.7 %collective-permute-start.3 = (f32[4,72,128]{2,1,0:T(8,128)S(1)}, f32[4,72,128]{2,1,0:T(8,128)S(1)}, u32[]{:S(2)}, u32[]{:S(2)}) collective-permute-start(f32[4,72,128]{2,1,0:T(8,128)S(1)} %join.1.shells_ref), channel_id=1, source_target_pairs={{0,30},{1,31},{2,0},{3,1},{4,2},{5,3},{6,4},{7,5},{8,6},{9,7},{10,... | collective-permute-start | bytes 442376 | tf_op jit(solution)/shard_map/ppermute | solution.py:350
  26.4 22.7 %collective-permute-start.4 = (f32[7,64,128]{2,1,0:T(8,128)S(1)}, f32[7,64,128]{2,1,0:T(8,128)S(1)}, u32[]{:S(2)}, u32[]{:S(2)}) collective-permute-start(f32[7,64,128]{2,1,0:T(8,128)S(1)} %speeds.1.planes_ref), channel_id=1, source_target_pairs={{0,16},{1,17},{2,18},{3,19},{4,20},{5,21},{6,22},{7,23},{8,24},{9,... | collective-permute-start | bytes 688136 | tf_op jit(solution)/shard_map/ppermute | solution.py:350
  40.4 8.7 %collective-permute-start.5 = (f32[3,48,128]{2,1,0:T(8,128)S(1)}, f32[3,48,128]{2,1,0:T(8,128)S(1)}, u32[]{:S(2)}, u32[]{:S(2)}) collective-permute-start(f32[3,48,128]{2,1,0:T(8,128)S(1)} %side_slabs.2.refs_0_), channel_id=1, source_target_pairs={{0,16},{1,17},{2,18},{3,19},{4,20},{5,21},{6,22},{7,23},{8,24},{9,... | collective-permute-start | bytes 221192 | tf_op jit(solution)/shard_map/ppermute | solution.py:350
  46.6 4.8 %collective-permute-start.6 = (f32[3,16,128]{2,1,0:T(8,128)S(1)}, f32[3,16,128]{2,1,0:T(8,128)S(1)}, u32[]{:S(2)}, u32[]{:S(2)}) collective-permute-start(f32[3,16,128]{2,1,0:T(8,128)S(1)} %side_slabs.3.refs_1_), channel_id=1, source_target_pairs={{0,16},{1,17},{2,18},{3,19},{4,20},{5,21},{6,22},{7,23},{8,24},{9,... | collective-permute-start | bytes 73736 | tf_op jit(solution)/shard_map/ppermute | solution.py:350

commit v5 on v4

--- a/solution.py
+++ b/solution.py
@@ -152,14 +152,16 @@
     return plane
 
 
-def build(shells_ref, rows_ref, far_ref, sum_ref, near_ref=None):
+def build(shells_ref, cells, rows_ref, far_ref, sum_ref, near_ref=None):
     root = math.sqrt(scale)
-    tall = shells_ref.shape[1]
+    low, high = cells
+    needed = [c % (CELLS + 2) for c in range(low - 1, high + 1)]
+    groups_at = sorted({c // 8 * 8 for c in needed})
     rows_ref[...] = jnp.zeros_like(rows_ref)
-    for at in range(0, tall, 8):
+    for at in groups_at:
         for comp in range(4):
             rows_ref[pl.ds(at * 8 + comp, 8, stride=8), :] = shells_ref[comp, at : at + 8, :]
-    for at in range(0, tall, 8):
+    for at in groups_at:
         value = rows_ref[at * 8 : (at + 8) * 8]
         row = lax.broadcasted_iota(jnp.int32, value.shape, 0) % 8
 
@@ -202,7 +204,7 @@
         put(sum_ref, [terms[0] + down(terms[1], 4), terms[2]])
 
 
-def pair_loop(cells, per, far_rows, sum_rows, centre, out, dist, heavy, light):
+def pair_loop(cells, per, far_rows, sum_rows, centre, out, dist, heavy):
     blocks = [(k, n) for k in range(3) for n in range(len(far_rows))]
     tall = LANES * len(blocks)
     wide = 3
@@ -228,18 +230,25 @@
         for at in range(0, per * tall, 64):
             s = dist[b][at : at + 64]
             inverse = lax.rsqrt(s)
-            w = jnp.exp2(-s) * (inverse * inverse * inverse)
-            head = w.astype(bf16)
-            heavy[b][at : at + 64] = head
-            light[b][at : at + 64] = (w - head.astype(f32)).astype(bf16)
+            heavy[b][at : at + 64] = jnp.exp2(-s) * (inverse * inverse * inverse)
 
     def sums(step, b):
         for u in range(per):
             c = step * per + u
-            terms = jnp.concatenate([sum_rows[n][beside(c, k)] for k, n in blocks], axis=1)
-            span = slice(u * tall, (u + 1) * tall)
-            total = lax.dot_general(terms, heavy[b][span], NN, preferred_element_type=f32)
-            total += lax.dot_general(terms, light[b][span], NN, preferred_element_type=f32)
+            total = None
+            for at in range(0, len(blocks), wide):
+                terms = jnp.concatenate(
+                    [sum_rows[n][beside(c, k)] for k, n in blocks[at : at + wide]], axis=1
+                )
+                low = u * tall + at * LANES
+                w = heavy[b][low : low + wide * LANES]
+                head = w.astype(bf16)
+                tail = (w - head.astype(f32)).astype(bf16)
+                part = lax.dot_general(
+                    terms, jnp.concatenate([head, tail], axis=1), NN, preferred_element_type=f32
+                )
+                part = part[:, :LANES] + part[:, LANES:]
+                total = part if total is None else total + part
             out[c] = total
 
     steps = count // per
@@ -251,11 +260,15 @@
         for b in range(2):
             step = 2 * i + b
             sums(step, b)
+            weights(1 - b)
             distances(jnp.minimum(step + 2, steps - 1), b)
-            weights(1 - b)
         return 0
 
     lax.fori_loop(0, steps // 2, body, 0)
+
+
+def copy_kernel(source_ref, target_ref):
+    target_ref[...] = source_ref[...]
 
 
 def join_kernel(n_dom, me_ref, *refs):
@@ -274,9 +287,9 @@
 
 
 def own_kernel(shells_ref, near_out, out_ref, rows, far_rows, sum_rows, *work):
-    build(shells_ref, rows, far_rows, sum_rows, near_out)
+    build(shells_ref, (0, CELLS), rows, far_rows, sum_rows, near_out)
     pair_loop(
-        (0, CELLS), 2, [far_rows], [sum_rows], near_out, out_ref, work[0:2], work[2:4], work[4:6]
+        (0, CELLS), 2, [far_rows], [sum_rows], near_out, out_ref, work[0:2], work[2:4]
     )
 
 
@@ -285,8 +298,8 @@
     count = high - low
     rows, far_rows, sum_rows, out, work = refs[0], refs[1:3], refs[3:5], refs[5], refs[6:]
     for side, there_ref in enumerate((up_ref, down_ref)):
-        build(there_ref, rows, far_rows[side], sum_rows[side])
-    pair_loop(cells, 1, far_rows, sum_rows, near_ref, out, work[0:2], work[2:4], work[4:6])
+        build(there_ref, cells, rows, far_rows[side], sum_rows[side])
+    pair_loop(cells, 1, far_rows, sum_rows, near_ref, out, work[0:2], work[2:4])
     both = out[...] + own_out[low:high]
     both = (both[:, :8] + both[:, 8:]).reshape(count * 8, LANES)
     rows[: count * 8] = both + pltpu.roll(both, count * 8 - 4, 0)
@@ -386,6 +399,7 @@
         ]
 
     places, speeds = swapped(whole[:n_dom]), swapped(whole[n_dom:])
+    places[0] = call(copy_kernel, 0, 1, shape(half, tall, LANES), name="own_piece")(places[0])
     shells = call(
         functools.partial(join_kernel, n_dom), 1, n_dom, shape(4, tall, LANES), name="join"
     )(me, *places)
@@ -400,7 +414,7 @@
     early = sent(planes, n_slab, n_dom, n_slab // 2, 0)
 
     def pair_work(size):
-        return [pltpu.VMEM((size, LANES), f32)] * 2 + [pltpu.VMEM((size, LANES), bf16)] * 4
+        return [pltpu.VMEM((size, LANES), f32)] * 4
 
     def row_work(copies):
         return (

time: 52.2 us -> 47.1 us (0.902)
  Pallas kernels: 33.1 us -> 28.9 us
  waiting for transfers between devices: 4.21 us -> 3.31 us
    pallas_call x2, Pallas kernels: 17.1 us -> 14.1 us  [per_device(): call(functools.partial(side_kernel, cells), 0, 5, shape(3, count, LANES),...]
    pallas_call x1, Pallas kernels: 8.27 us -> 7.01 us  [per_device(): call(own_kernel, 0, 1, [shape(CELLS, FEATURES, LANES, dtype=bf16), shape(...]
    ppermute x7, waiting for transfers between devices: 4.21 us -> 3.31 us  [sent(): return lax.ppermute(value, ('slab', 'dom'), pairs)]
  transfers between devices with their start and end apart: 7 -> 7, of which waited for: 2 -> 2; matrix products, arithmetic and copies ran while one was open for 0% -> 0% of each run, Pallas kernels for 52% -> 49%
where the time goes in v5:
time: 47.1 us; the launch traced here: 46.9 us
  Pallas kernels  28.9 us (61%)
  starting transfers between devices  12.5 us (27%)
  waiting for transfers between devices  3.31 us (7%)
  between operations  1.35 us (3%)
  local copies, waits for them, and re-layouts  0.89 us (2%)
    pallas_call x2, Pallas kernels, per_device(): call(functools.partial(side_kernel, cells), 0, 5, shape(3, count, LANES),...  14.1 us
    ppermute x7, starting transfers between devices, sent(): return lax.ppermute(value, ('slab', 'dom'), pairs)  12.5 us
    pallas_call x1, Pallas kernels, per_device(): call(own_kernel, 0, 1, [shape(CELLS, FEATURES, LANES, dtype=bf16), shape(...  7.01 us
    pallas_call x1, Pallas kernels, per_device(): call(functools.partial(pack_kernel, n_dom), 2, 0, [shape(half, tall, LANE...  5.34 us
    ppermute x7, waiting for transfers between devices, sent(): return lax.ppermute(value, ('slab', 'dom'), pairs)  3.31 us
  transfers between devices with their start and end apart: 7, of which 2 were waited for; matrix products, arithmetic and copies ran while one was open for 0% of the time, Pallas kernels for 49%

profile of v5, /device:TPU:0, one launch (start us, length us, event | category | flops | bytes accessed | tf_op | source)
XLA Modules:
  0.0 46.9 jit_solution(6085455206706260392)
XLA Ops:
  1.3 5.3 %pack.1 = (f32[2,72,128]{2,1,0:T(8,128)}, f32[2,72,128]{2,1,0:T(8,128)}, f32[2,64,128]{2,1,0:T(8,128)}, f32[2,64,128]{2,1,0:T(8,128)}) custom-call(s32[1]{0:T(128)} %bitcast.me_ref, s32[1]{0:T(128)S(6)} %copy.9.count_ref, f32[3,6144]{1,0:T(4,128)} %pos_any.1, f32[3,6144]{1,0:T(4,128)} %vel_any.1, f32[1,6144]{1,0:T(1,128)} %bitcast.3, s32[1,6144]{1,0:T(1,128)} %bitcast.4), custom_call_target="tpu_custom_call" | custom-call | tf_op jit(solution)/shard_map/pack/pallas_call | solution.py:376
  6.6 3.0 %collective-permute-start = (f32[2,72,128]{2,1,0:T(8,128)}, f32[2,72,128]{2,1,0:T(8,128)S(1)}, u32[]{:S(2)}, u32[]{:S(2)}) collective-permute-start(f32[2,72,128]{2,1,0:T(8,128)} %get-tuple-element.9), channel_id=1, source_target_pairs={{0,1},{1,0},{2,3},{3,2},{4,5},{5,4},{6,7},{7,6},{8,9},{9,8},{10,11... | collective-permute-start | bytes 221192 | tf_op jit(solution)/shard_map/ppermute | solution.py:363
  9.7 0.1 collective-permute-start.1
  9.7 0.9 %copy-done = f32[2,72,128]{2,1,0:T(8,128)S(1)} copy-done((f32[2,72,128]{2,1,0:T(8,128)S(1)}, f32[2,72,128]{2,1,0:T(8,128)}, u32[]{:S(2)}) %copy-start) | copy-done | bytes 73752
  10.6 1.8 %collective-permute-done.refs_1_ = f32[2,72,128]{2,1,0:T(8,128)S(1)} collective-permute-done((f32[2,72,128]{2,1,0:T(8,128)}, f32[2,72,128]{2,1,0:T(8,128)S(1)}, u32[]{:S(2)}, u32[]{:S(2)}) %collective-permute-start) | collective-permute-done | bytes 73760 | tf_op jit(solution)/shard_map/ppermute | solution.py:363
  12.4 0.2 join.1.shells_ref
  12.6 0.1 collective-permute-start.2
  12.7 4.4 %collective-permute-start.3 = (f32[4,72,128]{2,1,0:T(8,128)S(1)}, f32[4,72,128]{2,1,0:T(8,128)S(1)}, u32[]{:S(2)}, u32[]{:S(2)}) collective-permute-start(f32[4,72,128]{2,1,0:T(8,128)S(1)} %join.1.shells_ref), channel_id=1, source_target_pairs={{0,30},{1,31},{2,0},{3,1},{4,2},{5,3},{6,4},{7,5},{8,6},{9,7},{10,... | collective-permute-start | bytes 442376 | tf_op jit(solution)/shard_map/ppermute | solution.py:363
  17.1 7.0 %own_slab.1 = (bf16[64,32,128]{2,1,0:T(8,128)(2,1)S(1)}, f32[64,16,128]{2,1,0:T(8,128)S(1)}) custom-call(f32[4,72,128]{2,1,0:T(8,128)S(1)} %join.1.shells_ref), custom_call_target="tpu_custom_call" | custom-call | flops 8000000000 | bytes 1000000 | tf_op jit(solution)/shard_map/own_slab/pallas_call | solution.py:426
  24.1 0.0 collective-permute-done.1.refs_1_
  24.1 0.2 speeds.1.planes_ref
  24.3 1.8 %collective-permute-start.4 = (f32[7,64,128]{2,1,0:T(8,128)S(1)}, f32[7,64,128]{2,1,0:T(8,128)S(1)}, u32[]{:S(2)}, u32[]{:S(2)}) collective-permute-start(f32[7,64,128]{2,1,0:T(8,128)S(1)} %speeds.1.planes_ref), channel_id=1, source_target_pairs={{0,16},{1,17},{2,18},{3,19},{4,20},{5,21},{6,22},{7,23},{8,24},{9,... | collective-permute-start | bytes 688136 | tf_op jit(solution)/shard_map/ppermute | solution.py:363
  26.1 0.0 collective-permute-done.2.up_ref
  26.1 0.0 collective-permute-done.3.down_ref
  26.1 10.3 %side_slabs.2.refs_0_ = f32[3,48,128]{2,1,0:T(8,128)S(1)} custom-call(f32[4,72,128]{2,1,0:T(8,128)S(1)} %collective-permute-done.2.up_ref, f32[4,72,128]{2,1,0:T(8,128)S(1)} %collective-permute-done.3.down_ref, bf16[64,32,128]{2,1,0:T(8,128)(2,1)S(1)} %get-tuple-element.12.near_ref, f32[64,16,128]{2,1,0:T(8,128)S(1)} %get-tuple-element.13.own_out, ...), custom_call_target="tpu_custom_call" | custom-call | flops 8000000000 | bytes 1000000 | tf_op jit(solution)/shard_map/side_slabs/pallas_call | solution.py:440
  36.5 1.2 %collective-permute-start.5 = (f32[3,48,128]{2,1,0:T(8,128)S(1)}, f32[3,48,128]{2,1,0:T(8,128)S(1)}, u32[]{:S(2)}, u32[]{:S(2)}) collective-permute-start(f32[3,48,128]{2,1,0:T(8,128)S(1)} %side_slabs.2.refs_0_), channel_id=1, source_target_pairs={{0,16},{1,17},{2,18},{3,19},{4,20},{5,21},{6,22},{7,23},{8,24},{9,... | collective-permute-start | bytes 221192 | tf_op jit(solution)/shard_map/ppermute | solution.py:363
  37.7 3.7 %side_slabs.3.refs_1_ = f32[3,16,128]{2,1,0:T(8,128)S(1)} custom-call(f32[4,72,128]{2,1,0:T(8,128)S(1)} %collective-permute-done.2.up_ref, f32[4,72,128]{2,1,0:T(8,128)S(1)} %collective-permute-done.3.down_ref, bf16[64,32,128]{2,1,0:T(8,128)(2,1)S(1)} %get-tuple-element.12.near_ref, f32[64,16,128]{2,1,0:T(8,128)S(1)} %get-tuple-element.13.own_out, ...), custom_call_target="tpu_custom_call" | custom-call | flops 8000000000 | bytes 1000000 | tf_op jit(solution)/shard_map/side_slabs/pallas_call | solution.py:440
  41.5 1.8 %collective-permute-start.6 = (f32[3,16,128]{2,1,0:T(8,128)S(1)}, f32[3,16,128]{2,1,0:T(8,128)S(1)}, u32[]{:S(2)}, u32[]{:S(2)}) collective-permute-start(f32[3,16,128]{2,1,0:T(8,128)S(1)} %side_slabs.3.refs_1_), channel_id=1, source_target_pairs={{0,16},{1,17},{2,18},{3,19},{4,20},{5,21},{6,22},{7,23},{8,24},{9,... | collective-permute-start | bytes 73736 | tf_op jit(solution)/shard_map/ppermute | solution.py:363
  43.3 0.7 %state.1 = f32[10,1,64,128]{3,2,1,0:T(8,128)} custom-call(f32[7,64,128]{2,1,0:T(8,128)S(1)} %speeds.1.planes_ref, f32[3,48,128]{2,1,0:T(8,128)S(1)} %side_slabs.2.refs_0_, f32[3,16,128]{2,1,0:T(8,128)S(1)} %side_slabs.3.refs_1_), custom_call_target="tpu_custom_call" | custom-call | tf_op jit(solution)/shard_map/state/pallas_call | solution.py:452
  44.0 0.0 collective-permute-done.5.refs_0_
  44.0 0.0 collective-permute-done.4.planes_ref
  44.0 0.7 %buddy.1._ = f32[10,1,64,128]{3,2,1,0:T(8,128)} custom-call(f32[7,64,128]{2,1,0:T(8,128)S(1)} %collective-permute-done.4.planes_ref, f32[3,48,128]{2,1,0:T(8,128)S(1)} %collective-permute-done.5.refs_0_), custom_call_target="tpu_custom_call" | custom-call | tf_op jit(solution)/shard_map/buddy/pallas_call | solution.py:453
  44.8 1.5 %collective-permute-done.6.accel_ref = f32[3,16,128]{2,1,0:T(8,128)S(1)} collective-permute-done((f32[3,16,128]{2,1,0:T(8,128)S(1)}, f32[3,16,128]{2,1,0:T(8,128)S(1)}, u32[]{:S(2)}, u32[]{:S(2)}) %collective-permute-start.6) | collective-permute-done | bytes 24608 | tf_op jit(solution)/shard_map/ppermute | solution.py:363
  46.3 0.6 %buddy_end.1 = f32[10,1,64,128]{3,2,1,0:T(8,128)} custom-call(f32[10,1,64,128]{3,2,1,0:T(8,128)} %buddy.1._, f32[7,64,128]{2,1,0:T(8,128)S(1)} %collective-permute-done.4.planes_ref, f32[3,16,128]{2,1,0:T(8,128)S(1)} %collective-permute-done.6.accel_ref), custom_call_target="tpu_custom_call", output_to_operand_aliasing={{}: (0, {})} | custom-call | tf_op jit(solution)/shard_map/buddy_end/pallas_call | solution.py:454
  (4 shorter events, 0.0 us)
Async XLA Ops:
  6.6 5.8 %collective-permute-start = (f32[2,72,128]{2,1,0:T(8,128)}, f32[2,72,128]{2,1,0:T(8,128)S(1)}, u32[]{:S(2)}, u32[]{:S(2)}) collective-permute-start(f32[2,72,128]{2,1,0:T(8,128)} %get-tuple-element.9), channel_id=1, source_target_pairs={{0,1},{1,0},{2,3},{3,2},{4,5},{5,4},{6,7},{7,6},{8,9},{9,8},{10,11... | collective-permute-start | bytes 221192 | tf_op jit(solution)/shard_map/ppermute | solution.py:363
  9.7 14.5 %collective-permute-start.1 = (f32[2,64,128]{2,1,0:T(8,128)}, f32[2,64,128]{2,1,0:T(8,128)S(1)}, u32[]{:S(2)}, u32[]{:S(2)}) collective-permute-start(f32[2,64,128]{2,1,0:T(8,128)} %get-tuple-element.11), channel_id=1, source_target_pairs={{0,1},{1,0},{2,3},{3,2},{4,5},{5,4},{6,7},{7,6},{8,9},{9,8},{10,11... | collective-permute-start | bytes 196616 | tf_op jit(solution)/shard_map/ppermute | solution.py:363
  9.7 0.9 %copy-start = (f32[2,72,128]{2,1,0:T(8,128)S(1)}, f32[2,72,128]{2,1,0:T(8,128)}, u32[]{:S(2)}) copy-start(f32[2,72,128]{2,1,0:T(8,128)} %get-tuple-element.8.source_ref) | copy-start | bytes 221188
  12.6 11.5 %copy-start.1 = (f32[2,64,128]{2,1,0:T(8,128)S(1)}, f32[2,64,128]{2,1,0:T(8,128)}, u32[]{:S(2)}) copy-start(f32[2,64,128]{2,1,0:T(8,128)} %get-tuple-element.10.refs_0_) | copy-start | bytes 196612
  12.6 13.5 %collective-permute-start.2 = (f32[4,72,128]{2,1,0:T(8,128)S(1)}, f32[4,72,128]{2,1,0:T(8,128)S(1)}, u32[]{:S(2)}, u32[]{:S(2)}) collective-permute-start(f32[4,72,128]{2,1,0:T(8,128)S(1)} %join.1.shells_ref), channel_id=1, source_target_pairs={{0,2},{1,3},{2,4},{3,5},{4,6},{5,7},{6,8},{7,9},{8,10},{9,11},{10,... | collective-permute-start | bytes 442376 | tf_op jit(solution)/shard_map/ppermute | solution.py:363
  12.7 13.4 %collective-permute-start.3 = (f32[4,72,128]{2,1,0:T(8,128)S(1)}, f32[4,72,128]{2,1,0:T(8,128)S(1)}, u32[]{:S(2)}, u32[]{:S(2)}) collective-permute-start(f32[4,72,128]{2,1,0:T(8,128)S(1)} %join.1.shells_ref), channel_id=1, source_target_pairs={{0,30},{1,31},{2,0},{3,1},{4,2},{5,3},{6,4},{7,5},{8,6},{9,7},{10,... | collective-permute-start | bytes 442376 | tf_op jit(solution)/shard_map/ppermute | solution.py:363
  24.3 19.7 %collective-permute-start.4 = (f32[7,64,128]{2,1,0:T(8,128)S(1)}, f32[7,64,128]{2,1,0:T(8,128)S(1)}, u32[]{:S(2)}, u32[]{:S(2)}) collective-permute-start(f32[7,64,128]{2,1,0:T(8,128)S(1)} %speeds.1.planes_ref), channel_id=1, source_target_pairs={{0,16},{1,17},{2,18},{3,19},{4,20},{5,21},{6,22},{7,23},{8,24},{9,... | collective-permute-start | bytes 688136 | tf_op jit(solution)/shard_map/ppermute | solution.py:363
  36.5 7.6 %collective-permute-start.5 = (f32[3,48,128]{2,1,0:T(8,128)S(1)}, f32[3,48,128]{2,1,0:T(8,128)S(1)}, u32[]{:S(2)}, u32[]{:S(2)}) collective-permute-start(f32[3,48,128]{2,1,0:T(8,128)S(1)} %side_slabs.2.refs_0_), channel_id=1, source_target_pairs={{0,16},{1,17},{2,18},{3,19},{4,20},{5,21},{6,22},{7,23},{8,24},{9,... | collective-permute-start | bytes 221192 | tf_op jit(solution)/shard_map/ppermute | solution.py:363
  41.5 4.8 %collective-permute-start.6 = (f32[3,16,128]{2,1,0:T(8,128)S(1)}, f32[3,16,128]{2,1,0:T(8,128)S(1)}, u32[]{:S(2)}, u32[]{:S(2)}) collective-permute-start(f32[3,16,128]{2,1,0:T(8,128)S(1)} %side_slabs.3.refs_1_), channel_id=1, source_target_pairs={{0,16},{1,17},{2,18},{3,19},{4,20},{5,21},{6,22},{7,23},{8,24},{9,... | collective-permute-start | bytes 73736 | tf_op jit(solution)/shard_map/ppermute | solution.py:363

commit v6 on v5

--- a/solution.py
+++ b/solution.py
@@ -204,7 +204,7 @@
         put(sum_ref, [terms[0] + down(terms[1], 4), terms[2]])
 
 
-def pair_loop(cells, per, far_rows, sum_rows, centre, out, dist, heavy):
+def pair_loop(cells, per, apart, far_rows, sum_rows, centre, out, dist, heavy):
     blocks = [(k, n) for k in range(3) for n in range(len(far_rows))]
     tall = LANES * len(blocks)
     wide = 3
@@ -217,12 +217,12 @@
     def distances(step, b):
         for u in range(per):
             c = step * per + u
-            for at in range(0, len(blocks), wide):
+            for at in range(0, len(blocks), apart):
                 others = jnp.concatenate(
-                    [far_rows[n][beside(c, k)] for k, n in blocks[at : at + wide]], axis=1
+                    [far_rows[n][beside(c, k)] for k, n in blocks[at : at + apart]], axis=1
                 )
                 low = u * tall + at * LANES
-                dist[b][low : low + wide * LANES] = lax.dot_general(
+                dist[b][low : low + apart * LANES] = lax.dot_general(
                     others, centre[c + first], TN, preferred_element_type=f32
                 )
 
@@ -264,7 +264,7 @@
             distances(jnp.minimum(step + 2, steps - 1), b)
         return 0
 
-    lax.fori_loop(0, steps // 2, body, 0)
+    lax.fori_loop(0, steps // 2, body, 0, unroll=8)
 
 
 def copy_kernel(source_ref, target_ref):
@@ -289,7 +289,7 @@
 def own_kernel(shells_ref, near_out, out_ref, rows, far_rows, sum_rows, *work):
     build(shells_ref, (0, CELLS), rows, far_rows, sum_rows, near_out)
     pair_loop(
-        (0, CELLS), 2, [far_rows], [sum_rows], near_out, out_ref, work[0:2], work[2:4]
+        (0, CELLS), 2, 1, [far_rows], [sum_rows], near_out, out_ref, work[0:2], work[2:4]
     )
 
 
@@ -299,7 +299,7 @@
     rows, far_rows, sum_rows, out, work = refs[0], refs[1:3], refs[3:5], refs[5], refs[6:]
     for side, there_ref in enumerate((up_ref, down_ref)):
         build(there_ref, cells, rows, far_rows[side], sum_rows[side])
-    pair_loop(cells, 1, far_rows, sum_rows, near_ref, out, work[0:2], work[2:4])
+    pair_loop(cells, 1, 2, far_rows, sum_rows, near_ref, out, work[0:2], work[2:4])
     both = out[...] + own_out[low:high]
     both = (both[:, :8] + both[:, 8:]).reshape(count * 8, LANES)
     rows[: count * 8] = both + pltpu.roll(both, count * 8 - 4, 0)

time: 47.1 us -> 42.8 us (0.909)
  Pallas kernels: 28.9 us -> 24.2 us
    pallas_call x2, Pallas kernels: 14.1 us -> 11 us  [per_device(): call(functools.partial(side_kernel, cells), 0, 5, shape(3, count, LANES),...]
    pallas_call x1, Pallas kernels: 7.01 us -> 5.41 us  [per_device(): call(own_kernel, 0, 1, [shape(CELLS, FEATURES, LANES, dtype=bf16), shape(...]
  transfers between devices with their start and end apart: 7 -> 7, of which waited for: 2 -> 2; matrix products, arithmetic and copies ran while one was open for 0% -> 0% of each run, Pallas kernels for 49% -> 43%
where the time goes in v6:
time: 42.8 us; the launch traced here: 42.6 us
  Pallas kernels  24.2 us (57%)
  starting transfers between devices  12.4 us (29%)
  waiting for transfers between devices  3.59 us (8%)
  between operations  1.51 us (4%)
  local copies, waits for them, and re-layouts  0.89 us (2%)
    ppermute x7, starting transfers between devices, sent(): return lax.ppermute(value, ('slab', 'dom'), pairs)  12.4 us
    pallas_call x2, Pallas kernels, per_device(): call(functools.partial(side_kernel, cells), 0, 5, shape(3, count, LANES),...  11 us
    pallas_call x1, Pallas kernels, per_device(): call(own_kernel, 0, 1, [shape(CELLS, FEATURES, LANES, dtype=bf16), shape(...  5.41 us
    pallas_call x1, Pallas kernels, per_device(): call(functools.partial(pack_kernel, n_dom), 2, 0, [shape(half, tall, LANE...  5.35 us
    ppermute x7, waiting for transfers between devices, sent(): return lax.ppermute(value, ('slab', 'dom'), pairs)  3.59 us
    unnamed x4, local copies, waits for them, and re-layouts  0.89 us
  transfers between devices with their start and end apart: 7, of which 2 were waited for; matrix products, arithmetic and copies ran while one was open for 0% of the time, Pallas kernels for 43%

profile of v6, /device:TPU:0, one launch (start us, length us, event | category | flops | bytes accessed | tf_op | source)
XLA Modules:
  0.0 42.6 jit_solution(14088526823056613166)
XLA Ops:
  1.3 5.3 %pack.1 = (f32[2,72,128]{2,1,0:T(8,128)}, f32[2,72,128]{2,1,0:T(8,128)}, f32[2,64,128]{2,1,0:T(8,128)}, f32[2,64,128]{2,1,0:T(8,128)}) custom-call(s32[1]{0:T(128)} %bitcast.me_ref, s32[1]{0:T(128)S(6)} %copy.9.count_ref, f32[3,6144]{1,0:T(4,128)} %pos_any.1, f32[3,6144]{1,0:T(4,128)} %vel_any.1, f32[1,6144]{1,0:T(1,128)} %bitcast.3, s32[1,6144]{1,0:T(1,128)} %bitcast.4), custom_call_target="tpu_custom_call" | custom-call | tf_op jit(solution)/shard_map/pack/pallas_call | solution.py:376
  6.6 3.0 %collective-permute-start = (f32[2,72,128]{2,1,0:T(8,128)}, f32[2,72,128]{2,1,0:T(8,128)S(1)}, u32[]{:S(2)}, u32[]{:S(2)}) collective-permute-start(f32[2,72,128]{2,1,0:T(8,128)} %get-tuple-element.9), channel_id=1, source_target_pairs={{0,1},{1,0},{2,3},{3,2},{4,5},{5,4},{6,7},{7,6},{8,9},{9,8},{10,11... | collective-permute-start | bytes 221192 | tf_op jit(solution)/shard_map/ppermute | solution.py:363
  9.7 0.1 collective-permute-start.1
  9.7 0.9 %copy-done = f32[2,72,128]{2,1,0:T(8,128)S(1)} copy-done((f32[2,72,128]{2,1,0:T(8,128)S(1)}, f32[2,72,128]{2,1,0:T(8,128)}, u32[]{:S(2)}) %copy-start) | copy-done | bytes 73752
  10.6 1.8 %collective-permute-done.refs_1_ = f32[2,72,128]{2,1,0:T(8,128)S(1)} collective-permute-done((f32[2,72,128]{2,1,0:T(8,128)}, f32[2,72,128]{2,1,0:T(8,128)S(1)}, u32[]{:S(2)}, u32[]{:S(2)}) %collective-permute-start) | collective-permute-done | bytes 73760 | tf_op jit(solution)/shard_map/ppermute | solution.py:363
  12.4 0.2 join.1.shells_ref
  12.6 0.1 collective-permute-start.2
  12.7 4.4 %collective-permute-start.3 = (f32[4,72,128]{2,1,0:T(8,128)S(1)}, f32[4,72,128]{2,1,0:T(8,128)S(1)}, u32[]{:S(2)}, u32[]{:S(2)}) collective-permute-start(f32[4,72,128]{2,1,0:T(8,128)S(1)} %join.1.shells_ref), channel_id=1, source_target_pairs={{0,30},{1,31},{2,0},{3,1},{4,2},{5,3},{6,4},{7,5},{8,6},{9,7},{10,... | collective-permute-start | bytes 442376 | tf_op jit(solution)/shard_map/ppermute | solution.py:363
  17.1 5.4 %own_slab.1 = (bf16[64,32,128]{2,1,0:T(8,128)(2,1)S(1)}, f32[64,16,128]{2,1,0:T(8,128)S(1)}) custom-call(f32[4,72,128]{2,1,0:T(8,128)S(1)} %join.1.shells_ref), custom_call_target="tpu_custom_call" | custom-call | flops 8000000000 | bytes 1000000 | tf_op jit(solution)/shard_map/own_slab/pallas_call | solution.py:426
  22.5 0.0 collective-permute-done.1.refs_1_
  22.6 0.2 speeds.1.planes_ref
  22.7 1.8 %collective-permute-start.4 = (f32[7,64,128]{2,1,0:T(8,128)S(1)}, f32[7,64,128]{2,1,0:T(8,128)S(1)}, u32[]{:S(2)}, u32[]{:S(2)}) collective-permute-start(f32[7,64,128]{2,1,0:T(8,128)S(1)} %speeds.1.planes_ref), channel_id=1, source_target_pairs={{0,16},{1,17},{2,18},{3,19},{4,20},{5,21},{6,22},{7,23},{8,24},{9,... | collective-permute-start | bytes 688136 | tf_op jit(solution)/shard_map/ppermute | solution.py:363
  24.5 0.0 collective-permute-done.2.up_ref
  24.5 0.0 collective-permute-done.3.down_ref
  24.5 8.1 %side_slabs.2.refs_0_ = f32[3,48,128]{2,1,0:T(8,128)S(1)} custom-call(f32[4,72,128]{2,1,0:T(8,128)S(1)} %collective-permute-done.2.up_ref, f32[4,72,128]{2,1,0:T(8,128)S(1)} %collective-permute-done.3.down_ref, bf16[64,32,128]{2,1,0:T(8,128)(2,1)S(1)} %get-tuple-element.12.near_ref, f32[64,16,128]{2,1,0:T(8,128)S(1)} %get-tuple-element.13.own_out, ...), custom_call_target="tpu_custom_call" | custom-call | flops 8000000000 | bytes 1000000 | tf_op jit(solution)/shard_map/side_slabs/pallas_call | solution.py:440
  32.6 1.3 %collective-permute-start.5 = (f32[3,48,128]{2,1,0:T(8,128)S(1)}, f32[3,48,128]{2,1,0:T(8,128)S(1)}, u32[]{:S(2)}, u32[]{:S(2)}) collective-permute-start(f32[3,48,128]{2,1,0:T(8,128)S(1)} %side_slabs.2.refs_0_), channel_id=1, source_target_pairs={{0,16},{1,17},{2,18},{3,19},{4,20},{5,21},{6,22},{7,23},{8,24},{9,... | collective-permute-start | bytes 221192 | tf_op jit(solution)/shard_map/ppermute | solution.py:363
  33.9 2.9 %side_slabs.3.refs_1_ = f32[3,16,128]{2,1,0:T(8,128)S(1)} custom-call(f32[4,72,128]{2,1,0:T(8,128)S(1)} %collective-permute-done.2.up_ref, f32[4,72,128]{2,1,0:T(8,128)S(1)} %collective-permute-done.3.down_ref, bf16[64,32,128]{2,1,0:T(8,128)(2,1)S(1)} %get-tuple-element.12.near_ref, f32[64,16,128]{2,1,0:T(8,128)S(1)} %get-tuple-element.13.own_out, ...), custom_call_target="tpu_custom_call" | custom-call | flops 8000000000 | bytes 1000000 | tf_op jit(solution)/shard_map/side_slabs/pallas_call | solution.py:440
  36.8 1.8 %collective-permute-start.6 = (f32[3,16,128]{2,1,0:T(8,128)S(1)}, f32[3,16,128]{2,1,0:T(8,128)S(1)}, u32[]{:S(2)}, u32[]{:S(2)}) collective-permute-start(f32[3,16,128]{2,1,0:T(8,128)S(1)} %side_slabs.3.refs_1_), channel_id=1, source_target_pairs={{0,16},{1,17},{2,18},{3,19},{4,20},{5,21},{6,22},{7,23},{8,24},{9,... | collective-permute-start | bytes 73736 | tf_op jit(solution)/shard_map/ppermute | solution.py:363
  38.6 0.7 %state.1 = f32[10,1,64,128]{3,2,1,0:T(8,128)} custom-call(f32[7,64,128]{2,1,0:T(8,128)S(1)} %speeds.1.planes_ref, f32[3,48,128]{2,1,0:T(8,128)S(1)} %side_slabs.2.refs_0_, f32[3,16,128]{2,1,0:T(8,128)S(1)} %side_slabs.3.refs_1_), custom_call_target="tpu_custom_call" | custom-call | tf_op jit(solution)/shard_map/state/pallas_call | solution.py:452
  39.3 0.0 collective-permute-done.5.refs_0_
  39.3 0.0 collective-permute-done.4.planes_ref
  39.3 0.7 %buddy.1._ = f32[10,1,64,128]{3,2,1,0:T(8,128)} custom-call(f32[7,64,128]{2,1,0:T(8,128)S(1)} %collective-permute-done.4.planes_ref, f32[3,48,128]{2,1,0:T(8,128)S(1)} %collective-permute-done.5.refs_0_), custom_call_target="tpu_custom_call" | custom-call | tf_op jit(solution)/shard_map/buddy/pallas_call | solution.py:453
  40.1 1.8 %collective-permute-done.6.accel_ref = f32[3,16,128]{2,1,0:T(8,128)S(1)} collective-permute-done((f32[3,16,128]{2,1,0:T(8,128)S(1)}, f32[3,16,128]{2,1,0:T(8,128)S(1)}, u32[]{:S(2)}, u32[]{:S(2)}) %collective-permute-start.6) | collective-permute-done | bytes 24608 | tf_op jit(solution)/shard_map/ppermute | solution.py:363
  41.8 0.6 %buddy_end.1 = f32[10,1,64,128]{3,2,1,0:T(8,128)} custom-call(f32[10,1,64,128]{3,2,1,0:T(8,128)} %buddy.1._, f32[7,64,128]{2,1,0:T(8,128)S(1)} %collective-permute-done.4.planes_ref, f32[3,16,128]{2,1,0:T(8,128)S(1)} %collective-permute-done.6.accel_ref), custom_call_target="tpu_custom_call", output_to_operand_aliasing={{}: (0, {})} | custom-call | tf_op jit(solution)/shard_map/buddy_end/pallas_call | solution.py:454
  (4 shorter events, 0.0 us)
Async XLA Ops:
  6.6 5.8 %collective-permute-start = (f32[2,72,128]{2,1,0:T(8,128)}, f32[2,72,128]{2,1,0:T(8,128)S(1)}, u32[]{:S(2)}, u32[]{:S(2)}) collective-permute-start(f32[2,72,128]{2,1,0:T(8,128)} %get-tuple-element.9), channel_id=1, source_target_pairs={{0,1},{1,0},{2,3},{3,2},{4,5},{5,4},{6,7},{7,6},{8,9},{9,8},{10,11... | collective-permute-start | bytes 221192 | tf_op jit(solution)/shard_map/ppermute | solution.py:363
  9.7 12.9 %collective-permute-start.1 = (f32[2,64,128]{2,1,0:T(8,128)}, f32[2,64,128]{2,1,0:T(8,128)S(1)}, u32[]{:S(2)}, u32[]{:S(2)}) collective-permute-start(f32[2,64,128]{2,1,0:T(8,128)} %get-tuple-element.11), channel_id=1, source_target_pairs={{0,1},{1,0},{2,3},{3,2},{4,5},{5,4},{6,7},{7,6},{8,9},{9,8},{10,11... | collective-permute-start | bytes 196616 | tf_op jit(solution)/shard_map/ppermute | solution.py:363
  9.7 0.9 %copy-start = (f32[2,72,128]{2,1,0:T(8,128)S(1)}, f32[2,72,128]{2,1,0:T(8,128)}, u32[]{:S(2)}) copy-start(f32[2,72,128]{2,1,0:T(8,128)} %get-tuple-element.8.source_ref) | copy-start | bytes 221188
  12.6 9.9 %copy-start.1 = (f32[2,64,128]{2,1,0:T(8,128)S(1)}, f32[2,64,128]{2,1,0:T(8,128)}, u32[]{:S(2)}) copy-start(f32[2,64,128]{2,1,0:T(8,128)} %get-tuple-element.10.refs_0_) | copy-start | bytes 196612
  12.6 11.9 %collective-permute-start.2 = (f32[4,72,128]{2,1,0:T(8,128)S(1)}, f32[4,72,128]{2,1,0:T(8,128)S(1)}, u32[]{:S(2)}, u32[]{:S(2)}) collective-permute-start(f32[4,72,128]{2,1,0:T(8,128)S(1)} %join.1.shells_ref), channel_id=1, source_target_pairs={{0,2},{1,3},{2,4},{3,5},{4,6},{5,7},{6,8},{7,9},{8,10},{9,11},{10,... | collective-permute-start | bytes 442376 | tf_op jit(solution)/shard_map/ppermute | solution.py:363
  12.7 11.8 %collective-permute-start.3 = (f32[4,72,128]{2,1,0:T(8,128)S(1)}, f32[4,72,128]{2,1,0:T(8,128)S(1)}, u32[]{:S(2)}, u32[]{:S(2)}) collective-permute-start(f32[4,72,128]{2,1,0:T(8,128)S(1)} %join.1.shells_ref), channel_id=1, source_target_pairs={{0,30},{1,31},{2,0},{3,1},{4,2},{5,3},{6,4},{7,5},{8,6},{9,7},{10,... | collective-permute-start | bytes 442376 | tf_op jit(solution)/shard_map/ppermute | solution.py:363
  22.7 16.6 %collective-permute-start.4 = (f32[7,64,128]{2,1,0:T(8,128)S(1)}, f32[7,64,128]{2,1,0:T(8,128)S(1)}, u32[]{:S(2)}, u32[]{:S(2)}) collective-permute-start(f32[7,64,128]{2,1,0:T(8,128)S(1)} %speeds.1.planes_ref), channel_id=1, source_target_pairs={{0,16},{1,17},{2,18},{3,19},{4,20},{5,21},{6,22},{7,23},{8,24},{9,... | collective-permute-start | bytes 688136 | tf_op jit(solution)/shard_map/ppermute | solution.py:363
  32.6 6.7 %collective-permute-start.5 = (f32[3,48,128]{2,1,0:T(8,128)S(1)}, f32[3,48,128]{2,1,0:T(8,128)S(1)}, u32[]{:S(2)}, u32[]{:S(2)}) collective-permute-start(f32[3,48,128]{2,1,0:T(8,128)S(1)} %side_slabs.2.refs_0_), channel_id=1, source_target_pairs={{0,16},{1,17},{2,18},{3,19},{4,20},{5,21},{6,22},{7,23},{8,24},{9,... | collective-permute-start | bytes 221192 | tf_op jit(solution)/shard_map/ppermute | solution.py:363
  36.8 5.1 %collective-permute-start.6 = (f32[3,16,128]{2,1,0:T(8,128)S(1)}, f32[3,16,128]{2,1,0:T(8,128)S(1)}, u32[]{:S(2)}, u32[]{:S(2)}) collective-permute-start(f32[3,16,128]{2,1,0:T(8,128)S(1)} %side_slabs.3.refs_1_), channel_id=1, source_target_pairs={{0,16},{1,17},{2,18},{3,19},{4,20},{5,21},{6,22},{7,23},{8,24},{9,... | collective-permute-start | bytes 73736 | tf_op jit(solution)/shard_map/ppermute | solution.py:363

commit v7 on v6

--- a/solution.py
+++ b/solution.py
@@ -82,7 +82,7 @@
         span = slice(at, at + step)
         rank, target = rank_ref[:, span], target_ref[:, span]
         upper = rank >= part
-        mark = jnp.where(row == jnp.where(upper, rank - part, rank), 1.0, 0.0)
+        mark = row == jnp.where(upper, rank - part, rank)
         place = jnp.where(upper & (target >= 0), target + targets, target)
         hot = jnp.where(column == place, 1.0, 0.0).astype(bf16)
         values = [pos_ref[i : i + 1, span] + drift_step * vel_ref[i : i + 1, span] for i in range(3)]
@@ -90,7 +90,7 @@
         values += [vel_ref[i : i + 1, span] for i in range(3)]
         pieces = [split(value, 2) for value in values]
         left = [
-            jnp.concatenate([(mark * piece[k]).astype(bf16) for piece in pieces], axis=0)
+            jnp.concatenate([jnp.where(mark, piece[k], 0.0).astype(bf16) for piece in pieces], axis=0)
             for k in range(2)
         ]
         found = lax.dot_general(
@@ -398,11 +398,13 @@
             sent(parts[-k % n_dom], n_slab, n_dom, 0, -k) for k in range(1, n_dom)
         ]
 
-    places, speeds = swapped(whole[:n_dom]), swapped(whole[n_dom:])
+    places = swapped(whole[:n_dom])
     places[0] = call(copy_kernel, 0, 1, shape(half, tall, LANES), name="own_piece")(places[0])
     shells = call(
         functools.partial(join_kernel, n_dom), 1, n_dom, shape(4, tall, LANES), name="join"
     )(me, *places)
+    shells, held = lax.optimization_barrier((shells, whole[n_dom:]))
+    speeds = swapped(held)
     planes = call(
         functools.partial(speeds_kernel, n_dom),
         1,

time: 42.8 us -> 44.1 us (1.030)
  starting transfers between devices: 12.4 us -> 13.4 us
  waiting for transfers between devices: 3.59 us -> 4.1 us
    ppermute x7, starting transfers between devices: 12.4 us -> 13.4 us  [sent(): return lax.ppermute(value, ('slab', 'dom'), pairs)]
    ppermute x7, waiting for transfers between devices: 3.59 us -> 4.1 us  [sent(): return lax.ppermute(value, ('slab', 'dom'), pairs)]
    unnamed x4 -> x6, local copies, waits for them, and re-layouts: 0.89 us -> 0.89 us
  transfers between devices with their start and end apart: 7 -> 7, of which waited for: 2 -> 2; matrix products, arithmetic and copies ran while one was open for 0% -> 0% of each run, Pallas kernels for 43% -> 41%
where the time goes in v7:
time: 44.1 us; the launch traced here: 43.9 us
  Pallas kernels  24 us (54%)
  starting transfers between devices  13.4 us (30%)
  waiting for transfers between devices  4.1 us (9%)
  between operations  1.52 us (3%)
  local copies, waits for them, and re-layouts  0.89 us (2%)
    ppermute x7, starting transfers between devices, sent(): return lax.ppermute(value, ('slab', 'dom'), pairs)  13.4 us
    pallas_call x2, Pallas kernels, per_device(): call(functools.partial(side_kernel, cells), 0, 5, shape(3, count, LANES),...  11 us
    pallas_call x1, Pallas kernels, per_device(): call(own_kernel, 0, 1, [shape(CELLS, FEATURES, LANES, dtype=bf16), shape(...  5.42 us
    pallas_call x1, Pallas kernels, per_device(): call(functools.partial(pack_kernel, n_dom), 2, 0, [shape(half, tall, LANE...  5.09 us
    ppermute x7, waiting for transfers between devices, sent(): return lax.ppermute(value, ('slab', 'dom'), pairs)  4.1 us
    unnamed x6, local copies, waits for them, and re-layouts  0.89 us
  transfers between devices with their start and end apart: 7, of which 2 were waited for; matrix products, arithmetic and copies ran while one was open for 0% of the time, Pallas kernels for 41%

profile of v7, /device:TPU:0, one launch (start us, length us, event | category | flops | bytes accessed | tf_op | source)
XLA Modules:
  0.0 43.9 jit_solution(9229162753139461055)
XLA Ops:
  1.3 5.1 %pack.1 = (f32[2,72,128]{2,1,0:T(8,128)}, f32[2,72,128]{2,1,0:T(8,128)}, f32[2,64,128]{2,1,0:T(8,128)}, f32[2,64,128]{2,1,0:T(8,128)}) custom-call(s32[1]{0:T(128)} %bitcast.me_ref, s32[1]{0:T(128)S(6)} %copy.9.count_ref, f32[3,6144]{1,0:T(4,128)} %pos_any.1, f32[3,6144]{1,0:T(4,128)} %vel_any.1, f32[1,6144]{1,0:T(1,128)} %bitcast.3, s32[1,6144]{1,0:T(1,128)} %bitcast.4), custom_call_target="tpu_custom_call" | custom-call | tf_op jit(solution)/shard_map/pack/pallas_call | solution.py:376
  6.4 3.0 %collective-permute-start = (f32[2,72,128]{2,1,0:T(8,128)}, f32[2,72,128]{2,1,0:T(8,128)S(1)}, u32[]{:S(2)}, u32[]{:S(2)}) collective-permute-start(f32[2,72,128]{2,1,0:T(8,128)} %get-tuple-element.12), channel_id=1, source_target_pairs={{0,1},{1,0},{2,3},{3,2},{4,5},{5,4},{6,7},{7,6},{8,9},{9,8},{10,11... | collective-permute-start | bytes 221192 | tf_op jit(solution)/shard_map/ppermute | solution.py:363
  9.4 0.9 %copy-done = f32[2,72,128]{2,1,0:T(8,128)S(1)} copy-done((f32[2,72,128]{2,1,0:T(8,128)S(1)}, f32[2,72,128]{2,1,0:T(8,128)}, u32[]{:S(2)}) %copy-start) | copy-done | bytes 73752
  10.3 1.6 %collective-permute-done.refs_1_ = f32[2,72,128]{2,1,0:T(8,128)S(1)} collective-permute-done((f32[2,72,128]{2,1,0:T(8,128)}, f32[2,72,128]{2,1,0:T(8,128)S(1)}, u32[]{:S(2)}, u32[]{:S(2)}) %collective-permute-start) | collective-permute-done | bytes 73760 | tf_op jit(solution)/shard_map/ppermute | solution.py:363
  12.0 0.2 join.1.shells_ref
  12.1 0.1 collective-permute-start.2
  12.2 4.4 %collective-permute-start.3 = (f32[4,72,128]{2,1,0:T(8,128)S(1)}, f32[4,72,128]{2,1,0:T(8,128)S(1)}, u32[]{:S(2)}, u32[]{:S(2)}) collective-permute-start(f32[4,72,128]{2,1,0:T(8,128)S(1)} %join.1.shells_ref), channel_id=1, source_target_pairs={{0,30},{1,31},{2,0},{3,1},{4,2},{5,3},{6,4},{7,5},{8,6},{9,7},{10,... | collective-permute-start | bytes 442376 | tf_op jit(solution)/shard_map/ppermute | solution.py:363
  16.6 2.0 %collective-permute-start.1 = (f32[2,64,128]{2,1,0:T(8,128)S(1)}, f32[2,64,128]{2,1,0:T(8,128)S(1)}, u32[]{:S(2)}, u32[]{:S(2)}) collective-permute-start(f32[2,64,128]{2,1,0:T(8,128)S(1)} %copy-done.2), channel_id=1, source_target_pairs={{0,1},{1,0},{2,3},{3,2},{4,5},{5,4},{6,7},{7,6},{8,9},{9,8},{10,11... | collective-permute-start | bytes 196616 | tf_op jit(solution)/shard_map/ppermute | solution.py:363
  18.7 5.4 %own_slab.1 = (bf16[64,32,128]{2,1,0:T(8,128)(2,1)S(1)}, f32[64,16,128]{2,1,0:T(8,128)S(1)}) custom-call(f32[4,72,128]{2,1,0:T(8,128)S(1)} %join.1.shells_ref), custom_call_target="tpu_custom_call" | custom-call | flops 8000000000 | bytes 1000000 | tf_op jit(solution)/shard_map/own_slab/pallas_call | solution.py:428
  24.1 0.0 collective-permute-done.1.refs_1_
  24.1 0.2 speeds.1.planes_ref
  24.3 0.8 %collective-permute-start.4 = (f32[7,64,128]{2,1,0:T(8,128)S(1)}, f32[7,64,128]{2,1,0:T(8,128)S(1)}, u32[]{:S(2)}, u32[]{:S(2)}) collective-permute-start(f32[7,64,128]{2,1,0:T(8,128)S(1)} %speeds.1.planes_ref), channel_id=1, source_target_pairs={{0,16},{1,17},{2,18},{3,19},{4,20},{5,21},{6,22},{7,23},{8,24},{9,... | collective-permute-start | bytes 688136 | tf_op jit(solution)/shard_map/ppermute | solution.py:363
  25.1 0.0 collective-permute-done.2.up_ref
  25.1 0.0 collective-permute-done.3.down_ref
  25.1 8.1 %side_slabs.2.refs_0_ = f32[3,48,128]{2,1,0:T(8,128)S(1)} custom-call(f32[4,72,128]{2,1,0:T(8,128)S(1)} %collective-permute-done.2.up_ref, f32[4,72,128]{2,1,0:T(8,128)S(1)} %collective-permute-done.3.down_ref, bf16[64,32,128]{2,1,0:T(8,128)(2,1)S(1)} %get-tuple-element.18.near_ref, f32[64,16,128]{2,1,0:T(8,128)S(1)} %get-tuple-element.19.own_out, ...), custom_call_target="tpu_custom_call" | custom-call | flops 8000000000 | bytes 1000000 | tf_op jit(solution)/shard_map/side_slabs/pallas_call | solution.py:442
  33.2 2.2 %collective-permute-start.5 = (f32[3,48,128]{2,1,0:T(8,128)S(1)}, f32[3,48,128]{2,1,0:T(8,128)S(1)}, u32[]{:S(2)}, u32[]{:S(2)}) collective-permute-start(f32[3,48,128]{2,1,0:T(8,128)S(1)} %side_slabs.2.refs_0_), channel_id=1, source_target_pairs={{0,16},{1,17},{2,18},{3,19},{4,20},{5,21},{6,22},{7,23},{8,24},{9,... | collective-permute-start | bytes 221192 | tf_op jit(solution)/shard_map/ppermute | solution.py:363
  35.4 2.9 %side_slabs.3.refs_1_ = f32[3,16,128]{2,1,0:T(8,128)S(1)} custom-call(f32[4,72,128]{2,1,0:T(8,128)S(1)} %collective-permute-done.2.up_ref, f32[4,72,128]{2,1,0:T(8,128)S(1)} %collective-permute-done.3.down_ref, bf16[64,32,128]{2,1,0:T(8,128)(2,1)S(1)} %get-tuple-element.18.near_ref, f32[64,16,128]{2,1,0:T(8,128)S(1)} %get-tuple-element.19.own_out, ...), custom_call_target="tpu_custom_call" | custom-call | flops 8000000000 | bytes 1000000 | tf_op jit(solution)/shard_map/side_slabs/pallas_call | solution.py:442
  38.3 0.8 %collective-permute-start.6 = (f32[3,16,128]{2,1,0:T(8,128)S(1)}, f32[3,16,128]{2,1,0:T(8,128)S(1)}, u32[]{:S(2)}, u32[]{:S(2)}) collective-permute-start(f32[3,16,128]{2,1,0:T(8,128)S(1)} %side_slabs.3.refs_1_), channel_id=1, source_target_pairs={{0,16},{1,17},{2,18},{3,19},{4,20},{5,21},{6,22},{7,23},{8,24},{9,... | collective-permute-start | bytes 73736 | tf_op jit(solution)/shard_map/ppermute | solution.py:363
  39.2 0.7 %state.1 = f32[10,1,64,128]{3,2,1,0:T(8,128)} custom-call(f32[7,64,128]{2,1,0:T(8,128)S(1)} %speeds.1.planes_ref, f32[3,48,128]{2,1,0:T(8,128)S(1)} %side_slabs.2.refs_0_, f32[3,16,128]{2,1,0:T(8,128)S(1)} %side_slabs.3.refs_1_), custom_call_target="tpu_custom_call" | custom-call | tf_op jit(solution)/shard_map/state/pallas_call | solution.py:454
  39.9 0.0 collective-permute-done.5.refs_0_
  39.9 0.0 collective-permute-done.4.planes_ref
  39.9 0.7 %buddy.1._ = f32[10,1,64,128]{3,2,1,0:T(8,128)} custom-call(f32[7,64,128]{2,1,0:T(8,128)S(1)} %collective-permute-done.4.planes_ref, f32[3,48,128]{2,1,0:T(8,128)S(1)} %collective-permute-done.5.refs_0_), custom_call_target="tpu_custom_call" | custom-call | tf_op jit(solution)/shard_map/buddy/pallas_call | solution.py:455
  40.7 2.4 %collective-permute-done.6.accel_ref = f32[3,16,128]{2,1,0:T(8,128)S(1)} collective-permute-done((f32[3,16,128]{2,1,0:T(8,128)S(1)}, f32[3,16,128]{2,1,0:T(8,128)S(1)}, u32[]{:S(2)}, u32[]{:S(2)}) %collective-permute-start.6) | collective-permute-done | bytes 24608 | tf_op jit(solution)/shard_map/ppermute | solution.py:363
  43.1 0.6 %buddy_end.1 = f32[10,1,64,128]{3,2,1,0:T(8,128)} custom-call(f32[10,1,64,128]{3,2,1,0:T(8,128)} %buddy.1._, f32[7,64,128]{2,1,0:T(8,128)S(1)} %collective-permute-done.4.planes_ref, f32[3,16,128]{2,1,0:T(8,128)S(1)} %collective-permute-done.6.accel_ref), custom_call_target="tpu_custom_call", output_to_operand_aliasing={{}: (0, {})} | custom-call | tf_op jit(solution)/shard_map/buddy_end/pallas_call | solution.py:456
  (6 shorter events, 0.0 us)
Async XLA Ops:
  6.4 5.6 %collective-permute-start = (f32[2,72,128]{2,1,0:T(8,128)}, f32[2,72,128]{2,1,0:T(8,128)S(1)}, u32[]{:S(2)}, u32[]{:S(2)}) collective-permute-start(f32[2,72,128]{2,1,0:T(8,128)} %get-tuple-element.12), channel_id=1, source_target_pairs={{0,1},{1,0},{2,3},{3,2},{4,5},{5,4},{6,7},{7,6},{8,9},{9,8},{10,11... | collective-permute-start | bytes 221192 | tf_op jit(solution)/shard_map/ppermute | solution.py:363
  9.4 0.9 %copy-start = (f32[2,72,128]{2,1,0:T(8,128)S(1)}, f32[2,72,128]{2,1,0:T(8,128)}, u32[]{:S(2)}) copy-start(f32[2,72,128]{2,1,0:T(8,128)} %get-tuple-element.11.source_ref) | copy-start | bytes 221188
  10.3 6.3 %copy-start.2 = (f32[2,64,128]{2,1,0:T(8,128)S(1)}, f32[2,64,128]{2,1,0:T(8,128)}, u32[]{:S(2)}) copy-start(f32[2,64,128]{2,1,0:T(8,128)} %get-tuple-element.17) | copy-start | bytes 196612
  12.1 12.0 %copy-start.1 = (f32[2,64,128]{2,1,0:T(8,128)S(1)}, f32[2,64,128]{2,1,0:T(8,128)}, u32[]{:S(2)}) copy-start(f32[2,64,128]{2,1,0:T(8,128)} %get-tuple-element.16.refs_0_) | copy-start | bytes 196612
  12.1 13.0 %collective-permute-start.2 = (f32[4,72,128]{2,1,0:T(8,128)S(1)}, f32[4,72,128]{2,1,0:T(8,128)S(1)}, u32[]{:S(2)}, u32[]{:S(2)}) collective-permute-start(f32[4,72,128]{2,1,0:T(8,128)S(1)} %join.1.shells_ref), channel_id=1, source_target_pairs={{0,2},{1,3},{2,4},{3,5},{4,6},{5,7},{6,8},{7,9},{8,10},{9,11},{10,... | collective-permute-start | bytes 442376 | tf_op jit(solution)/shard_map/ppermute | solution.py:363
  12.2 12.9 %collective-permute-start.3 = (f32[4,72,128]{2,1,0:T(8,128)S(1)}, f32[4,72,128]{2,1,0:T(8,128)S(1)}, u32[]{:S(2)}, u32[]{:S(2)}) collective-permute-start(f32[4,72,128]{2,1,0:T(8,128)S(1)} %join.1.shells_ref), channel_id=1, source_target_pairs={{0,30},{1,31},{2,0},{3,1},{4,2},{5,3},{6,4},{7,5},{8,6},{9,7},{10,... | collective-permute-start | bytes 442376 | tf_op jit(solution)/shard_map/ppermute | solution.py:363
  16.6 7.4 %collective-permute-start.1 = (f32[2,64,128]{2,1,0:T(8,128)S(1)}, f32[2,64,128]{2,1,0:T(8,128)S(1)}, u32[]{:S(2)}, u32[]{:S(2)}) collective-permute-start(f32[2,64,128]{2,1,0:T(8,128)S(1)} %copy-done.2), channel_id=1, source_target_pairs={{0,1},{1,0},{2,3},{3,2},{4,5},{5,4},{6,7},{7,6},{8,9},{9,8},{10,11... | collective-permute-start | bytes 196616 | tf_op jit(solution)/shard_map/ppermute | solution.py:363
  24.3 15.7 %collective-permute-start.4 = (f32[7,64,128]{2,1,0:T(8,128)S(1)}, f32[7,64,128]{2,1,0:T(8,128)S(1)}, u32[]{:S(2)}, u32[]{:S(2)}) collective-permute-start(f32[7,64,128]{2,1,0:T(8,128)S(1)} %speeds.1.planes_ref), channel_id=1, source_target_pairs={{0,16},{1,17},{2,18},{3,19},{4,20},{5,21},{6,22},{7,23},{8,24},{9,... | collective-permute-start | bytes 688136 | tf_op jit(solution)/shard_map/ppermute | solution.py:363
  33.2 6.7 %collective-permute-start.5 = (f32[3,48,128]{2,1,0:T(8,128)S(1)}, f32[3,48,128]{2,1,0:T(8,128)S(1)}, u32[]{:S(2)}, u32[]{:S(2)}) collective-permute-start(f32[3,48,128]{2,1,0:T(8,128)S(1)} %side_slabs.2.refs_0_), channel_id=1, source_target_pairs={{0,16},{1,17},{2,18},{3,19},{4,20},{5,21},{6,22},{7,23},{8,24},{9,... | collective-permute-start | bytes 221192 | tf_op jit(solution)/shard_map/ppermute | solution.py:363
  38.3 4.8 %collective-permute-start.6 = (f32[3,16,128]{2,1,0:T(8,128)S(1)}, f32[3,16,128]{2,1,0:T(8,128)S(1)}, u32[]{:S(2)}, u32[]{:S(2)}) collective-permute-start(f32[3,16,128]{2,1,0:T(8,128)S(1)} %side_slabs.3.refs_1_), channel_id=1, source_target_pairs={{0,16},{1,17},{2,18},{3,19},{4,20},{5,21},{6,22},{7,23},{8,24},{9,... | collective-permute-start | bytes 73736 | tf_op jit(solution)/shard_map/ppermute | solution.py:363

commit v8 on v7

--- a/solution.py
+++ b/solution.py
@@ -324,6 +324,12 @@
         low = high
 
 
+def place_kernel(planes_ref, out_ref):
+    for comp in range(4):
+        out_ref[comp, 0] = planes_ref[comp]
+    out_ref[4:] = jnp.zeros((6, 1) + planes_ref.shape[1:], f32)
+
+
 def last_kick_kernel(low, _, planes_ref, accel_ref, out_ref, kicked, sem):
     high = low + accel_ref.shape[1]
     for comp in range(3):
@@ -398,13 +404,11 @@
             sent(parts[-k % n_dom], n_slab, n_dom, 0, -k) for k in range(1, n_dom)
         ]
 
-    places = swapped(whole[:n_dom])
+    places, speeds = swapped(whole[:n_dom]), swapped(whole[n_dom:])
     places[0] = call(copy_kernel, 0, 1, shape(half, tall, LANES), name="own_piece")(places[0])
     shells = call(
         functools.partial(join_kernel, n_dom), 1, n_dom, shape(4, tall, LANES), name="join"
     )(me, *places)
-    shells, held = lax.optimization_barrier((shells, whole[n_dom:]))
-    speeds = swapped(held)
     planes = call(
         functools.partial(speeds_kernel, n_dom),
         1,
@@ -434,35 +438,29 @@
         name="own_slab",
         cost=pl.CostEstimate(flops=8_000_000_000, bytes_accessed=1_000_000, transcendentals=0),
     )(shells)
-    accels = []
-    cut = CELLS * 3 // 4
-    for cells in ((0, cut), (cut, CELLS)):
-        count = cells[1] - cells[0]
-        accels.append(
-            call(
-                functools.partial(side_kernel, cells),
-                0,
-                5,
-                shape(3, count, LANES),
-                row_work(2) + [pltpu.VMEM((count, 16, LANES), f32)] + pair_work(768),
-                name="side_slabs",
-                cost=pl.CostEstimate(flops=8_000_000_000, bytes_accessed=1_000_000, transcendentals=0),
-            )(below, above, near, sums, shells)
-        )
-    later = [sent(accel, n_slab, n_dom, n_slab // 2, 0) for accel in accels]
+    accel = call(
+        functools.partial(side_kernel, (0, CELLS)),
+        0,
+        5,
+        shape(3, CELLS, LANES),
+        row_work(2) + [pltpu.VMEM((CELLS, 16, LANES), f32)] + pair_work(768),
+        name="side_slabs",
+        cost=pl.CostEstimate(flops=8_000_000_000, bytes_accessed=1_000_000, transcendentals=0),
+    )(below, above, near, sums, shells)
+    later = sent(accel, n_slab, n_dom, n_slab // 2, 0)
     out = shape(10, 1, CELLS, LANES)
-    state = call(kick_kernel, 0, 3, out, name="state")(planes, *accels)
-    part = call(kick_kernel, 0, 2, out, name="buddy")(early, later[0])
+    state = call(kick_kernel, 0, 2, out, name="state")(planes, accel)
+    part = call(place_kernel, 0, 1, out, name="buddy")(early)
     buddy = call(
-        functools.partial(last_kick_kernel, cut),
+        functools.partial(last_kick_kernel, 0),
         0,
         2,
         out,
-        [pltpu.VMEM((6, 1, CELLS - cut, LANES), f32), pltpu.SemaphoreType.DMA],
+        [pltpu.VMEM((6, 1, CELLS, LANES), f32), pltpu.SemaphoreType.DMA],
         name="buddy_end",
         n_any=1,
         n_same=1,
-    )(part, early, later[1])
+    )(part, early, later)
     return state, buddy
 
 

time: 44.1 us -> 41.3 us (0.937)
  starting transfers between devices: 13.4 us -> 10.6 us
  waiting for transfers between devices: 4.1 us -> 4.66 us
    ppermute x7 -> x6, starting transfers between devices: 13.4 us -> 10.6 us  [sent(): return lax.ppermute(value, ('slab', 'dom'), pairs)]
    ppermute x7 -> x6, waiting for transfers between devices: 4.1 us -> 4.66 us  [sent(): return lax.ppermute(value, ('slab', 'dom'), pairs)]
    pallas_call x5 -> x4, Pallas kernels: 13.1 us -> 12.7 us  [the longest x1 10.5 us: per_device(): call(functools.partial(side_kernel, (0, CELLS)), 0, 5, shape(3, CELLS, LA...]
    unnamed x6 -> x4, local copies, waits for them, and re-layouts: 0.89 us -> 0.89 us
  transfers between devices with their start and end apart: 7 -> 6, of which waited for: 2 -> 2; matrix products, arithmetic and copies ran while one was open for 0% -> 0% of each run, Pallas kernels for 41% -> 43%
where the time goes in v8:
time: 41.3 us; the launch traced here: 41.1 us
  Pallas kernels  23.6 us (57%)
  starting transfers between devices  10.6 us (26%)
  waiting for transfers between devices  4.66 us (11%)
  between operations  1.34 us (3%)
  local copies, waits for them, and re-layouts  0.89 us (2%)
    ppermute x6, starting transfers between devices, sent(): return lax.ppermute(value, ('slab', 'dom'), pairs)  10.6 us
    pallas_call x1, Pallas kernels, per_device(): call(functools.partial(side_kernel, (0, CELLS)), 0, 5, shape(3, CELLS, LA...  10.5 us
    pallas_call x1, Pallas kernels, per_device(): call(own_kernel, 0, 1, [shape(CELLS, FEATURES, LANES, dtype=bf16), shape(...  5.41 us
    pallas_call x1, Pallas kernels, per_device(): call(functools.partial(pack_kernel, n_dom), 2, 0, [shape(half, tall, LANE...  5.09 us
    ppermute x6, waiting for transfers between devices, sent(): return lax.ppermute(value, ('slab', 'dom'), pairs)  4.66 us
    unnamed x4, local copies, waits for them, and re-layouts  0.89 us
  transfers between devices with their start and end apart: 6, of which 2 were waited for; matrix products, arithmetic and copies ran while one was open for 0% of the time, Pallas kernels for 43%

profile of v8, /device:TPU:0, one launch (start us, length us, event | category | flops | bytes accessed | tf_op | source)
XLA Modules:
  0.0 41.1 jit_solution(1765701504363075935)
XLA Ops:
  1.3 5.1 %pack.1 = (f32[2,72,128]{2,1,0:T(8,128)}, f32[2,72,128]{2,1,0:T(8,128)}, f32[2,64,128]{2,1,0:T(8,128)}, f32[2,64,128]{2,1,0:T(8,128)}) custom-call(s32[1]{0:T(128)} %bitcast.me_ref, s32[1]{0:T(128)S(6)} %copy.9.count_ref, f32[3,6144]{1,0:T(4,128)} %pos_any.1, f32[3,6144]{1,0:T(4,128)} %vel_any.1, f32[1,6144]{1,0:T(1,128)} %bitcast.3, s32[1,6144]{1,0:T(1,128)} %bitcast.4), custom_call_target="tpu_custom_call" | custom-call | tf_op jit(solution)/shard_map/pack/pallas_call | solution.py:382
  6.4 3.0 %collective-permute-start = (f32[2,72,128]{2,1,0:T(8,128)}, f32[2,72,128]{2,1,0:T(8,128)S(1)}, u32[]{:S(2)}, u32[]{:S(2)}) collective-permute-start(f32[2,72,128]{2,1,0:T(8,128)} %get-tuple-element.9), channel_id=1, source_target_pairs={{0,1},{1,0},{2,3},{3,2},{4,5},{5,4},{6,7},{7,6},{8,9},{9,8},{10,11... | collective-permute-start | bytes 221192 | tf_op jit(solution)/shard_map/ppermute | solution.py:369
  9.4 0.1 collective-permute-start.1
  9.5 0.0 copy-start
  9.5 0.9 %copy-done = f32[2,72,128]{2,1,0:T(8,128)S(1)} copy-done((f32[2,72,128]{2,1,0:T(8,128)S(1)}, f32[2,72,128]{2,1,0:T(8,128)}, u32[]{:S(2)}) %copy-start) | copy-done | bytes 73752
  10.4 1.8 %collective-permute-done.refs_1_ = f32[2,72,128]{2,1,0:T(8,128)S(1)} collective-permute-done((f32[2,72,128]{2,1,0:T(8,128)}, f32[2,72,128]{2,1,0:T(8,128)S(1)}, u32[]{:S(2)}, u32[]{:S(2)}) %collective-permute-start) | collective-permute-done | bytes 73760 | tf_op jit(solution)/shard_map/ppermute | solution.py:369
  12.2 0.2 join.1.shells_ref
  12.3 0.0 copy-start.1
  12.4 0.1 collective-permute-start.2
  12.4 4.4 %collective-permute-start.3 = (f32[4,72,128]{2,1,0:T(8,128)S(1)}, f32[4,72,128]{2,1,0:T(8,128)S(1)}, u32[]{:S(2)}, u32[]{:S(2)}) collective-permute-start(f32[4,72,128]{2,1,0:T(8,128)S(1)} %join.1.shells_ref), channel_id=1, source_target_pairs={{0,30},{1,31},{2,0},{3,1},{4,2},{5,3},{6,4},{7,5},{8,6},{9,7},{10,... | collective-permute-start | bytes 442376 | tf_op jit(solution)/shard_map/ppermute | solution.py:369
  16.9 5.4 %own_slab.1 = (bf16[64,32,128]{2,1,0:T(8,128)(2,1)S(1)}, f32[64,16,128]{2,1,0:T(8,128)S(1)}) custom-call(f32[4,72,128]{2,1,0:T(8,128)S(1)} %join.1.shells_ref), custom_call_target="tpu_custom_call" | custom-call | flops 8000000000 | bytes 1000000 | tf_op jit(solution)/shard_map/own_slab/pallas_call | solution.py:432
  22.3 0.0 collective-permute-done.1.refs_1_
  22.3 0.0 copy-done.1
  22.3 0.2 speeds.1.planes_ref
  22.5 1.8 %collective-permute-start.4 = (f32[7,64,128]{2,1,0:T(8,128)S(1)}, f32[7,64,128]{2,1,0:T(8,128)S(1)}, u32[]{:S(2)}, u32[]{:S(2)}) collective-permute-start(f32[7,64,128]{2,1,0:T(8,128)S(1)} %speeds.1.planes_ref), channel_id=1, source_target_pairs={{0,16},{1,17},{2,18},{3,19},{4,20},{5,21},{6,22},{7,23},{8,24},{9,... | collective-permute-start | bytes 688136 | tf_op jit(solution)/shard_map/ppermute | solution.py:369
  24.3 0.0 collective-permute-done.2.up_ref
  24.3 0.0 collective-permute-done.3.down_ref
  24.3 10.5 %side_slabs.1.refs_0_ = f32[3,64,128]{2,1,0:T(8,128)S(1)} custom-call(f32[4,72,128]{2,1,0:T(8,128)S(1)} %collective-permute-done.2.up_ref, f32[4,72,128]{2,1,0:T(8,128)S(1)} %collective-permute-done.3.down_ref, bf16[64,32,128]{2,1,0:T(8,128)(2,1)S(1)} %get-tuple-element.12.near_ref, f32[64,16,128]{2,1,0:T(8,128)S(1)} %get-tuple-element.13.own_out, ...), custom_call_target="tpu_custom_call" | custom-call | flops 8000000000 | bytes 1000000 | tf_op jit(solution)/shard_map/side_slabs/pallas_call | solution.py:441
  34.8 1.2 %collective-permute-start.5 = (f32[3,64,128]{2,1,0:T(8,128)S(1)}, f32[3,64,128]{2,1,0:T(8,128)S(1)}, u32[]{:S(2)}, u32[]{:S(2)}) collective-permute-start(f32[3,64,128]{2,1,0:T(8,128)S(1)} %side_slabs.1.refs_0_), channel_id=1, source_target_pairs={{0,16},{1,17},{2,18},{3,19},{4,20},{5,21},{6,22},{7,23},{8,24},{9,... | collective-permute-start | bytes 294920 | tf_op jit(solution)/shard_map/ppermute | solution.py:369
  36.1 0.7 %state.1 = f32[10,1,64,128]{3,2,1,0:T(8,128)} custom-call(f32[7,64,128]{2,1,0:T(8,128)S(1)} %speeds.1.planes_ref, f32[3,64,128]{2,1,0:T(8,128)S(1)} %side_slabs.1.refs_0_), custom_call_target="tpu_custom_call" | custom-call | tf_op jit(solution)/shard_map/state/pallas_call | solution.py:452
  36.8 0.0 collective-permute-done.4.planes_ref
  36.8 0.7 %buddy.1._ = f32[10,1,64,128]{3,2,1,0:T(8,128)} custom-call(f32[7,64,128]{2,1,0:T(8,128)S(1)} %collective-permute-done.4.planes_ref), custom_call_target="tpu_custom_call" | custom-call | tf_op jit(solution)/shard_map/buddy/pallas_call | solution.py:453
  37.6 2.9 %collective-permute-done.5.accel_ref = f32[3,64,128]{2,1,0:T(8,128)S(1)} collective-permute-done((f32[3,64,128]{2,1,0:T(8,128)S(1)}, f32[3,64,128]{2,1,0:T(8,128)S(1)}, u32[]{:S(2)}, u32[]{:S(2)}) %collective-permute-start.5) | collective-permute-done | bytes 98336 | tf_op jit(solution)/shard_map/ppermute | solution.py:369
  40.4 0.7 %buddy_end.1 = f32[10,1,64,128]{3,2,1,0:T(8,128)} custom-call(f32[10,1,64,128]{3,2,1,0:T(8,128)} %buddy.1._, f32[7,64,128]{2,1,0:T(8,128)S(1)} %collective-permute-done.4.planes_ref, f32[3,64,128]{2,1,0:T(8,128)S(1)} %collective-permute-done.5.accel_ref), custom_call_target="tpu_custom_call", output_to_operand_aliasing={{}: (0, {})} | custom-call | tf_op jit(solution)/shard_map/buddy_end/pallas_call | solution.py:454
  (1 shorter events, 0.0 us)
Async XLA Ops:
  6.4 5.8 %collective-permute-start = (f32[2,72,128]{2,1,0:T(8,128)}, f32[2,72,128]{2,1,0:T(8,128)S(1)}, u32[]{:S(2)}, u32[]{:S(2)}) collective-permute-start(f32[2,72,128]{2,1,0:T(8,128)} %get-tuple-element.9), channel_id=1, source_target_pairs={{0,1},{1,0},{2,3},{3,2},{4,5},{5,4},{6,7},{7,6},{8,9},{9,8},{10,11... | collective-permute-start | bytes 221192 | tf_op jit(solution)/shard_map/ppermute | solution.py:369
  9.4 12.9 %collective-permute-start.1 = (f32[2,64,128]{2,1,0:T(8,128)}, f32[2,64,128]{2,1,0:T(8,128)S(1)}, u32[]{:S(2)}, u32[]{:S(2)}) collective-permute-start(f32[2,64,128]{2,1,0:T(8,128)} %get-tuple-element.11), channel_id=1, source_target_pairs={{0,1},{1,0},{2,3},{3,2},{4,5},{5,4},{6,7},{7,6},{8,9},{9,8},{10,11... | collective-permute-start | bytes 196616 | tf_op jit(solution)/shard_map/ppermute | solution.py:369
  9.5 0.9 %copy-start = (f32[2,72,128]{2,1,0:T(8,128)S(1)}, f32[2,72,128]{2,1,0:T(8,128)}, u32[]{:S(2)}) copy-start(f32[2,72,128]{2,1,0:T(8,128)} %get-tuple-element.8.source_ref) | copy-start | bytes 221188
  12.3 9.9 %copy-start.1 = (f32[2,64,128]{2,1,0:T(8,128)S(1)}, f32[2,64,128]{2,1,0:T(8,128)}, u32[]{:S(2)}) copy-start(f32[2,64,128]{2,1,0:T(8,128)} %get-tuple-element.10.refs_0_) | copy-start | bytes 196612
  12.4 11.9 %collective-permute-start.2 = (f32[4,72,128]{2,1,0:T(8,128)S(1)}, f32[4,72,128]{2,1,0:T(8,128)S(1)}, u32[]{:S(2)}, u32[]{:S(2)}) collective-permute-start(f32[4,72,128]{2,1,0:T(8,128)S(1)} %join.1.shells_ref), channel_id=1, source_target_pairs={{0,2},{1,3},{2,4},{3,5},{4,6},{5,7},{6,8},{7,9},{8,10},{9,11},{10,... | collective-permute-start | bytes 442376 | tf_op jit(solution)/shard_map/ppermute | solution.py:369
  12.4 11.8 %collective-permute-start.3 = (f32[4,72,128]{2,1,0:T(8,128)S(1)}, f32[4,72,128]{2,1,0:T(8,128)S(1)}, u32[]{:S(2)}, u32[]{:S(2)}) collective-permute-start(f32[4,72,128]{2,1,0:T(8,128)S(1)} %join.1.shells_ref), channel_id=1, source_target_pairs={{0,30},{1,31},{2,0},{3,1},{4,2},{5,3},{6,4},{7,5},{8,6},{9,7},{10,... | collective-permute-start | bytes 442376 | tf_op jit(solution)/shard_map/ppermute | solution.py:369
  22.5 14.3 %collective-permute-start.4 = (f32[7,64,128]{2,1,0:T(8,128)S(1)}, f32[7,64,128]{2,1,0:T(8,128)S(1)}, u32[]{:S(2)}, u32[]{:S(2)}) collective-permute-start(f32[7,64,128]{2,1,0:T(8,128)S(1)} %speeds.1.planes_ref), channel_id=1, source_target_pairs={{0,16},{1,17},{2,18},{3,19},{4,20},{5,21},{6,22},{7,23},{8,24},{9,... | collective-permute-start | bytes 688136 | tf_op jit(solution)/shard_map/ppermute | solution.py:369
  34.8 5.6 %collective-permute-start.5 = (f32[3,64,128]{2,1,0:T(8,128)S(1)}, f32[3,64,128]{2,1,0:T(8,128)S(1)}, u32[]{:S(2)}, u32[]{:S(2)}) collective-permute-start(f32[3,64,128]{2,1,0:T(8,128)S(1)} %side_slabs.1.refs_0_), channel_id=1, source_target_pairs={{0,16},{1,17},{2,18},{3,19},{4,20},{5,21},{6,22},{7,23},{8,24},{9,... | collective-permute-start | bytes 294920 | tf_op jit(solution)/shard_map/ppermute | solution.py:369

commit v9 on v8

--- a/solution.py
+++ b/solution.py
@@ -204,10 +204,9 @@
         put(sum_ref, [terms[0] + down(terms[1], 4), terms[2]])
 
 
-def pair_loop(cells, per, apart, far_rows, sum_rows, centre, out, dist, heavy):
+def pair_loop(cells, per, apart, wide, far_rows, sum_rows, centre, out, dist, heavy):
     blocks = [(k, n) for k in range(3) for n in range(len(far_rows))]
     tall = LANES * len(blocks)
-    wide = 3
     first, count = cells[0], cells[1] - cells[0]
 
     def beside(c, k):
@@ -289,7 +288,7 @@
 def own_kernel(shells_ref, near_out, out_ref, rows, far_rows, sum_rows, *work):
     build(shells_ref, (0, CELLS), rows, far_rows, sum_rows, near_out)
     pair_loop(
-        (0, CELLS), 2, 1, [far_rows], [sum_rows], near_out, out_ref, work[0:2], work[2:4]
+        (0, CELLS), 2, 1, 3, [far_rows], [sum_rows], near_out, out_ref, work[0:2], work[2:4]
     )
 
 
@@ -299,7 +298,7 @@
     rows, far_rows, sum_rows, out, work = refs[0], refs[1:3], refs[3:5], refs[5], refs[6:]
     for side, there_ref in enumerate((up_ref, down_ref)):
         build(there_ref, cells, rows, far_rows[side], sum_rows[side])
-    pair_loop(cells, 1, 2, far_rows, sum_rows, near_ref, out, work[0:2], work[2:4])
+    pair_loop(cells, 1, 6, 6, far_rows, sum_rows, near_ref, out, work[0:2], work[2:4])
     both = out[...] + own_out[low:high]
     both = (both[:, :8] + both[:, 8:]).reshape(count * 8, LANES)
     rows[: count * 8] = both + pltpu.roll(both, count * 8 - 4, 0)
@@ -419,6 +418,8 @@
     below, above = (sent(shells, n_slab, n_dom, side, 0) for side in (1, -1))
     early = sent(planes, n_slab, n_dom, n_slab // 2, 0)
 
+    ready, _ = lax.optimization_barrier((shells, planes))
+
     def pair_work(size):
         return [pltpu.VMEM((size, LANES), f32)] * 4
 
@@ -437,7 +438,7 @@
         row_work(1) + pair_work(768),
         name="own_slab",
         cost=pl.CostEstimate(flops=8_000_000_000, bytes_accessed=1_000_000, transcendentals=0),
-    )(shells)
+    )(ready)
     accel = call(
         functools.partial(side_kernel, (0, CELLS)),
         0,

time: 41.3 us -> 40.5 us (0.981)
  starting transfers between devices: 10.6 us -> 12.4 us
  waiting for transfers between devices: 4.66 us -> 2.91 us
  Pallas kernels: 23.6 us -> 22.8 us
    ppermute x6, starting transfers between devices: 10.6 us -> 12.4 us  [sent(): return lax.ppermute(value, ('slab', 'dom'), pairs)]
    ppermute x6, waiting for transfers between devices: 4.66 us -> 2.91 us  [sent(): return lax.ppermute(value, ('slab', 'dom'), pairs)]
    pallas_call x1, Pallas kernels: 10.5 us -> 9.76 us  [per_device(): call(functools.partial(side_kernel, (0, CELLS)), 0, 5, shape(3, CELLS, LA...]
  transfers between devices with their start and end apart: 6 -> 6, of which waited for: 2 -> 2; matrix products, arithmetic and copies ran while one was open for 0% -> 0% of each run, Pallas kernels for 43% -> 42%
where the time goes in v9:
time: 40.5 us; the launch traced here: 40.4 us
  Pallas kernels  22.8 us (56%)
  starting transfers between devices  12.4 us (31%)
  waiting for transfers between devices  2.91 us (7%)
  between operations  1.34 us (3%)
  local copies, waits for them, and re-layouts  0.89 us (2%)
    ppermute x6, starting transfers between devices, sent(): return lax.ppermute(value, ('slab', 'dom'), pairs)  12.4 us
    pallas_call x1, Pallas kernels, per_device(): call(functools.partial(side_kernel, (0, CELLS)), 0, 5, shape(3, CELLS, LA...  9.76 us
    pallas_call x1, Pallas kernels, per_device(): call(own_kernel, 0, 1, [shape(CELLS, FEATURES, LANES, dtype=bf16), shape(...  5.4 us
    pallas_call x1, Pallas kernels, per_device(): call(functools.partial(pack_kernel, n_dom), 2, 0, [shape(half, tall, LANE...  5.09 us
    ppermute x6, waiting for transfers between devices, sent(): return lax.ppermute(value, ('slab', 'dom'), pairs)  2.91 us
    unnamed x4, local copies, waits for them, and re-layouts  0.89 us
  transfers between devices with their start and end apart: 6, of which 2 were waited for; matrix products, arithmetic and copies ran while one was open for 0% of the time, Pallas kernels for 42%

profile of v9, /device:TPU:0, one launch (start us, length us, event | category | flops | bytes accessed | tf_op | source)
XLA Modules:
  0.0 40.4 jit_solution(2771958965037710425)
XLA Ops:
  1.3 5.1 %pack.1 = (f32[2,72,128]{2,1,0:T(8,128)}, f32[2,72,128]{2,1,0:T(8,128)}, f32[2,64,128]{2,1,0:T(8,128)}, f32[2,64,128]{2,1,0:T(8,128)}) custom-call(s32[1]{0:T(128)} %bitcast.me_ref, s32[1]{0:T(128)S(6)} %copy.9.count_ref, f32[3,6144]{1,0:T(4,128)} %pos_any.1, f32[3,6144]{1,0:T(4,128)} %vel_any.1, f32[1,6144]{1,0:T(1,128)} %bitcast.3, s32[1,6144]{1,0:T(1,128)} %bitcast.4), custom_call_target="tpu_custom_call" | custom-call | tf_op jit(solution)/shard_map/pack/pallas_call | solution.py:381
  6.4 3.0 %collective-permute-start = (f32[2,72,128]{2,1,0:T(8,128)}, f32[2,72,128]{2,1,0:T(8,128)S(1)}, u32[]{:S(2)}, u32[]{:S(2)}) collective-permute-start(f32[2,72,128]{2,1,0:T(8,128)} %get-tuple-element.10), channel_id=1, source_target_pairs={{0,1},{1,0},{2,3},{3,2},{4,5},{5,4},{6,7},{7,6},{8,9},{9,8},{10,11... | collective-permute-start | bytes 221192 | tf_op jit(solution)/shard_map/ppermute | solution.py:368
  9.4 0.1 collective-permute-start.1
  9.5 0.0 copy-start
  9.5 0.9 %copy-done = f32[2,72,128]{2,1,0:T(8,128)S(1)} copy-done((f32[2,72,128]{2,1,0:T(8,128)S(1)}, f32[2,72,128]{2,1,0:T(8,128)}, u32[]{:S(2)}) %copy-start) | copy-done | bytes 73752
  10.4 0.0 copy-start.1
  10.4 1.8 %collective-permute-done.refs_1_ = f32[2,72,128]{2,1,0:T(8,128)S(1)} collective-permute-done((f32[2,72,128]{2,1,0:T(8,128)}, f32[2,72,128]{2,1,0:T(8,128)S(1)}, u32[]{:S(2)}, u32[]{:S(2)}) %collective-permute-start) | collective-permute-done | bytes 73760 | tf_op jit(solution)/shard_map/ppermute | solution.py:368
  12.2 0.2 join.1.shells_ref
  12.3 0.1 collective-permute-start.2
  12.4 4.4 %collective-permute-start.3 = (f32[4,72,128]{2,1,0:T(8,128)S(1)}, f32[4,72,128]{2,1,0:T(8,128)S(1)}, u32[]{:S(2)}, u32[]{:S(2)}) collective-permute-start(f32[4,72,128]{2,1,0:T(8,128)S(1)} %join.1.shells_ref), channel_id=1, source_target_pairs={{0,30},{1,31},{2,0},{3,1},{4,2},{5,3},{6,4},{7,5},{8,6},{9,7},{10,... | collective-permute-start | bytes 442376 | tf_op jit(solution)/shard_map/ppermute | solution.py:368
  16.8 0.0 collective-permute-done.1.refs_1_
  16.8 0.0 copy-done.1
  16.9 0.2 speeds.1.planes_ref
  17.0 1.8 %collective-permute-start.4 = (f32[7,64,128]{2,1,0:T(8,128)S(1)}, f32[7,64,128]{2,1,0:T(8,128)S(1)}, u32[]{:S(2)}, u32[]{:S(2)}) collective-permute-start(f32[7,64,128]{2,1,0:T(8,128)S(1)} %speeds.1.planes_ref), channel_id=1, source_target_pairs={{0,16},{1,17},{2,18},{3,19},{4,20},{5,21},{6,22},{7,23},{8,24},{9,... | collective-permute-start | bytes 688136 | tf_op jit(solution)/shard_map/ppermute | solution.py:368
  18.8 5.4 %own_slab.1 = (bf16[64,32,128]{2,1,0:T(8,128)(2,1)S(1)}, f32[64,16,128]{2,1,0:T(8,128)S(1)}) custom-call(f32[4,72,128]{2,1,0:T(8,128)S(1)} %join.1.shells_ref), custom_call_target="tpu_custom_call" | custom-call | flops 8000000000 | bytes 1000000 | tf_op jit(solution)/shard_map/own_slab/pallas_call | solution.py:433
  24.2 0.0 collective-permute-done.2.up_ref
  24.2 0.0 collective-permute-done.3.down_ref
  24.2 9.8 %side_slabs.1.refs_0_ = f32[3,64,128]{2,1,0:T(8,128)S(1)} custom-call(f32[4,72,128]{2,1,0:T(8,128)S(1)} %collective-permute-done.2.up_ref, f32[4,72,128]{2,1,0:T(8,128)S(1)} %collective-permute-done.3.down_ref, bf16[64,32,128]{2,1,0:T(8,128)(2,1)S(1)} %get-tuple-element.14.near_ref, f32[64,16,128]{2,1,0:T(8,128)S(1)} %get-tuple-element.15.own_out, ...), custom_call_target="tpu_custom_call" | custom-call | flops 8000000000 | bytes 1000000 | tf_op jit(solution)/shard_map/side_slabs/pallas_call | solution.py:442
  34.0 3.0 %collective-permute-start.5 = (f32[3,64,128]{2,1,0:T(8,128)S(1)}, f32[3,64,128]{2,1,0:T(8,128)S(1)}, u32[]{:S(2)}, u32[]{:S(2)}) collective-permute-start(f32[3,64,128]{2,1,0:T(8,128)S(1)} %side_slabs.1.refs_0_), channel_id=1, source_target_pairs={{0,16},{1,17},{2,18},{3,19},{4,20},{5,21},{6,22},{7,23},{8,24},{9,... | collective-permute-start | bytes 294920 | tf_op jit(solution)/shard_map/ppermute | solution.py:368
  37.0 0.7 %state.1 = f32[10,1,64,128]{3,2,1,0:T(8,128)} custom-call(f32[7,64,128]{2,1,0:T(8,128)S(1)} %speeds.1.planes_ref, f32[3,64,128]{2,1,0:T(8,128)S(1)} %side_slabs.1.refs_0_), custom_call_target="tpu_custom_call" | custom-call | tf_op jit(solution)/shard_map/state/pallas_call | solution.py:453
  37.8 0.0 collective-permute-done.4.planes_ref
  37.8 0.7 %buddy.1._ = f32[10,1,64,128]{3,2,1,0:T(8,128)} custom-call(f32[7,64,128]{2,1,0:T(8,128)S(1)} %collective-permute-done.4.planes_ref), custom_call_target="tpu_custom_call" | custom-call | tf_op jit(solution)/shard_map/buddy/pallas_call | solution.py:454
  38.5 1.1 %collective-permute-done.5.accel_ref = f32[3,64,128]{2,1,0:T(8,128)S(1)} collective-permute-done((f32[3,64,128]{2,1,0:T(8,128)S(1)}, f32[3,64,128]{2,1,0:T(8,128)S(1)}, u32[]{:S(2)}, u32[]{:S(2)}) %collective-permute-start.5) | collective-permute-done | bytes 98336 | tf_op jit(solution)/shard_map/ppermute | solution.py:368
  39.7 0.7 %buddy_end.1 = f32[10,1,64,128]{3,2,1,0:T(8,128)} custom-call(f32[10,1,64,128]{3,2,1,0:T(8,128)} %buddy.1._, f32[7,64,128]{2,1,0:T(8,128)S(1)} %collective-permute-done.4.planes_ref, f32[3,64,128]{2,1,0:T(8,128)S(1)} %collective-permute-done.5.accel_ref), custom_call_target="tpu_custom_call", output_to_operand_aliasing={{}: (0, {})} | custom-call | tf_op jit(solution)/shard_map/buddy_end/pallas_call | solution.py:455
  (1 shorter events, 0.0 us)
Async XLA Ops:
  6.4 5.8 %collective-permute-start = (f32[2,72,128]{2,1,0:T(8,128)}, f32[2,72,128]{2,1,0:T(8,128)S(1)}, u32[]{:S(2)}, u32[]{:S(2)}) collective-permute-start(f32[2,72,128]{2,1,0:T(8,128)} %get-tuple-element.10), channel_id=1, source_target_pairs={{0,1},{1,0},{2,3},{3,2},{4,5},{5,4},{6,7},{7,6},{8,9},{9,8},{10,11... | collective-permute-start | bytes 221192 | tf_op jit(solution)/shard_map/ppermute | solution.py:368
  9.4 7.4 %collective-permute-start.1 = (f32[2,64,128]{2,1,0:T(8,128)}, f32[2,64,128]{2,1,0:T(8,128)S(1)}, u32[]{:S(2)}, u32[]{:S(2)}) collective-permute-start(f32[2,64,128]{2,1,0:T(8,128)} %get-tuple-element.12), channel_id=1, source_target_pairs={{0,1},{1,0},{2,3},{3,2},{4,5},{5,4},{6,7},{7,6},{8,9},{9,8},{10,11... | collective-permute-start | bytes 196616 | tf_op jit(solution)/shard_map/ppermute | solution.py:368
  9.5 0.9 %copy-start = (f32[2,72,128]{2,1,0:T(8,128)S(1)}, f32[2,72,128]{2,1,0:T(8,128)}, u32[]{:S(2)}) copy-start(f32[2,72,128]{2,1,0:T(8,128)} %get-tuple-element.9.source_ref) | copy-start | bytes 221188
  10.4 6.5 %copy-start.1 = (f32[2,64,128]{2,1,0:T(8,128)S(1)}, f32[2,64,128]{2,1,0:T(8,128)}, u32[]{:S(2)}) copy-start(f32[2,64,128]{2,1,0:T(8,128)} %get-tuple-element.11.refs_0_) | copy-start | bytes 196612
  12.3 11.9 %collective-permute-start.2 = (f32[4,72,128]{2,1,0:T(8,128)S(1)}, f32[4,72,128]{2,1,0:T(8,128)S(1)}, u32[]{:S(2)}, u32[]{:S(2)}) collective-permute-start(f32[4,72,128]{2,1,0:T(8,128)S(1)} %join.1.shells_ref), channel_id=1, source_target_pairs={{0,2},{1,3},{2,4},{3,5},{4,6},{5,7},{6,8},{7,9},{8,10},{9,11},{10,... | collective-permute-start | bytes 442376 | tf_op jit(solution)/shard_map/ppermute | solution.py:368
  12.4 11.8 %collective-permute-start.3 = (f32[4,72,128]{2,1,0:T(8,128)S(1)}, f32[4,72,128]{2,1,0:T(8,128)S(1)}, u32[]{:S(2)}, u32[]{:S(2)}) collective-permute-start(f32[4,72,128]{2,1,0:T(8,128)S(1)} %join.1.shells_ref), channel_id=1, source_target_pairs={{0,30},{1,31},{2,0},{3,1},{4,2},{5,3},{6,4},{7,5},{8,6},{9,7},{10,... | collective-permute-start | bytes 442376 | tf_op jit(solution)/shard_map/ppermute | solution.py:368
  17.0 20.8 %collective-permute-start.4 = (f32[7,64,128]{2,1,0:T(8,128)S(1)}, f32[7,64,128]{2,1,0:T(8,128)S(1)}, u32[]{:S(2)}, u32[]{:S(2)}) collective-permute-start(f32[7,64,128]{2,1,0:T(8,128)S(1)} %speeds.1.planes_ref), channel_id=1, source_target_pairs={{0,16},{1,17},{2,18},{3,19},{4,20},{5,21},{6,22},{7,23},{8,24},{9,... | collective-permute-start | bytes 688136 | tf_op jit(solution)/shard_map/ppermute | solution.py:368
  34.0 5.6 %collective-permute-start.5 = (f32[3,64,128]{2,1,0:T(8,128)S(1)}, f32[3,64,128]{2,1,0:T(8,128)S(1)}, u32[]{:S(2)}, u32[]{:S(2)}) collective-permute-start(f32[3,64,128]{2,1,0:T(8,128)S(1)} %side_slabs.1.refs_0_), channel_id=1, source_target_pairs={{0,16},{1,17},{2,18},{3,19},{4,20},{5,21},{6,22},{7,23},{8,24},{9,... | collective-permute-start | bytes 294920 | tf_op jit(solution)/shard_map/ppermute | solution.py:368

commit v10 on v9

--- a/solution.py
+++ b/solution.py
@@ -285,10 +285,13 @@
         planes_ref[4 + comp] = pltpu.roll(merged(pieces, comp, n_dom), turn, 1)
 
 
-def own_kernel(shells_ref, near_out, out_ref, rows, far_rows, sum_rows, *work):
-    build(shells_ref, (0, CELLS), rows, far_rows, sum_rows, near_out)
+def own_rows_kernel(shells_ref, near_ref, far_ref, sum_ref, rows):
+    build(shells_ref, (0, CELLS), rows, far_ref, sum_ref, near_ref)
+
+
+def own_kernel(near_ref, far_ref, sum_ref, out_ref, *work):
     pair_loop(
-        (0, CELLS), 2, 1, 3, [far_rows], [sum_rows], near_out, out_ref, work[0:2], work[2:4]
+        (0, CELLS), 2, 1, 3, [far_ref], [sum_ref], near_ref, out_ref, work[0:2], work[2:4]
     )
 
 
@@ -408,17 +411,31 @@
     shells = call(
         functools.partial(join_kernel, n_dom), 1, n_dom, shape(4, tall, LANES), name="join"
     )(me, *places)
+    below, above = (sent(shells, n_slab, n_dom, side, 0) for side in (1, -1))
+    near, far_rows, sum_rows = call(
+        own_rows_kernel,
+        0,
+        1,
+        [
+            shape(CELLS, FEATURES, LANES, dtype=bf16),
+            shape(tall, FEATURES, LANES, dtype=bf16),
+            shape(tall, 16, LANES, dtype=bf16),
+        ],
+        [pltpu.VMEM((tall * 8, LANES), f32)],
+        name="own_rows",
+        cost=pl.CostEstimate(flops=1_000_000_000, bytes_accessed=1_000_000, transcendentals=0),
+    )(shells)
+    kept, near = lax.optimization_barrier((shells, near))
     planes = call(
         functools.partial(speeds_kernel, n_dom),
         1,
         1 + n_dom,
         shape(7, CELLS, LANES),
         name="speeds",
-    )(me, shells, *speeds)
-    below, above = (sent(shells, n_slab, n_dom, side, 0) for side in (1, -1))
+    )(me, kept, *speeds)
     early = sent(planes, n_slab, n_dom, n_slab // 2, 0)
 
-    ready, _ = lax.optimization_barrier((shells, planes))
+    far_rows, _ = lax.optimization_barrier((far_rows, planes))
 
     def pair_work(size):
         return [pltpu.VMEM((size, LANES), f32)] * 4
@@ -430,15 +447,15 @@
             + [pltpu.VMEM((tall, 16, LANES), bf16)] * copies
         )
 
-    near, sums = call(
+    sums = call(
         own_kernel,
         0,
-        1,
-        [shape(CELLS, FEATURES, LANES, dtype=bf16), shape(CELLS, 16, LANES)],
-        row_work(1) + pair_work(768),
+        3,
+        shape(CELLS, 16, LANES),
+        pair_work(768),
         name="own_slab",
         cost=pl.CostEstimate(flops=8_000_000_000, bytes_accessed=1_000_000, transcendentals=0),
-    )(ready)
+    )(near, far_rows, sum_rows)
     accel = call(
         functools.partial(side_kernel, (0, CELLS)),
         0,

time: 40.5 us -> 42.1 us (1.040)
  waiting for transfers between devices: 2.91 us -> 3.96 us
    ppermute x6, waiting for transfers between devices: 2.91 us -> 3.96 us  [sent(): return lax.ppermute(value, ('slab', 'dom'), pairs)]
    pallas_call x1 -> x2, Pallas kernels: 5.4 us -> 5.6 us  [the longest x1 4.8 us: per_device(): call(own_kernel, 0, 3, shape(CELLS, 16, LANES), pair_work(768), name='own...]
  transfers between devices with their start and end apart: 6 -> 6, of which waited for: 2 -> 2; matrix products, arithmetic and copies ran while one was open for 0% -> 0% of each run, Pallas kernels for 42% -> 41%
where the time goes in v10:
time: 42.1 us; the launch traced here: 41.9 us
  Pallas kernels  23 us (55%)
  starting transfers between devices  12.7 us (30%)
  waiting for transfers between devices  3.96 us (9%)
  between operations  1.36 us (3%)
  local copies, waits for them, and re-layouts  0.89 us (2%)
    ppermute x6, starting transfers between devices, sent(): return lax.ppermute(value, ('slab', 'dom'), pairs)  12.7 us
    pallas_call x1, Pallas kernels, per_device(): call(functools.partial(side_kernel, (0, CELLS)), 0, 5, shape(3, CELLS, LA...  9.8 us
    pallas_call x1, Pallas kernels, per_device(): call(functools.partial(pack_kernel, n_dom), 2, 0, [shape(half, tall, LANE...  5.09 us
    pallas_call x1, Pallas kernels, per_device(): call(own_kernel, 0, 3, shape(CELLS, 16, LANES), pair_work(768), name='own...  4.8 us
    ppermute x6, waiting for transfers between devices, sent(): return lax.ppermute(value, ('slab', 'dom'), pairs)  3.96 us
    unnamed x4, local copies, waits for them, and re-layouts  0.89 us
  transfers between devices with their start and end apart: 6, of which 2 were waited for; matrix products, arithmetic and copies ran while one was open for 0% of the time, Pallas kernels for 41%

profile of v10, /device:TPU:0, one launch (start us, length us, event | category | flops | bytes accessed | tf_op | source)
XLA Modules:
  0.0 41.9 jit_solution(9997135749495483292)
XLA Ops:
  1.3 5.1 %pack.1 = (f32[2,72,128]{2,1,0:T(8,128)}, f32[2,72,128]{2,1,0:T(8,128)}, f32[2,64,128]{2,1,0:T(8,128)}, f32[2,64,128]{2,1,0:T(8,128)}) custom-call(s32[1]{0:T(128)} %bitcast.me_ref, s32[1]{0:T(128)S(6)} %copy.9.count_ref, f32[3,6144]{1,0:T(4,128)} %pos_any.1, f32[3,6144]{1,0:T(4,128)} %vel_any.1, f32[1,6144]{1,0:T(1,128)} %bitcast.3, s32[1,6144]{1,0:T(1,128)} %bitcast.4), custom_call_target="tpu_custom_call" | custom-call | tf_op jit(solution)/shard_map/pack/pallas_call | solution.py:384
  6.4 3.0 %collective-permute-start = (f32[2,72,128]{2,1,0:T(8,128)}, f32[2,72,128]{2,1,0:T(8,128)S(1)}, u32[]{:S(2)}, u32[]{:S(2)}) collective-permute-start(f32[2,72,128]{2,1,0:T(8,128)} %get-tuple-element.13), channel_id=1, source_target_pairs={{0,1},{1,0},{2,3},{3,2},{4,5},{5,4},{6,7},{7,6},{8,9},{9,8},{10,11... | collective-permute-start | bytes 221192 | tf_op jit(solution)/shard_map/ppermute | solution.py:371
  9.4 0.1 collective-permute-start.1
  9.5 0.9 %copy-done = f32[2,72,128]{2,1,0:T(8,128)S(1)} copy-done((f32[2,72,128]{2,1,0:T(8,128)S(1)}, f32[2,72,128]{2,1,0:T(8,128)}, u32[]{:S(2)}) %copy-start) | copy-done | bytes 73752
  10.4 1.8 %collective-permute-done.refs_1_ = f32[2,72,128]{2,1,0:T(8,128)S(1)} collective-permute-done((f32[2,72,128]{2,1,0:T(8,128)}, f32[2,72,128]{2,1,0:T(8,128)S(1)}, u32[]{:S(2)}, u32[]{:S(2)}) %collective-permute-start) | collective-permute-done | bytes 73760 | tf_op jit(solution)/shard_map/ppermute | solution.py:371
  12.2 0.2 join.1.shells_ref
  12.3 0.0 copy-start.1
  12.4 0.1 collective-permute-start.2
  12.4 4.4 %collective-permute-start.3 = (f32[4,72,128]{2,1,0:T(8,128)S(1)}, f32[4,72,128]{2,1,0:T(8,128)S(1)}, u32[]{:S(2)}, u32[]{:S(2)}) collective-permute-start(f32[4,72,128]{2,1,0:T(8,128)S(1)} %join.1.shells_ref), channel_id=1, source_target_pairs={{0,30},{1,31},{2,0},{3,1},{4,2},{5,3},{6,4},{7,5},{8,6},{9,7},{10,... | collective-permute-start | bytes 442376 | tf_op jit(solution)/shard_map/ppermute | solution.py:371
  16.9 0.8 %own_rows.1 = (bf16[64,32,128]{2,1,0:T(8,128)(2,1)S(1)}, bf16[72,32,128]{2,1,0:T(8,128)(2,1)S(1)}, bf16[72,16,128]{2,1,0:T(8,128)(2,1)S(1)}) custom-call(f32[4,72,128]{2,1,0:T(8,128)S(1)} %join.1.shells_ref), custom_call_target="tpu_custom_call" | custom-call | flops 1000000000 | bytes 1000000 | tf_op jit(solution)/shard_map/own_rows/pallas_call | solution.py:415
  17.7 0.0 collective-permute-done.1.refs_1_
  17.7 0.0 copy-done.1
  17.7 0.2 speeds.1.planes_ref
  17.8 1.8 %collective-permute-start.4 = (f32[7,64,128]{2,1,0:T(8,128)S(1)}, f32[7,64,128]{2,1,0:T(8,128)S(1)}, u32[]{:S(2)}, u32[]{:S(2)}) collective-permute-start(f32[7,64,128]{2,1,0:T(8,128)S(1)} %speeds.1.planes_ref), channel_id=1, source_target_pairs={{0,16},{1,17},{2,18},{3,19},{4,20},{5,21},{6,22},{7,23},{8,24},{9,... | collective-permute-start | bytes 688136 | tf_op jit(solution)/shard_map/ppermute | solution.py:371
  19.7 4.8 %own_slab.1.own_out = f32[64,16,128]{2,1,0:T(8,128)S(1)} custom-call(bf16[64,32,128]{2,1,0:T(8,128)(2,1)S(1)} %get-tuple-element.18.near_ref, bf16[72,32,128]{2,1,0:T(8,128)(2,1)S(1)} %get-tuple-element.20.far_ref, bf16[72,16,128]{2,1,0:T(8,128)(2,1)S(1)} %get-tuple-element.21.sum_ref), custom_call_target="tpu_custom_call" | custom-call | flops 8000000000 | bytes 1000000 | tf_op jit(solution)/shard_map/own_slab/pallas_call | solution.py:450
  24.5 0.0 collective-permute-done.2.up_ref
  24.5 0.0 collective-permute-done.3.down_ref
  24.5 9.8 %side_slabs.1.refs_0_ = f32[3,64,128]{2,1,0:T(8,128)S(1)} custom-call(f32[4,72,128]{2,1,0:T(8,128)S(1)} %collective-permute-done.2.up_ref, f32[4,72,128]{2,1,0:T(8,128)S(1)} %collective-permute-done.3.down_ref, bf16[64,32,128]{2,1,0:T(8,128)(2,1)S(1)} %get-tuple-element.18.near_ref, f32[64,16,128]{2,1,0:T(8,128)S(1)} %own_slab.1.own_out, ...), custom_call_target="tpu_custom_call" | custom-call | flops 8000000000 | bytes 1000000 | tf_op jit(solution)/shard_map/side_slabs/pallas_call | solution.py:459
  34.3 3.3 %collective-permute-start.5 = (f32[3,64,128]{2,1,0:T(8,128)S(1)}, f32[3,64,128]{2,1,0:T(8,128)S(1)}, u32[]{:S(2)}, u32[]{:S(2)}) collective-permute-start(f32[3,64,128]{2,1,0:T(8,128)S(1)} %side_slabs.1.refs_0_), channel_id=1, source_target_pairs={{0,16},{1,17},{2,18},{3,19},{4,20},{5,21},{6,22},{7,23},{8,24},{9,... | collective-permute-start | bytes 294920 | tf_op jit(solution)/shard_map/ppermute | solution.py:371
  37.6 0.7 %state.1 = f32[10,1,64,128]{3,2,1,0:T(8,128)} custom-call(f32[7,64,128]{2,1,0:T(8,128)S(1)} %speeds.1.planes_ref, f32[3,64,128]{2,1,0:T(8,128)S(1)} %side_slabs.1.refs_0_), custom_call_target="tpu_custom_call" | custom-call | tf_op jit(solution)/shard_map/state/pallas_call | solution.py:470
  38.3 0.0 collective-permute-done.4.planes_ref
  38.3 0.7 %buddy.1._ = f32[10,1,64,128]{3,2,1,0:T(8,128)} custom-call(f32[7,64,128]{2,1,0:T(8,128)S(1)} %collective-permute-done.4.planes_ref), custom_call_target="tpu_custom_call" | custom-call | tf_op jit(solution)/shard_map/buddy/pallas_call | solution.py:471
  39.1 2.2 %collective-permute-done.5.accel_ref = f32[3,64,128]{2,1,0:T(8,128)S(1)} collective-permute-done((f32[3,64,128]{2,1,0:T(8,128)S(1)}, f32[3,64,128]{2,1,0:T(8,128)S(1)}, u32[]{:S(2)}, u32[]{:S(2)}) %collective-permute-start.5) | collective-permute-done | bytes 98336 | tf_op jit(solution)/shard_map/ppermute | solution.py:371
  41.2 0.7 %buddy_end.1 = f32[10,1,64,128]{3,2,1,0:T(8,128)} custom-call(f32[10,1,64,128]{3,2,1,0:T(8,128)} %buddy.1._, f32[7,64,128]{2,1,0:T(8,128)S(1)} %collective-permute-done.4.planes_ref, f32[3,64,128]{2,1,0:T(8,128)S(1)} %collective-permute-done.5.accel_ref), custom_call_target="tpu_custom_call", output_to_operand_aliasing={{}: (0, {})} | custom-call | tf_op jit(solution)/shard_map/buddy_end/pallas_call | solution.py:472
  (2 shorter events, 0.0 us)
Async XLA Ops:
  6.4 5.8 %collective-permute-start = (f32[2,72,128]{2,1,0:T(8,128)}, f32[2,72,128]{2,1,0:T(8,128)S(1)}, u32[]{:S(2)}, u32[]{:S(2)}) collective-permute-start(f32[2,72,128]{2,1,0:T(8,128)} %get-tuple-element.13), channel_id=1, source_target_pairs={{0,1},{1,0},{2,3},{3,2},{4,5},{5,4},{6,7},{7,6},{8,9},{9,8},{10,11... | collective-permute-start | bytes 221192 | tf_op jit(solution)/shard_map/ppermute | solution.py:371
  9.4 8.3 %collective-permute-start.1 = (f32[2,64,128]{2,1,0:T(8,128)}, f32[2,64,128]{2,1,0:T(8,128)S(1)}, u32[]{:S(2)}, u32[]{:S(2)}) collective-permute-start(f32[2,64,128]{2,1,0:T(8,128)} %get-tuple-element.17), channel_id=1, source_target_pairs={{0,1},{1,0},{2,3},{3,2},{4,5},{5,4},{6,7},{7,6},{8,9},{9,8},{10,11... | collective-permute-start | bytes 196616 | tf_op jit(solution)/shard_map/ppermute | solution.py:371
  9.5 0.9 %copy-start = (f32[2,72,128]{2,1,0:T(8,128)S(1)}, f32[2,72,128]{2,1,0:T(8,128)}, u32[]{:S(2)}) copy-start(f32[2,72,128]{2,1,0:T(8,128)} %get-tuple-element.12.source_ref) | copy-start | bytes 221188
  12.3 5.3 %copy-start.1 = (f32[2,64,128]{2,1,0:T(8,128)S(1)}, f32[2,64,128]{2,1,0:T(8,128)}, u32[]{:S(2)}) copy-start(f32[2,64,128]{2,1,0:T(8,128)} %get-tuple-element.16.refs_0_) | copy-start | bytes 196612
  12.4 12.1 %collective-permute-start.2 = (f32[4,72,128]{2,1,0:T(8,128)S(1)}, f32[4,72,128]{2,1,0:T(8,128)S(1)}, u32[]{:S(2)}, u32[]{:S(2)}) collective-permute-start(f32[4,72,128]{2,1,0:T(8,128)S(1)} %join.1.shells_ref), channel_id=1, source_target_pairs={{0,2},{1,3},{2,4},{3,5},{4,6},{5,7},{6,8},{7,9},{8,10},{9,11},{10,... | collective-permute-start | bytes 442376 | tf_op jit(solution)/shard_map/ppermute | solution.py:371
  12.4 12.0 %collective-permute-start.3 = (f32[4,72,128]{2,1,0:T(8,128)S(1)}, f32[4,72,128]{2,1,0:T(8,128)S(1)}, u32[]{:S(2)}, u32[]{:S(2)}) collective-permute-start(f32[4,72,128]{2,1,0:T(8,128)S(1)} %join.1.shells_ref), channel_id=1, source_target_pairs={{0,30},{1,31},{2,0},{3,1},{4,2},{5,3},{6,4},{7,5},{8,6},{9,7},{10,... | collective-permute-start | bytes 442376 | tf_op jit(solution)/shard_map/ppermute | solution.py:371
  17.8 20.5 %collective-permute-start.4 = (f32[7,64,128]{2,1,0:T(8,128)S(1)}, f32[7,64,128]{2,1,0:T(8,128)S(1)}, u32[]{:S(2)}, u32[]{:S(2)}) collective-permute-start(f32[7,64,128]{2,1,0:T(8,128)S(1)} %speeds.1.planes_ref), channel_id=1, source_target_pairs={{0,16},{1,17},{2,18},{3,19},{4,20},{5,21},{6,22},{7,23},{8,24},{9,... | collective-permute-start | bytes 688136 | tf_op jit(solution)/shard_map/ppermute | solution.py:371
  34.3 6.9 %collective-permute-start.5 = (f32[3,64,128]{2,1,0:T(8,128)S(1)}, f32[3,64,128]{2,1,0:T(8,128)S(1)}, u32[]{:S(2)}, u32[]{:S(2)}) collective-permute-start(f32[3,64,128]{2,1,0:T(8,128)S(1)} %side_slabs.1.refs_0_), channel_id=1, source_target_pairs={{0,16},{1,17},{2,18},{3,19},{4,20},{5,21},{6,22},{7,23},{8,24},{9,... | collective-permute-start | bytes 294920 | tf_op jit(solution)/shard_map/ppermute | solution.py:371

commit v11 on v10

--- a/solution.py
+++ b/solution.py
@@ -289,20 +289,20 @@
     build(shells_ref, (0, CELLS), rows, far_ref, sum_ref, near_ref)
 
 
-def own_kernel(near_ref, far_ref, sum_ref, out_ref, *work):
+def own_kernel(cells, near_ref, far_ref, sum_ref, out_ref, *work):
     pair_loop(
-        (0, CELLS), 2, 1, 3, [far_ref], [sum_ref], near_ref, out_ref, work[0:2], work[2:4]
+        cells, 2, 1, 3, [far_ref], [sum_ref], near_ref, out_ref, work[0:2], work[2:4]
     )
 
 
-def side_kernel(cells, up_ref, down_ref, near_ref, own_out, shells_ref, accel_ref, *refs):
+def side_kernel(cells, up_ref, down_ref, near_ref, own_low, own_high, shells_ref, accel_ref, *refs):
     low, high = cells
     count = high - low
     rows, far_rows, sum_rows, out, work = refs[0], refs[1:3], refs[3:5], refs[5], refs[6:]
     for side, there_ref in enumerate((up_ref, down_ref)):
         build(there_ref, cells, rows, far_rows[side], sum_rows[side])
     pair_loop(cells, 1, 6, 6, far_rows, sum_rows, near_ref, out, work[0:2], work[2:4])
-    both = out[...] + own_out[low:high]
+    both = out[...] + jnp.concatenate([own_low[...], own_high[...]], axis=0)[low:high]
     both = (both[:, :8] + both[:, 8:]).reshape(count * 8, LANES)
     rows[: count * 8] = both + pltpu.roll(both, count * 8 - 4, 0)
     total = [rows[pl.ds(comp, count, stride=8), :] for comp in range(4)]
@@ -425,7 +425,23 @@
         name="own_rows",
         cost=pl.CostEstimate(flops=1_000_000_000, bytes_accessed=1_000_000, transcendentals=0),
     )(shells)
-    kept, near = lax.optimization_barrier((shells, near))
+
+    def pair_work(size):
+        return [pltpu.VMEM((size, LANES), f32)] * 4
+
+    def own_sums(far_rows, *cells):
+        return call(
+            functools.partial(own_kernel, cells),
+            0,
+            3,
+            shape(cells[1] - cells[0], 16, LANES),
+            pair_work(768),
+            name="own_slab",
+            cost=pl.CostEstimate(flops=4_000_000_000, bytes_accessed=1_000_000, transcendentals=0),
+        )(near, far_rows, sum_rows)
+
+    low_sums = own_sums(far_rows, 0, CELLS // 2)
+    kept, low_sums = lax.optimization_barrier((shells, low_sums))
     planes = call(
         functools.partial(speeds_kernel, n_dom),
         1,
@@ -436,9 +452,7 @@
     early = sent(planes, n_slab, n_dom, n_slab // 2, 0)
 
     far_rows, _ = lax.optimization_barrier((far_rows, planes))
-
-    def pair_work(size):
-        return [pltpu.VMEM((size, LANES), f32)] * 4
+    high_sums = own_sums(far_rows, CELLS // 2, CELLS)
 
     def row_work(copies):
         return (
@@ -447,24 +461,15 @@
             + [pltpu.VMEM((tall, 16, LANES), bf16)] * copies
         )
 
-    sums = call(
-        own_kernel,
-        0,
-        3,
-        shape(CELLS, 16, LANES),
-        pair_work(768),
-        name="own_slab",
-        cost=pl.CostEstimate(flops=8_000_000_000, bytes_accessed=1_000_000, transcendentals=0),
-    )(near, far_rows, sum_rows)
     accel = call(
         functools.partial(side_kernel, (0, CELLS)),
         0,
-        5,
+        6,
         shape(3, CELLS, LANES),
         row_work(2) + [pltpu.VMEM((CELLS, 16, LANES), f32)] + pair_work(768),
         name="side_slabs",
         cost=pl.CostEstimate(flops=8_000_000_000, bytes_accessed=1_000_000, transcendentals=0),
-    )(below, above, near, sums, shells)
+    )(below, above, near, low_sums, high_sums, shells)
     later = sent(accel, n_slab, n_dom, n_slab // 2, 0)
     out = shape(10, 1, CELLS, LANES)
     state = call(kick_kernel, 0, 2, out, name="state")(planes, accel)

time: 42.1 us -> 40.9 us (0.971)
  starting transfers between devices: 12.7 us -> 10.7 us
  waiting for transfers between devices: 3.96 us -> 4.65 us
    ppermute x6, starting transfers between devices: 12.7 us -> 10.7 us  [sent(): return lax.ppermute(value, ('slab', 'dom'), pairs)]
    ppermute x6, waiting for transfers between devices: 3.96 us -> 4.65 us  [sent(): return lax.ppermute(value, ('slab', 'dom'), pairs)]
    pallas_call x2 -> x3, Pallas kernels: 14.6 us -> 14.6 us  [the longest x1 9.8 us: per_device(): call(functools.partial(side_kernel, (0, CELLS)), 0, 6, shape(3, CELLS, LA...]
  transfers between devices with their start and end apart: 6 -> 6, of which waited for: 2 -> 2; matrix products, arithmetic and copies ran while one was open for 0% -> 0% of each run, Pallas kernels for 41% -> 42%
where the time goes in v11:
time: 40.9 us; the launch traced here: 40.7 us
  Pallas kernels  23 us (56%)
  starting transfers between devices  10.7 us (26%)
  waiting for transfers between devices  4.65 us (11%)
  between operations  1.53 us (4%)
  local copies, waits for them, and re-layouts  0.89 us (2%)
    ppermute x6, starting transfers between devices, sent(): return lax.ppermute(value, ('slab', 'dom'), pairs)  10.7 us
    pallas_call x1, Pallas kernels, per_device(): call(functools.partial(side_kernel, (0, CELLS)), 0, 6, shape(3, CELLS, LA...  9.8 us
    pallas_call x1, Pallas kernels, per_device(): call(functools.partial(pack_kernel, n_dom), 2, 0, [shape(half, tall, LANE...  5.1 us
    pallas_call x2, Pallas kernels, own_sums(): call(functools.partial(own_kernel, cells), 0, 3, shape(cells[1] - cells[0...  4.79 us
    ppermute x6, waiting for transfers between devices, sent(): return lax.ppermute(value, ('slab', 'dom'), pairs)  4.65 us
    unnamed x4, local copies, waits for them, and re-layouts  0.89 us
  transfers between devices with their start and end apart: 6, of which 2 were waited for; matrix products, arithmetic and copies ran while one was open for 0% of the time, Pallas kernels for 42%

profile of v11, /device:TPU:0, one launch (start us, length us, event | category | flops | bytes accessed | tf_op | source)
XLA Modules:
  0.0 40.7 jit_solution(5990662961768613331)
XLA Ops:
  1.3 5.1 %pack.1 = (f32[2,72,128]{2,1,0:T(8,128)}, f32[2,72,128]{2,1,0:T(8,128)}, f32[2,64,128]{2,1,0:T(8,128)}, f32[2,64,128]{2,1,0:T(8,128)}) custom-call(s32[1]{0:T(128)} %bitcast.me_ref, s32[1]{0:T(128)S(6)} %copy.9.count_ref, f32[3,6144]{1,0:T(4,128)} %pos_any.1, f32[3,6144]{1,0:T(4,128)} %vel_any.1, f32[1,6144]{1,0:T(1,128)} %bitcast.3, s32[1,6144]{1,0:T(1,128)} %bitcast.4), custom_call_target="tpu_custom_call" | custom-call | tf_op jit(solution)/shard_map/pack/pallas_call | solution.py:384
  6.4 3.0 %collective-permute-start = (f32[2,72,128]{2,1,0:T(8,128)}, f32[2,72,128]{2,1,0:T(8,128)S(1)}, u32[]{:S(2)}, u32[]{:S(2)}) collective-permute-start(f32[2,72,128]{2,1,0:T(8,128)} %get-tuple-element.13), channel_id=1, source_target_pairs={{0,1},{1,0},{2,3},{3,2},{4,5},{5,4},{6,7},{7,6},{8,9},{9,8},{10,11... | collective-permute-start | bytes 221192 | tf_op jit(solution)/shard_map/ppermute | solution.py:371
  9.4 0.1 collective-permute-start.1
  9.5 0.9 %copy-done = f32[2,72,128]{2,1,0:T(8,128)S(1)} copy-done((f32[2,72,128]{2,1,0:T(8,128)S(1)}, f32[2,72,128]{2,1,0:T(8,128)}, u32[]{:S(2)}) %copy-start) | copy-done | bytes 73752
  10.4 1.8 %collective-permute-done.refs_1_ = f32[2,72,128]{2,1,0:T(8,128)S(1)} collective-permute-done((f32[2,72,128]{2,1,0:T(8,128)}, f32[2,72,128]{2,1,0:T(8,128)S(1)}, u32[]{:S(2)}, u32[]{:S(2)}) %collective-permute-start) | collective-permute-done | bytes 73760 | tf_op jit(solution)/shard_map/ppermute | solution.py:371
  12.2 0.2 join.1.shells_ref
  12.4 0.8 %own_rows.1 = (bf16[64,32,128]{2,1,0:T(8,128)(2,1)S(1)}, bf16[72,32,128]{2,1,0:T(8,128)(2,1)S(1)}, bf16[72,16,128]{2,1,0:T(8,128)(2,1)S(1)}) custom-call(f32[4,72,128]{2,1,0:T(8,128)S(1)} %join.1.shells_ref), custom_call_target="tpu_custom_call" | custom-call | flops 1000000000 | bytes 1000000 | tf_op jit(solution)/shard_map/own_rows/pallas_call | solution.py:415
  13.2 0.1 collective-permute-start.2
  13.2 4.4 %collective-permute-start.3 = (f32[4,72,128]{2,1,0:T(8,128)S(1)}, f32[4,72,128]{2,1,0:T(8,128)S(1)}, u32[]{:S(2)}, u32[]{:S(2)}) collective-permute-start(f32[4,72,128]{2,1,0:T(8,128)S(1)} %join.1.shells_ref), channel_id=1, source_target_pairs={{0,30},{1,31},{2,0},{3,1},{4,2},{5,3},{6,4},{7,5},{8,6},{9,7},{10,... | collective-permute-start | bytes 442376 | tf_op jit(solution)/shard_map/ppermute | solution.py:371
  17.7 2.4 %own_slab.2.own_low = f32[32,16,128]{2,1,0:T(8,128)S(1)} custom-call(bf16[64,32,128]{2,1,0:T(8,128)(2,1)S(1)} %get-tuple-element.14.near_ref, bf16[72,32,128]{2,1,0:T(8,128)(2,1)S(1)} %get-tuple-element.21.far_ref, bf16[72,16,128]{2,1,0:T(8,128)(2,1)S(1)} %get-tuple-element.16.sum_ref), custom_call_target="tpu_custom_call" | custom-call | flops 4000000000 | bytes 1000000 | tf_op jit(solution)/shard_map/own_slab/pallas_call | solution.py:433
  20.1 0.0 collective-permute-done.1.refs_1_
  20.1 0.0 copy-done.1
  20.1 0.2 speeds.1.planes_ref
  20.3 1.8 %collective-permute-start.4 = (f32[7,64,128]{2,1,0:T(8,128)S(1)}, f32[7,64,128]{2,1,0:T(8,128)S(1)}, u32[]{:S(2)}, u32[]{:S(2)}) collective-permute-start(f32[7,64,128]{2,1,0:T(8,128)S(1)} %speeds.1.planes_ref), channel_id=1, source_target_pairs={{0,16},{1,17},{2,18},{3,19},{4,20},{5,21},{6,22},{7,23},{8,24},{9,... | collective-permute-start | bytes 688136 | tf_op jit(solution)/shard_map/ppermute | solution.py:371
  22.1 2.4 %own_slab.3.own_high = f32[32,16,128]{2,1,0:T(8,128)S(1)} custom-call(bf16[64,32,128]{2,1,0:T(8,128)(2,1)S(1)} %get-tuple-element.14.near_ref, bf16[72,32,128]{2,1,0:T(8,128)(2,1)S(1)} %get-tuple-element.21.far_ref, bf16[72,16,128]{2,1,0:T(8,128)(2,1)S(1)} %get-tuple-element.16.sum_ref), custom_call_target="tpu_custom_call" | custom-call | flops 4000000000 | bytes 1000000 | tf_op jit(solution)/shard_map/own_slab/pallas_call | solution.py:433
  24.5 0.0 collective-permute-done.2.up_ref
  24.5 0.0 collective-permute-done.3.down_ref
  24.5 9.8 %side_slabs.1.refs_0_ = f32[3,64,128]{2,1,0:T(8,128)S(1)} custom-call(f32[4,72,128]{2,1,0:T(8,128)S(1)} %collective-permute-done.2.up_ref, f32[4,72,128]{2,1,0:T(8,128)S(1)} %collective-permute-done.3.down_ref, bf16[64,32,128]{2,1,0:T(8,128)(2,1)S(1)} %get-tuple-element.14.near_ref, f32[32,16,128]{2,1,0:T(8,128)S(1)} %own_slab.2.own_low, ...), custom_call_target="tpu_custom_call" | custom-call | flops 8000000000 | bytes 1000000 | tf_op jit(solution)/shard_map/side_slabs/pallas_call | solution.py:464
  34.3 1.3 %collective-permute-start.5 = (f32[3,64,128]{2,1,0:T(8,128)S(1)}, f32[3,64,128]{2,1,0:T(8,128)S(1)}, u32[]{:S(2)}, u32[]{:S(2)}) collective-permute-start(f32[3,64,128]{2,1,0:T(8,128)S(1)} %side_slabs.1.refs_0_), channel_id=1, source_target_pairs={{0,16},{1,17},{2,18},{3,19},{4,20},{5,21},{6,22},{7,23},{8,24},{9,... | collective-permute-start | bytes 294920 | tf_op jit(solution)/shard_map/ppermute | solution.py:371
  35.6 0.7 %state.1 = f32[10,1,64,128]{3,2,1,0:T(8,128)} custom-call(f32[7,64,128]{2,1,0:T(8,128)S(1)} %speeds.1.planes_ref, f32[3,64,128]{2,1,0:T(8,128)S(1)} %side_slabs.1.refs_0_), custom_call_target="tpu_custom_call" | custom-call | tf_op jit(solution)/shard_map/state/pallas_call | solution.py:475
  36.3 0.0 collective-permute-done.4.planes_ref
  36.3 0.7 %buddy.1._ = f32[10,1,64,128]{3,2,1,0:T(8,128)} custom-call(f32[7,64,128]{2,1,0:T(8,128)S(1)} %collective-permute-done.4.planes_ref), custom_call_target="tpu_custom_call" | custom-call | tf_op jit(solution)/shard_map/buddy/pallas_call | solution.py:476
  37.0 2.8 %collective-permute-done.5.accel_ref = f32[3,64,128]{2,1,0:T(8,128)S(1)} collective-permute-done((f32[3,64,128]{2,1,0:T(8,128)S(1)}, f32[3,64,128]{2,1,0:T(8,128)S(1)}, u32[]{:S(2)}, u32[]{:S(2)}) %collective-permute-start.5) | collective-permute-done | bytes 98336 | tf_op jit(solution)/shard_map/ppermute | solution.py:371
  39.9 0.7 %buddy_end.1 = f32[10,1,64,128]{3,2,1,0:T(8,128)} custom-call(f32[10,1,64,128]{3,2,1,0:T(8,128)} %buddy.1._, f32[7,64,128]{2,1,0:T(8,128)S(1)} %collective-permute-done.4.planes_ref, f32[3,64,128]{2,1,0:T(8,128)S(1)} %collective-permute-done.5.accel_ref), custom_call_target="tpu_custom_call", output_to_operand_aliasing={{}: (0, {})} | custom-call | tf_op jit(solution)/shard_map/buddy_end/pallas_call | solution.py:477
  (3 shorter events, 0.0 us)
Async XLA Ops:
  6.4 5.8 %collective-permute-start = (f32[2,72,128]{2,1,0:T(8,128)}, f32[2,72,128]{2,1,0:T(8,128)S(1)}, u32[]{:S(2)}, u32[]{:S(2)}) collective-permute-start(f32[2,72,128]{2,1,0:T(8,128)} %get-tuple-element.13), channel_id=1, source_target_pairs={{0,1},{1,0},{2,3},{3,2},{4,5},{5,4},{6,7},{7,6},{8,9},{9,8},{10,11... | collective-permute-start | bytes 221192 | tf_op jit(solution)/shard_map/ppermute | solution.py:371
  9.4 10.7 %collective-permute-start.1 = (f32[2,64,128]{2,1,0:T(8,128)}, f32[2,64,128]{2,1,0:T(8,128)S(1)}, u32[]{:S(2)}, u32[]{:S(2)}) collective-permute-start(f32[2,64,128]{2,1,0:T(8,128)} %get-tuple-element.19), channel_id=1, source_target_pairs={{0,1},{1,0},{2,3},{3,2},{4,5},{5,4},{6,7},{7,6},{8,9},{9,8},{10,11... | collective-permute-start | bytes 196616 | tf_op jit(solution)/shard_map/ppermute | solution.py:371
  9.5 0.9 %copy-start = (f32[2,72,128]{2,1,0:T(8,128)S(1)}, f32[2,72,128]{2,1,0:T(8,128)}, u32[]{:S(2)}) copy-start(f32[2,72,128]{2,1,0:T(8,128)} %get-tuple-element.12.source_ref) | copy-start | bytes 221188
  13.2 11.3 %collective-permute-start.2 = (f32[4,72,128]{2,1,0:T(8,128)S(1)}, f32[4,72,128]{2,1,0:T(8,128)S(1)}, u32[]{:S(2)}, u32[]{:S(2)}) collective-permute-start(f32[4,72,128]{2,1,0:T(8,128)S(1)} %join.1.shells_ref), channel_id=1, source_target_pairs={{0,2},{1,3},{2,4},{3,5},{4,6},{5,7},{6,8},{7,9},{8,10},{9,11},{10,... | collective-permute-start | bytes 442376 | tf_op jit(solution)/shard_map/ppermute | solution.py:371
  13.2 11.2 %collective-permute-start.3 = (f32[4,72,128]{2,1,0:T(8,128)S(1)}, f32[4,72,128]{2,1,0:T(8,128)S(1)}, u32[]{:S(2)}, u32[]{:S(2)}) collective-permute-start(f32[4,72,128]{2,1,0:T(8,128)S(1)} %join.1.shells_ref), channel_id=1, source_target_pairs={{0,30},{1,31},{2,0},{3,1},{4,2},{5,3},{6,4},{7,5},{8,6},{9,7},{10,... | collective-permute-start | bytes 442376 | tf_op jit(solution)/shard_map/ppermute | solution.py:371
  17.7 2.4 %copy-start.1 = (f32[2,64,128]{2,1,0:T(8,128)S(1)}, f32[2,64,128]{2,1,0:T(8,128)}, u32[]{:S(2)}) copy-start(f32[2,64,128]{2,1,0:T(8,128)} %get-tuple-element.18.refs_0_) | copy-start | bytes 196612
  20.3 16.0 %collective-permute-start.4 = (f32[7,64,128]{2,1,0:T(8,128)S(1)}, f32[7,64,128]{2,1,0:T(8,128)S(1)}, u32[]{:S(2)}, u32[]{:S(2)}) collective-permute-start(f32[7,64,128]{2,1,0:T(8,128)S(1)} %speeds.1.planes_ref), channel_id=1, source_target_pairs={{0,16},{1,17},{2,18},{3,19},{4,20},{5,21},{6,22},{7,23},{8,24},{9,... | collective-permute-start | bytes 688136 | tf_op jit(solution)/shard_map/ppermute | solution.py:371
  34.3 5.6 %collective-permute-start.5 = (f32[3,64,128]{2,1,0:T(8,128)S(1)}, f32[3,64,128]{2,1,0:T(8,128)S(1)}, u32[]{:S(2)}, u32[]{:S(2)}) collective-permute-start(f32[3,64,128]{2,1,0:T(8,128)S(1)} %side_slabs.1.refs_0_), channel_id=1, source_target_pairs={{0,16},{1,17},{2,18},{3,19},{4,20},{5,21},{6,22},{7,23},{8,24},{9,... | collective-permute-start | bytes 294920 | tf_op jit(solution)/shard_map/ppermute | solution.py:371

commit v12 on v11

--- a/solution.py
+++ b/solution.py
@@ -263,7 +263,8 @@
             distances(jnp.minimum(step + 2, steps - 1), b)
         return 0
 
-    lax.fori_loop(0, steps // 2, body, 0, unroll=8)
+    unroll = max(u for u in range(1, 9) if steps // 2 % u == 0)
+    lax.fori_loop(0, steps // 2, body, 0, unroll=unroll)
 
 
 def copy_kernel(source_ref, target_ref):
@@ -285,8 +286,9 @@
         planes_ref[4 + comp] = pltpu.roll(merged(pieces, comp, n_dom), turn, 1)
 
 
-def own_rows_kernel(shells_ref, near_ref, far_ref, sum_ref, rows):
+def first_own_kernel(cells, shells_ref, near_ref, far_ref, sum_ref, out_ref, rows, *work):
     build(shells_ref, (0, CELLS), rows, far_ref, sum_ref, near_ref)
+    own_kernel(cells, near_ref, far_ref, sum_ref, out_ref, *work)
 
 
 def own_kernel(cells, near_ref, far_ref, sum_ref, out_ref, *work):
@@ -412,35 +414,25 @@
         functools.partial(join_kernel, n_dom), 1, n_dom, shape(4, tall, LANES), name="join"
     )(me, *places)
     below, above = (sent(shells, n_slab, n_dom, side, 0) for side in (1, -1))
-    near, far_rows, sum_rows = call(
-        own_rows_kernel,
+
+    def pair_work(size):
+        return [pltpu.VMEM((size, LANES), f32)] * 4
+
+    cut = CELLS // 4
+    near, far_rows, sum_rows, low_sums = call(
+        functools.partial(first_own_kernel, (0, cut)),
         0,
         1,
         [
             shape(CELLS, FEATURES, LANES, dtype=bf16),
             shape(tall, FEATURES, LANES, dtype=bf16),
             shape(tall, 16, LANES, dtype=bf16),
+            shape(cut, 16, LANES),
         ],
-        [pltpu.VMEM((tall * 8, LANES), f32)],
-        name="own_rows",
-        cost=pl.CostEstimate(flops=1_000_000_000, bytes_accessed=1_000_000, transcendentals=0),
+        [pltpu.VMEM((tall * 8, LANES), f32)] + pair_work(768),
+        name="own_slab",
+        cost=pl.CostEstimate(flops=8_000_000_000, bytes_accessed=1_000_000, transcendentals=0),
     )(shells)
-
-    def pair_work(size):
-        return [pltpu.VMEM((size, LANES), f32)] * 4
-
-    def own_sums(far_rows, *cells):
-        return call(
-            functools.partial(own_kernel, cells),
-            0,
-            3,
-            shape(cells[1] - cells[0], 16, LANES),
-            pair_work(768),
-            name="own_slab",
-            cost=pl.CostEstimate(flops=4_000_000_000, bytes_accessed=1_000_000, transcendentals=0),
-        )(near, far_rows, sum_rows)
-
-    low_sums = own_sums(far_rows, 0, CELLS // 2)
     kept, low_sums = lax.optimization_barrier((shells, low_sums))
     planes = call(
         functools.partial(speeds_kernel, n_dom),
@@ -452,7 +444,15 @@
     early = sent(planes, n_slab, n_dom, n_slab // 2, 0)
 
     far_rows, _ = lax.optimization_barrier((far_rows, planes))
-    high_sums = own_sums(far_rows, CELLS // 2, CELLS)
+    high_sums = call(
+        functools.partial(own_kernel, (cut, CELLS)),
+        0,
+        3,
+        shape(CELLS - cut, 16, LANES),
+        pair_work(768),
+        name="own_slab",
+        cost=pl.CostEstimate(flops=8_000_000_000, bytes_accessed=1_000_000, transcendentals=0),
+    )(near, far_rows, sum_rows)
 
     def row_work(copies):
         return (

time: 40.9 us -> 43 us (1.051)
  starting transfers between devices: 10.7 us -> 14.1 us
  waiting for transfers between devices: 4.65 us -> 3.26 us
    ppermute x6, starting transfers between devices: 10.7 us -> 14.1 us  [sent(): return lax.ppermute(value, ('slab', 'dom'), pairs)]
    ppermute x6, waiting for transfers between devices: 4.65 us -> 3.26 us  [sent(): return lax.ppermute(value, ('slab', 'dom'), pairs)]
    pallas_call x3 -> x2, Pallas kernels: 5.6 us -> 5.84 us  [the longest x1 3.73 us: per_device(): call(functools.partial(own_kernel, (cut, CELLS)), 0, 3, shape(CELLS - cut...]
  transfers between devices with their start and end apart: 6 -> 6, of which waited for: 2 -> 2; matrix products, arithmetic and copies ran while one was open for 0% -> 0% of each run, Pallas kernels for 42% -> 41%
where the time goes in v12:
time: 43 us; the launch traced here: 42.8 us
  Pallas kernels  23.2 us (54%)
  starting transfers between devices  14.1 us (33%)
  waiting for transfers between devices  3.26 us (8%)
  between operations  1.35 us (3%)
  local copies, waits for them, and re-layouts  0.89 us (2%)
    ppermute x6, starting transfers between devices, sent(): return lax.ppermute(value, ('slab', 'dom'), pairs)  14.1 us
    pallas_call x1, Pallas kernels, per_device(): call(functools.partial(side_kernel, (0, CELLS)), 0, 6, shape(3, CELLS, LA...  9.77 us
    pallas_call x1, Pallas kernels, per_device(): call(functools.partial(pack_kernel, n_dom), 2, 0, [shape(half, tall, LANE...  5.09 us
    pallas_call x1, Pallas kernels, per_device(): call(functools.partial(own_kernel, (cut, CELLS)), 0, 3, shape(CELLS - cut...  3.73 us
    ppermute x6, waiting for transfers between devices, sent(): return lax.ppermute(value, ('slab', 'dom'), pairs)  3.26 us
    pallas_call x1, Pallas kernels, per_device(): call(functools.partial(first_own_kernel, (0, cut)), 0, 1, [shape(CELLS, F...  2.11 us
    unnamed x4, local copies, waits for them, and re-layouts  0.89 us
  transfers between devices with their start and end apart: 6, of which 2 were waited for; matrix products, arithmetic and copies ran while one was open for 0% of the time, Pallas kernels for 41%

profile of v12, /device:TPU:0, one launch (start us, length us, event | category | flops | bytes accessed | tf_op | source)
XLA Modules:
  0.0 42.8 jit_solution(16424006578685123605)
XLA Ops:
  1.3 5.1 %pack.1 = (f32[2,72,128]{2,1,0:T(8,128)}, f32[2,72,128]{2,1,0:T(8,128)}, f32[2,64,128]{2,1,0:T(8,128)}, f32[2,64,128]{2,1,0:T(8,128)}) custom-call(s32[1]{0:T(128)} %bitcast.me_ref, s32[1]{0:T(128)S(6)} %copy.9.count_ref, f32[3,6144]{1,0:T(4,128)} %pos_any.1, f32[3,6144]{1,0:T(4,128)} %vel_any.1, f32[1,6144]{1,0:T(1,128)} %bitcast.3, s32[1,6144]{1,0:T(1,128)} %bitcast.4), custom_call_target="tpu_custom_call" | custom-call | tf_op jit(solution)/shard_map/pack/pallas_call | solution.py:386
  6.4 3.0 %collective-permute-start = (f32[2,72,128]{2,1,0:T(8,128)}, f32[2,72,128]{2,1,0:T(8,128)S(1)}, u32[]{:S(2)}, u32[]{:S(2)}) collective-permute-start(f32[2,72,128]{2,1,0:T(8,128)} %get-tuple-element.14), channel_id=1, source_target_pairs={{0,1},{1,0},{2,3},{3,2},{4,5},{5,4},{6,7},{7,6},{8,9},{9,8},{10,11... | collective-permute-start | bytes 221192 | tf_op jit(solution)/shard_map/ppermute | solution.py:373
  9.4 0.1 collective-permute-start.1
  9.5 0.9 %copy-done = f32[2,72,128]{2,1,0:T(8,128)S(1)} copy-done((f32[2,72,128]{2,1,0:T(8,128)S(1)}, f32[2,72,128]{2,1,0:T(8,128)}, u32[]{:S(2)}) %copy-start) | copy-done | bytes 73752
  10.4 1.8 %collective-permute-done.refs_1_ = f32[2,72,128]{2,1,0:T(8,128)S(1)} collective-permute-done((f32[2,72,128]{2,1,0:T(8,128)}, f32[2,72,128]{2,1,0:T(8,128)S(1)}, u32[]{:S(2)}, u32[]{:S(2)}) %collective-permute-start) | collective-permute-done | bytes 73760 | tf_op jit(solution)/shard_map/ppermute | solution.py:373
  12.2 0.2 join.1.shells_ref
  12.3 0.0 copy-start.1
  12.4 2.1 %own_slab.2 = (bf16[64,32,128]{2,1,0:T(8,128)(2,1)S(1)}, bf16[72,32,128]{2,1,0:T(8,128)(2,1)S(1)}, bf16[72,16,128]{2,1,0:T(8,128)(2,1)S(1)}, f32[16,16,128]{2,1,0:T(8,128)S(1)}) custom-call(f32[4,72,128]{2,1,0:T(8,128)S(1)} %join.1.shells_ref), custom_call_target="tpu_custom_call" | custom-call | flops 8000000000 | bytes 1000000 | tf_op jit(solution)/shard_map/own_slab/pallas_call | solution.py:422
  14.5 0.1 collective-permute-start.2
  14.5 4.4 %collective-permute-start.3 = (f32[4,72,128]{2,1,0:T(8,128)S(1)}, f32[4,72,128]{2,1,0:T(8,128)S(1)}, u32[]{:S(2)}, u32[]{:S(2)}) collective-permute-start(f32[4,72,128]{2,1,0:T(8,128)S(1)} %join.1.shells_ref), channel_id=1, source_target_pairs={{0,30},{1,31},{2,0},{3,1},{4,2},{5,3},{6,4},{7,5},{8,6},{9,7},{10,... | collective-permute-start | bytes 442376 | tf_op jit(solution)/shard_map/ppermute | solution.py:373
  19.0 0.0 collective-permute-done.1.refs_1_
  19.0 0.0 copy-done.1
  19.0 0.2 speeds.1.planes_ref
  19.1 1.8 %collective-permute-start.4 = (f32[7,64,128]{2,1,0:T(8,128)S(1)}, f32[7,64,128]{2,1,0:T(8,128)S(1)}, u32[]{:S(2)}, u32[]{:S(2)}) collective-permute-start(f32[7,64,128]{2,1,0:T(8,128)S(1)} %speeds.1.planes_ref), channel_id=1, source_target_pairs={{0,16},{1,17},{2,18},{3,19},{4,20},{5,21},{6,22},{7,23},{8,24},{9,... | collective-permute-start | bytes 688136 | tf_op jit(solution)/shard_map/ppermute | solution.py:373
  21.0 3.7 %own_slab.3.own_high = f32[48,16,128]{2,1,0:T(8,128)S(1)} custom-call(bf16[64,32,128]{2,1,0:T(8,128)(2,1)S(1)} %get-tuple-element.19.near_ref, bf16[72,32,128]{2,1,0:T(8,128)(2,1)S(1)} %get-tuple-element.22.far_ref, bf16[72,16,128]{2,1,0:T(8,128)(2,1)S(1)} %get-tuple-element.23.sum_ref), custom_call_target="tpu_custom_call" | custom-call | flops 8000000000 | bytes 1000000 | tf_op jit(solution)/shard_map/own_slab/pallas_call | solution.py:447
  24.7 0.0 collective-permute-done.2.up_ref
  24.7 0.0 collective-permute-done.3.down_ref
  24.7 9.8 %side_slabs.1.refs_0_ = f32[3,64,128]{2,1,0:T(8,128)S(1)} custom-call(f32[4,72,128]{2,1,0:T(8,128)S(1)} %collective-permute-done.2.up_ref, f32[4,72,128]{2,1,0:T(8,128)S(1)} %collective-permute-done.3.down_ref, bf16[64,32,128]{2,1,0:T(8,128)(2,1)S(1)} %get-tuple-element.19.near_ref, f32[16,16,128]{2,1,0:T(8,128)S(1)} %get-tuple-element.20.own_low, ...), custom_call_target="tpu_custom_call" | custom-call | flops 8000000000 | bytes 1000000 | tf_op jit(solution)/shard_map/side_slabs/pallas_call | solution.py:464
  34.5 4.7 %collective-permute-start.5 = (f32[3,64,128]{2,1,0:T(8,128)S(1)}, f32[3,64,128]{2,1,0:T(8,128)S(1)}, u32[]{:S(2)}, u32[]{:S(2)}) collective-permute-start(f32[3,64,128]{2,1,0:T(8,128)S(1)} %side_slabs.1.refs_0_), channel_id=1, source_target_pairs={{0,16},{1,17},{2,18},{3,19},{4,20},{5,21},{6,22},{7,23},{8,24},{9,... | collective-permute-start | bytes 294920 | tf_op jit(solution)/shard_map/ppermute | solution.py:373
  39.2 0.7 %state.1 = f32[10,1,64,128]{3,2,1,0:T(8,128)} custom-call(f32[7,64,128]{2,1,0:T(8,128)S(1)} %speeds.1.planes_ref, f32[3,64,128]{2,1,0:T(8,128)S(1)} %side_slabs.1.refs_0_), custom_call_target="tpu_custom_call" | custom-call | tf_op jit(solution)/shard_map/state/pallas_call | solution.py:475
  39.9 0.0 collective-permute-done.4.planes_ref
  39.9 0.7 %buddy.1._ = f32[10,1,64,128]{3,2,1,0:T(8,128)} custom-call(f32[7,64,128]{2,1,0:T(8,128)S(1)} %collective-permute-done.4.planes_ref), custom_call_target="tpu_custom_call" | custom-call | tf_op jit(solution)/shard_map/buddy/pallas_call | solution.py:476
  40.7 1.5 %collective-permute-done.5.accel_ref = f32[3,64,128]{2,1,0:T(8,128)S(1)} collective-permute-done((f32[3,64,128]{2,1,0:T(8,128)S(1)}, f32[3,64,128]{2,1,0:T(8,128)S(1)}, u32[]{:S(2)}, u32[]{:S(2)}) %collective-permute-start.5) | collective-permute-done | bytes 98336 | tf_op jit(solution)/shard_map/ppermute | solution.py:373
  42.1 0.7 %buddy_end.1 = f32[10,1,64,128]{3,2,1,0:T(8,128)} custom-call(f32[10,1,64,128]{3,2,1,0:T(8,128)} %buddy.1._, f32[7,64,128]{2,1,0:T(8,128)S(1)} %collective-permute-done.4.planes_ref, f32[3,64,128]{2,1,0:T(8,128)S(1)} %collective-permute-done.5.accel_ref), custom_call_target="tpu_custom_call", output_to_operand_aliasing={{}: (0, {})} | custom-call | tf_op jit(solution)/shard_map/buddy_end/pallas_call | solution.py:477
  (2 shorter events, 0.0 us)
Async XLA Ops:
  6.4 5.8 %collective-permute-start = (f32[2,72,128]{2,1,0:T(8,128)}, f32[2,72,128]{2,1,0:T(8,128)S(1)}, u32[]{:S(2)}, u32[]{:S(2)}) collective-permute-start(f32[2,72,128]{2,1,0:T(8,128)} %get-tuple-element.14), channel_id=1, source_target_pairs={{0,1},{1,0},{2,3},{3,2},{4,5},{5,4},{6,7},{7,6},{8,9},{9,8},{10,11... | collective-permute-start | bytes 221192 | tf_op jit(solution)/shard_map/ppermute | solution.py:373
  9.4 9.6 %collective-permute-start.1 = (f32[2,64,128]{2,1,0:T(8,128)}, f32[2,64,128]{2,1,0:T(8,128)S(1)}, u32[]{:S(2)}, u32[]{:S(2)}) collective-permute-start(f32[2,64,128]{2,1,0:T(8,128)} %get-tuple-element.18), channel_id=1, source_target_pairs={{0,1},{1,0},{2,3},{3,2},{4,5},{5,4},{6,7},{7,6},{8,9},{9,8},{10,11... | collective-permute-start | bytes 196616 | tf_op jit(solution)/shard_map/ppermute | solution.py:373
  9.5 0.9 %copy-start = (f32[2,72,128]{2,1,0:T(8,128)S(1)}, f32[2,72,128]{2,1,0:T(8,128)}, u32[]{:S(2)}) copy-start(f32[2,72,128]{2,1,0:T(8,128)} %get-tuple-element.13.source_ref) | copy-start | bytes 221188
  12.3 6.6 %copy-start.1 = (f32[2,64,128]{2,1,0:T(8,128)S(1)}, f32[2,64,128]{2,1,0:T(8,128)}, u32[]{:S(2)}) copy-start(f32[2,64,128]{2,1,0:T(8,128)} %get-tuple-element.17.refs_0_) | copy-start | bytes 196612
  14.5 10.2 %collective-permute-start.2 = (f32[4,72,128]{2,1,0:T(8,128)S(1)}, f32[4,72,128]{2,1,0:T(8,128)S(1)}, u32[]{:S(2)}, u32[]{:S(2)}) collective-permute-start(f32[4,72,128]{2,1,0:T(8,128)S(1)} %join.1.shells_ref), channel_id=1, source_target_pairs={{0,2},{1,3},{2,4},{3,5},{4,6},{5,7},{6,8},{7,9},{8,10},{9,11},{10,... | collective-permute-start | bytes 442376 | tf_op jit(solution)/shard_map/ppermute | solution.py:373
  14.5 10.2 %collective-permute-start.3 = (f32[4,72,128]{2,1,0:T(8,128)S(1)}, f32[4,72,128]{2,1,0:T(8,128)S(1)}, u32[]{:S(2)}, u32[]{:S(2)}) collective-permute-start(f32[4,72,128]{2,1,0:T(8,128)S(1)} %join.1.shells_ref), channel_id=1, source_target_pairs={{0,30},{1,31},{2,0},{3,1},{4,2},{5,3},{6,4},{7,5},{8,6},{9,7},{10,... | collective-permute-start | bytes 442376 | tf_op jit(solution)/shard_map/ppermute | solution.py:373
  19.1 20.8 %collective-permute-start.4 = (f32[7,64,128]{2,1,0:T(8,128)S(1)}, f32[7,64,128]{2,1,0:T(8,128)S(1)}, u32[]{:S(2)}, u32[]{:S(2)}) collective-permute-start(f32[7,64,128]{2,1,0:T(8,128)S(1)} %speeds.1.planes_ref), channel_id=1, source_target_pairs={{0,16},{1,17},{2,18},{3,19},{4,20},{5,21},{6,22},{7,23},{8,24},{9,... | collective-permute-start | bytes 688136 | tf_op jit(solution)/shard_map/ppermute | solution.py:373
  34.5 7.6 %collective-permute-start.5 = (f32[3,64,128]{2,1,0:T(8,128)S(1)}, f32[3,64,128]{2,1,0:T(8,128)S(1)}, u32[]{:S(2)}, u32[]{:S(2)}) collective-permute-start(f32[3,64,128]{2,1,0:T(8,128)S(1)} %side_slabs.1.refs_0_), channel_id=1, source_target_pairs={{0,16},{1,17},{2,18},{3,19},{4,20},{5,21},{6,22},{7,23},{8,24},{9,... | collective-permute-start | bytes 294920 | tf_op jit(solution)/shard_map/ppermute | solution.py:373
